TPU v7x, 32 devices: a whole 2x2x4 slice. The times are simulated.
32 devices in a mesh: dp: 4 (over z), shard: 8 (over y, x, core).
Axes of the slice: x: 2, y: 2, z: 4, core: 2. Of those that a mesh axis runs over, the one named last changes fastest.
Arguments:
- prefill_x: bfloat16 [24576, 1536], P(('dp', 'shard')), may hold values from -6 to 6
- decode_x: bfloat16 [16, 1536], P('dp'), may hold values from -6 to 6
- norm_gain: bfloat16 [1536], P(('dp', 'shard')), may hold values from 0.099609375 to 1.8984375
- wqkv: bfloat16 [1536, 3072], P(('dp', 'shard')), may hold values from -0.15625 to 0.15625
- wo: bfloat16 [1536, 1536], P(('dp', 'shard')), may hold values from -0.15625 to 0.15625
- k_cache: bfloat16 [16, 4096, 768], P('dp', 'shard'), may hold values from -360 to 360
- v_cache: bfloat16 [16, 4096, 768], P('dp', 'shard'), may hold values from -6 to 6
- cache_len: int32 [16], P('dp'), may hold values from 1 to 4096, as said below
Outputs:
- prefill_out: bfloat16 [24576, 1536], P(('dp', 'shard'))
- decode_out: bfloat16 [16, 1536], P('dp')
Inputs may be any that keep to these rules, and one draw needn't show every extreme that they name: `cache_len`: some request has exactly 4096 cached positions.
All inputs are finite; a program needn't handle non-finite values.
Results may differ from a plain program's by a relative error of at most 0.0095.
The roundings to bfloat16 on the way count: a program that leaves them out, or rounds other values in their place, can miss the bound.
Values may be sent and summed in bfloat16 or wider, within the bound.
No kernel may reach another device: no remote copies, remote signals or barrier semaphores. Data moves between devices by JAX's collectives and lax.ppermute only.
A program may use at most 128 MiB of HBM per device.

v0:
```python
import jax
import jax.numpy as jnp
from jax import lax
from jax.sharding import PartitionSpec as P

H = 16
KV = 8
HD = 96


THETA = 100000.0
EPS = 1e-05
NEGATIVE = -1e30


def rotate(tensor, positions):
    half_width = tensor.shape[-1] // 2
    frequency = jnp.power(
        THETA, -jnp.arange(half_width, dtype=jnp.float32) * (2.0 / tensor.shape[-1])
    )
    angles = positions.astype(jnp.float32)[:, None] * frequency[None, :]
    cosine = jnp.cos(angles)[:, None, :]
    sine_part = jnp.sin(angles)[:, None, :]
    leading = tensor[..., :half_width]
    trailing = tensor[..., half_width:]
    return jnp.concatenate(
        [leading * cosine - trailing * sine_part, trailing * cosine + leading * sine_part], axis=-1
    )


def causal_stretch(queries, new_keys, new_values):
    row_count = queries.shape[0]
    group_size = H // KV
    query_heads = jnp.moveaxis(queries.reshape(row_count, KV, group_size, HD), 1, 0)
    key_heads = jnp.moveaxis(new_keys, 1, 0)
    value_heads = jnp.moveaxis(new_values, 1, 0)
    indices = jnp.arange(row_count, dtype=jnp.int32)
    allowed = indices[None, :] <= indices[:, None]

    def one_head(operands):
        query_head, key_head, value_head = operands
        scores = jnp.einsum(
            "qgd,sd->gqs", query_head, key_head, preferred_element_type=jnp.float32
        ) * HD ** (-0.5)
        scores = jnp.where(allowed[None], scores, NEGATIVE)
        highest = jnp.max(scores, axis=-1, keepdims=True)
        expanded = jnp.exp(scores - highest)
        weights = (expanded / jnp.sum(expanded, axis=-1, keepdims=True)).astype(jnp.bfloat16)
        return jnp.einsum(
            "gqs,sd->qgd", weights, value_head, preferred_element_type=jnp.float32
        ).astype(jnp.bfloat16)

    attended = lax.map(one_head, (query_heads, key_heads, value_heads))
    return jnp.moveaxis(attended, 0, 1).reshape(row_count, H * HD)


def per_device(prefill_x, decode_x, norm_gain, wqkv, wo, k_cache, v_cache, cache_len):
    stretch_rows = prefill_x.shape[0]
    request_count = decode_x.shape[0]
    stacked = jnp.concatenate([prefill_x, decode_x], axis=0).astype(jnp.float32)
    scaled = stacked * lax.rsqrt(jnp.mean(stacked * stacked, axis=-1, keepdims=True) + EPS)
    weight_rows = lax.all_gather(wqkv, ("dp", "shard"), axis=0, tiled=True)
    gain_rows = lax.all_gather(norm_gain, ("dp", "shard"), axis=0, tiled=True)
    columns = scaled
    left_side = (columns * gain_rows.astype(jnp.float32)[None, :]).astype(jnp.bfloat16)
    united_rows = jnp.dot(left_side, weight_rows, preferred_element_type=jnp.float32)
    row_total = united_rows.shape[0]
    positions = jnp.concatenate([jnp.arange(stretch_rows, dtype=jnp.int32), cache_len])
    queries = rotate(united_rows[:, : H * HD].reshape(row_total, H, HD), positions).astype(
        jnp.bfloat16
    )
    new_keys = rotate(
        united_rows[:, H * HD : (H + KV) * HD].reshape(row_total, KV, HD), positions
    ).astype(jnp.bfloat16)
    new_values = united_rows[:, (H + KV) * HD :].reshape(row_total, KV, HD).astype(jnp.bfloat16)
    prefill_mix = causal_stretch(
        queries[:stretch_rows], new_keys[:stretch_rows], new_values[:stretch_rows]
    )
    score_scale = HD ** (-0.5)
    cache_span = k_cache.shape[1]
    decode_queries = queries[stretch_rows:].reshape(request_count, KV, H // KV, HD)
    self_keys = new_keys[stretch_rows:]
    self_values = new_values[stretch_rows:]
    key_blocks = k_cache.reshape(request_count, cache_span, KV, HD)
    value_blocks = v_cache.reshape(request_count, cache_span, KV, HD)
    scores = (
        jnp.einsum(
            "rkgd,rpkd->rkgp", decode_queries, key_blocks, preferred_element_type=jnp.float32
        )
        * score_scale
    )
    positions_here = lax.axis_index("shard") * cache_span + jnp.arange(cache_span, dtype=jnp.int32)
    live_mask = positions_here[None, None, None, :] < cache_len[:, None, None, None]
    scores = jnp.where(live_mask, scores, NEGATIVE)
    block_peaks = jnp.max(scores, axis=-1)
    expanded = jnp.where(live_mask, jnp.exp(scores - block_peaks[..., None]), 0.0)
    partial_totals = jnp.sum(expanded, axis=-1)
    partial_sums = jnp.einsum(
        "rkgp,rpkd->rkgd",
        expanded.astype(jnp.bfloat16),
        value_blocks,
        preferred_element_type=jnp.float32,
    )
    group_top = lax.pmax(block_peaks, "shard")
    rescale = jnp.exp(block_peaks - group_top)
    numer_all, denom_all = lax.psum(
        (partial_sums * rescale[..., None], partial_totals * rescale), "shard"
    )
    self_scores = (
        jnp.einsum("rkgd,rkd->rkg", decode_queries, self_keys, preferred_element_type=jnp.float32)
        * score_scale
    )
    overall = jnp.maximum(group_top, self_scores)
    old_weight = jnp.exp(group_top - overall)
    own_weight = jnp.exp(self_scores - overall)
    numerator = (
        numer_all * old_weight[..., None]
        + own_weight[..., None] * self_values.astype(jnp.float32)[:, :, None, :]
    )
    denominator = denom_all * old_weight + own_weight
    decode_mix = (
        (numerator / denominator[..., None]).reshape(request_count, H * HD).astype(jnp.bfloat16)
    )
    attended = jnp.concatenate([prefill_mix, decode_mix], axis=0)
    columns = attended
    projected = jnp.dot(
        columns,
        lax.all_gather(wo, ("dp", "shard"), axis=0, tiled=True),
        preferred_element_type=jnp.float32,
    )
    return (
        projected[:stretch_rows].astype(jnp.bfloat16),
        projected[stretch_rows:].astype(jnp.bfloat16),
    )


def solution(mesh):
    in_specs = (
        P(("dp", "shard"), None),
        P("dp", None),
        P(("dp", "shard")),
        P(("dp", "shard"), None),
        P(("dp", "shard"), None),
        P("dp", "shard", None),
        P("dp", "shard", None),
        P("dp"),
    )
    out_specs = (P(("dp", "shard"), None), P("dp", None))
    return jax.shard_map(
        per_device, mesh=mesh, in_specs=in_specs, out_specs=out_specs, check_vma=False
    )
```

profile of v0, /device:TPU:0, one launch (start us, length us, event | category | flops | bytes accessed | tf_op | source)
XLA Modules:
  0.0 272.5 jit_solution(13633832169304413606)
XLA Ops:
  9.6 42.5 %all-reduce = bf16[1536]{0:T(1024)(128)(2,1)S(1)} all-reduce(bf16[1536]{0:T(1024)(128)(2,1)S(1)} %dynamic-update-slice), channel_id=1, replica_groups=mesh['dp'=4,'shard'=8] {'dp','shard'}, use_global_device_ids=true, to_apply=%add | all-reduce | flops 1536 | bytes 6144
  52.1 2.3 fusion.41
  55.0 3.2 %copy.25 = bf16[4,512,768]{1,2,0:T(8,128)(2,1)S(1)} copy(bf16[4,512,768]{2,1,0:T(8,128)(2,1)} %param.15) | data formatting | bytes 6291456 | tf_op args[5]
  58.2 4.6 %copy.26 = bf16[4,512,768]{1,2,0:T(8,128)(2,1)} copy(bf16[4,512,768]{2,1,0:T(8,128)(2,1)} %param.16) | data formatting | bytes 6291456 | tf_op args[6]
  63.6 33.0 %all-gather.3.cloned.1.call-done = bf16[1536,3072]{1,0:T(8,128)(2,1)} async-done(((bf16[48,3072]{1,0:T(8,128)(2,1)}), bf16[1536,3072]{1,0:T(8,128)(2,1)}) %all-gather.3.cloned.1.call-update) | async-done | bytes 9437200 | tf_op jit(solution)/shard_map/all_gather | solution.py:62
  96.5 13.1 %fusion.77 = (bf16[772,3072]{1,0:T(8,128)(2,1)}, f32[772,3072]{1,0:T(8,128)S(1)}) fusion(bf16[1536,3072]{1,0:T(8,128)(2,1)} %all-gather.3.cloned.1.call-done, f32[1536]{0:T(1024)S(1)} %convert_element_type.48, f32[772]{0:T(1024)S(1)} %add_rsqrt_fusion, bf16[4,1536]{1,0:T(4,128)(2,1)S(1)} %copy-done.6, bf16[768,1536]{1,0:T(8,128)(2,1)} %param.10), kind=kOutput, calls=%fused_computation.86 | convolution fusion | flops 7296178176 | bytes 26047504 | tf_op jit(solution)/shard_map/dot_general | solution.py:66
  109.6 2.6 slice.73
  113.9 5.9 %copy.23 = f32[772,1536]{0,1:T(8,128)} copy(f32[772,1536]{1,0:T(8,128)} %slice.73) | data formatting | bytes 9486336 | tf_op jit(solution)/shard_map/slice | solution.py:69
  119.8 3.4 %subtract_convert_fusion = (bf16[772,16,48]{0,2,1:T(8,128)(2,1)S(1)}, bf16[772,16,48]{0,2,1:T(8,128)(2,1)S(1)}) fusion(f32[772,16,96]{0,2,1:T(8,128)} %bitcast.84, f32[772,48]{0,1:T(8,128)S(1)} %get-tuple-element.71, f32[772,48]{0,1:T(8,128)S(1)} %get-tuple-element.70), kind=kLoop, calls=%fused_computation.43 | loop fusion | flops 4743168 | bytes 7411200 | tf_op jit(solution)/shard_map/convert.6
  123.2 1.6 fusion.51
  126.5 24.8 %pmax.7 = f32[4,8,2]{2,1,0:T(8,128)S(1)} all-reduce(f32[4,8,2]{2,1,0:T(8,128)S(1)} %get-tuple-element.72), channel_id=1, replica_groups=mesh['dp'=4,'shard'=8] {'shard'}, use_global_device_ids=true, to_apply=%region_6.7 | all-reduce | flops 64 | bytes 512 | tf_op jit(solution)/shard_map/pmax | solution.py:104
  151.5 2.2 copy.22
  157.2 2.9 %convolution_multiply_fusion.1 = f32[4,8,2,96]{3,2,1,0:T(2,128)S(1)} fusion(bf16[4,512,8,96]{1,3,2,0:T(8,128)(2,1)} %bitcast.87, f32[4,8,2,512]{3,2,1,0:T(2,128)} %copy-done.4, pred[4,512]{1,0:T(4,128)(4,1)S(1)} %copy-done.5, f32[4,8,2]{2,1,0:T(8,128)S(1)} %get-tuple-element.72, f32[4,8,2]{2,1,0:T(8,128)S(1)} %get-tuple-element.63), kind=kOutput, calls=%fused_computation.57 | convolution fusion | flops 6395904 | bytes 3303936 | tf_op jit(solution)/shard_map/rkgp,rpkd->rkgd/dot_general | solution.py:98
  160.1 22.9 %all-reduce.1 = (f32[4,8,2,96]{3,2,1,0:T(2,128)S(1)}, f32[4,8,2]{2,1,0:T(8,128)S(1)}) all-reduce(f32[4,8,2,96]{3,2,1,0:T(2,128)S(1)} %convolution_multiply_fusion.1, f32[4,8,2]{2,1,0:T(8,128)S(1)} %get-tuple-element.62), channel_id=1, replica_groups=mesh['dp'=4,'shard'=8] {'shard'}, use_global_device_ids=true, to_apply=%region_7.8 | all-reduce | flops 6208 | bytes 49664 | tf_op jit(solution)/shard_map/psum | solution.py:106
  186.4 70.1 %while.11 = (s32[]{:T(128)}, bf16[8,768,2,96]{1,3,2,0:T(8,128)(2,1)}, bf16[8,768,96]{1,2,0:T(8,128)(2,1)}, bf16[8,768,96]{1,2,0:T(8,128)(2,1)S(1)}, bf16[8,768,2,96]{1,3,2,0:T(8,128)(2,1)}, /*index=5*/s32[]{:T(128)}) while((s32[]{:T(128)}, bf16[8,768,2,96]{1,3,2,0:T(8,128)(2,1)}, bf16[8,768,96]{1,2,0:T(8,128)(2,1)}, ...), condition=%wide.region_4.5_spmd.clone, body=%wide.region_1.4_spmd.clone.sunk | while | flops 460800768 | bytes 11515973 | solution.py:53
  186.6 4.9 %fusion.94 = (f32[2,768]{1,0:T(2,128)S(1)}, f32[2,768,768]{1,2,0:T(8,128)}) fusion(pred[768,768]{0,1:T(8,128)(4,1)S(1)} %iota_compare_fusion.2, bf16[8,768,2,96]{1,3,2,0:T(8,128)(2,1)} %get-tuple-element.127, s32[]{:T(128)} %get-tuple-element.117, bf16[8,768,96]{1,2,0:T(8,128)(2,1)S(1)} %get-tuple-element.126), kind=kOutput, calls=%fused_computation.84.clone.1 | convolution fusion | flops 231211776 | bytes 5757952 | tf_op jit(solution)/shard_map/while/body/eval_jaxpr/sub | solution.py:47
  191.5 3.7 %fusion.95 = bf16[8,768,2,96]{1,3,2,0:T(8,128)(2,1)} fusion(bf16[8,768,2,96]{1,3,2,0:T(8,128)(2,1)} %get-tuple-element.118, s32[]{:T(128)} %get-tuple-element.117, f32[2,768,768]{1,2,0:T(8,128)} %get-tuple-element.109, f32[2,768]{1,0:T(2,128)S(1)} %get-tuple-element.110, bf16[8,768,96]{1,2,0:T(8,128)(2,1)} %get-tuple-element.125), kind=kOutput, calls=%fused_computation.13.clone.1 | convolution fusion | flops 228999168 | bytes 5168128 | tf_op jit(solution)/shard_map/while/body/eval_jaxpr/gqs,sd->qgd/dot_general | solution.py:49
  195.4 4.9 %fusion.94 = (f32[2,768]{1,0:T(2,128)S(1)}, f32[2,768,768]{1,2,0:T(8,128)}) fusion(pred[768,768]{0,1:T(8,128)(4,1)S(1)} %iota_compare_fusion.2, bf16[8,768,2,96]{1,3,2,0:T(8,128)(2,1)} %get-tuple-element.127, s32[]{:T(128)} %get-tuple-element.117, bf16[8,768,96]{1,2,0:T(8,128)(2,1)S(1)} %get-tuple-element.126), kind=kOutput, calls=%fused_computation.84.clone.1 | convolution fusion | flops 231211776 | bytes 5757952 | tf_op jit(solution)/shard_map/while/body/eval_jaxpr/sub | solution.py:47
  200.3 3.7 %fusion.95 = bf16[8,768,2,96]{1,3,2,0:T(8,128)(2,1)} fusion(bf16[8,768,2,96]{1,3,2,0:T(8,128)(2,1)} %get-tuple-element.118, s32[]{:T(128)} %get-tuple-element.117, f32[2,768,768]{1,2,0:T(8,128)} %get-tuple-element.109, f32[2,768]{1,0:T(2,128)S(1)} %get-tuple-element.110, bf16[8,768,96]{1,2,0:T(8,128)(2,1)} %get-tuple-element.125), kind=kOutput, calls=%fused_computation.13.clone.1 | convolution fusion | flops 228999168 | bytes 5168128 | tf_op jit(solution)/shard_map/while/body/eval_jaxpr/gqs,sd->qgd/dot_general | solution.py:49
  204.1 4.9 %fusion.94 = (f32[2,768]{1,0:T(2,128)S(1)}, f32[2,768,768]{1,2,0:T(8,128)}) fusion(pred[768,768]{0,1:T(8,128)(4,1)S(1)} %iota_compare_fusion.2, bf16[8,768,2,96]{1,3,2,0:T(8,128)(2,1)} %get-tuple-element.127, s32[]{:T(128)} %get-tuple-element.117, bf16[8,768,96]{1,2,0:T(8,128)(2,1)S(1)} %get-tuple-element.126), kind=kOutput, calls=%fused_computation.84.clone.1 | convolution fusion | flops 231211776 | bytes 5757952 | tf_op jit(solution)/shard_map/while/body/eval_jaxpr/sub | solution.py:47
  209.0 3.7 %fusion.95 = bf16[8,768,2,96]{1,3,2,0:T(8,128)(2,1)} fusion(bf16[8,768,2,96]{1,3,2,0:T(8,128)(2,1)} %get-tuple-element.118, s32[]{:T(128)} %get-tuple-element.117, f32[2,768,768]{1,2,0:T(8,128)} %get-tuple-element.109, f32[2,768]{1,0:T(2,128)S(1)} %get-tuple-element.110, bf16[8,768,96]{1,2,0:T(8,128)(2,1)} %get-tuple-element.125), kind=kOutput, calls=%fused_computation.13.clone.1 | convolution fusion | flops 228999168 | bytes 5168128 | tf_op jit(solution)/shard_map/while/body/eval_jaxpr/gqs,sd->qgd/dot_general | solution.py:49
  212.9 4.9 %fusion.94 = (f32[2,768]{1,0:T(2,128)S(1)}, f32[2,768,768]{1,2,0:T(8,128)}) fusion(pred[768,768]{0,1:T(8,128)(4,1)S(1)} %iota_compare_fusion.2, bf16[8,768,2,96]{1,3,2,0:T(8,128)(2,1)} %get-tuple-element.127, s32[]{:T(128)} %get-tuple-element.117, bf16[8,768,96]{1,2,0:T(8,128)(2,1)S(1)} %get-tuple-element.126), kind=kOutput, calls=%fused_computation.84.clone.1 | convolution fusion | flops 231211776 | bytes 5757952 | tf_op jit(solution)/shard_map/while/body/eval_jaxpr/sub | solution.py:47
  217.8 3.7 %fusion.95 = bf16[8,768,2,96]{1,3,2,0:T(8,128)(2,1)} fusion(bf16[8,768,2,96]{1,3,2,0:T(8,128)(2,1)} %get-tuple-element.118, s32[]{:T(128)} %get-tuple-element.117, f32[2,768,768]{1,2,0:T(8,128)} %get-tuple-element.109, f32[2,768]{1,0:T(2,128)S(1)} %get-tuple-element.110, bf16[8,768,96]{1,2,0:T(8,128)(2,1)} %get-tuple-element.125), kind=kOutput, calls=%fused_computation.13.clone.1 | convolution fusion | flops 228999168 | bytes 5168128 | tf_op jit(solution)/shard_map/while/body/eval_jaxpr/gqs,sd->qgd/dot_general | solution.py:49
  221.6 4.9 %fusion.94 = (f32[2,768]{1,0:T(2,128)S(1)}, f32[2,768,768]{1,2,0:T(8,128)}) fusion(pred[768,768]{0,1:T(8,128)(4,1)S(1)} %iota_compare_fusion.2, bf16[8,768,2,96]{1,3,2,0:T(8,128)(2,1)} %get-tuple-element.127, s32[]{:T(128)} %get-tuple-element.117, bf16[8,768,96]{1,2,0:T(8,128)(2,1)S(1)} %get-tuple-element.126), kind=kOutput, calls=%fused_computation.84.clone.1 | convolution fusion | flops 231211776 | bytes 5757952 | tf_op jit(solution)/shard_map/while/body/eval_jaxpr/sub | solution.py:47
  226.6 3.7 %fusion.95 = bf16[8,768,2,96]{1,3,2,0:T(8,128)(2,1)} fusion(bf16[8,768,2,96]{1,3,2,0:T(8,128)(2,1)} %get-tuple-element.118, s32[]{:T(128)} %get-tuple-element.117, f32[2,768,768]{1,2,0:T(8,128)} %get-tuple-element.109, f32[2,768]{1,0:T(2,128)S(1)} %get-tuple-element.110, bf16[8,768,96]{1,2,0:T(8,128)(2,1)} %get-tuple-element.125), kind=kOutput, calls=%fused_computation.13.clone.1 | convolution fusion | flops 228999168 | bytes 5168128 | tf_op jit(solution)/shard_map/while/body/eval_jaxpr/gqs,sd->qgd/dot_general | solution.py:49
  230.4 4.9 %fusion.94 = (f32[2,768]{1,0:T(2,128)S(1)}, f32[2,768,768]{1,2,0:T(8,128)}) fusion(pred[768,768]{0,1:T(8,128)(4,1)S(1)} %iota_compare_fusion.2, bf16[8,768,2,96]{1,3,2,0:T(8,128)(2,1)} %get-tuple-element.127, s32[]{:T(128)} %get-tuple-element.117, bf16[8,768,96]{1,2,0:T(8,128)(2,1)S(1)} %get-tuple-element.126), kind=kOutput, calls=%fused_computation.84.clone.1 | convolution fusion | flops 231211776 | bytes 5757952 | tf_op jit(solution)/shard_map/while/body/eval_jaxpr/sub | solution.py:47
  235.3 3.7 %fusion.95 = bf16[8,768,2,96]{1,3,2,0:T(8,128)(2,1)} fusion(bf16[8,768,2,96]{1,3,2,0:T(8,128)(2,1)} %get-tuple-element.118, s32[]{:T(128)} %get-tuple-element.117, f32[2,768,768]{1,2,0:T(8,128)} %get-tuple-element.109, f32[2,768]{1,0:T(2,128)S(1)} %get-tuple-element.110, bf16[8,768,96]{1,2,0:T(8,128)(2,1)} %get-tuple-element.125), kind=kOutput, calls=%fused_computation.13.clone.1 | convolution fusion | flops 228999168 | bytes 5168128 | tf_op jit(solution)/shard_map/while/body/eval_jaxpr/gqs,sd->qgd/dot_general | solution.py:49
  239.2 4.9 %fusion.94 = (f32[2,768]{1,0:T(2,128)S(1)}, f32[2,768,768]{1,2,0:T(8,128)}) fusion(pred[768,768]{0,1:T(8,128)(4,1)S(1)} %iota_compare_fusion.2, bf16[8,768,2,96]{1,3,2,0:T(8,128)(2,1)} %get-tuple-element.127, s32[]{:T(128)} %get-tuple-element.117, bf16[8,768,96]{1,2,0:T(8,128)(2,1)S(1)} %get-tuple-element.126), kind=kOutput, calls=%fused_computation.84.clone.1 | convolution fusion | flops 231211776 | bytes 5757952 | tf_op jit(solution)/shard_map/while/body/eval_jaxpr/sub | solution.py:47
  244.1 3.7 %fusion.95 = bf16[8,768,2,96]{1,3,2,0:T(8,128)(2,1)} fusion(bf16[8,768,2,96]{1,3,2,0:T(8,128)(2,1)} %get-tuple-element.118, s32[]{:T(128)} %get-tuple-element.117, f32[2,768,768]{1,2,0:T(8,128)} %get-tuple-element.109, f32[2,768]{1,0:T(2,128)S(1)} %get-tuple-element.110, bf16[8,768,96]{1,2,0:T(8,128)(2,1)} %get-tuple-element.125), kind=kOutput, calls=%fused_computation.13.clone.1 | convolution fusion | flops 228999168 | bytes 5168128 | tf_op jit(solution)/shard_map/while/body/eval_jaxpr/gqs,sd->qgd/dot_general | solution.py:49
  247.9 4.9 %fusion.94 = (f32[2,768]{1,0:T(2,128)S(1)}, f32[2,768,768]{1,2,0:T(8,128)}) fusion(pred[768,768]{0,1:T(8,128)(4,1)S(1)} %iota_compare_fusion.2, bf16[8,768,2,96]{1,3,2,0:T(8,128)(2,1)} %get-tuple-element.127, s32[]{:T(128)} %get-tuple-element.117, bf16[8,768,96]{1,2,0:T(8,128)(2,1)S(1)} %get-tuple-element.126), kind=kOutput, calls=%fused_computation.84.clone.1 | convolution fusion | flops 231211776 | bytes 5757952 | tf_op jit(solution)/shard_map/while/body/eval_jaxpr/sub | solution.py:47
  252.9 3.7 %fusion.95 = bf16[8,768,2,96]{1,3,2,0:T(8,128)(2,1)} fusion(bf16[8,768,2,96]{1,3,2,0:T(8,128)(2,1)} %get-tuple-element.118, s32[]{:T(128)} %get-tuple-element.117, f32[2,768,768]{1,2,0:T(8,128)} %get-tuple-element.109, f32[2,768]{1,0:T(2,128)S(1)} %get-tuple-element.110, bf16[8,768,96]{1,2,0:T(8,128)(2,1)} %get-tuple-element.125), kind=kOutput, calls=%fused_computation.13.clone.1 | convolution fusion | flops 228999168 | bytes 5168128 | tf_op jit(solution)/shard_map/while/body/eval_jaxpr/gqs,sd->qgd/dot_general | solution.py:49
  256.5 7.0 %convolution_convert_fusion = bf16[772,1536]{1,0:T(8,128)(2,1)S(1)} fusion(bf16[1536,1536]{1,0:T(8,128)(2,1)} %all-gather.5.cloned.1.call-done, bf16[4,1536]{0,1:T(8,128)(2,1)S(1)} %bitcast.90, bf16[768,1536]{0,1:T(8,128)(2,1)} %bitcast.94), kind=kOutput, calls=%fused_computation.36 | convolution fusion | flops 3648681984 | bytes 9461760 | tf_op jit(solution)/shard_map/dot_general | solution.py:126
  (60 shorter events, 17.6 us)
Async XLA Ops:
  7.2 47.2 %copy-start.7 = (s32[4]{0:T(128)S(1)}, s32[4]{0:T(128)}, u32[]{:S(2)}) copy-start(s32[4]{0:T(128)} %param.17) | copy-start | bytes 52
  7.2 89.4 %all-gather.3.cloned.1.call-start = ((), (), s32[]{:S(2)}) async-start(), calls=%async_computation | async-start | bytes 9732096 | tf_op jit(solution)/shard_map/all_gather | solution.py:62
  7.9 248.6 %all-gather.5.cloned.1.call-start = ((), (), s32[]{:S(2)}) async-start(), calls=%async_computation.1 | async-start | bytes 4866048 | tf_op jit(solution)/shard_map/all_gather | solution.py:128
  58.2 38.3 %copy-start.6 = (bf16[4,1536]{1,0:T(4,128)(2,1)S(1)}, bf16[4,1536]{1,0:T(4,128)(2,1)}, u32[]{:S(2)}) copy-start(bf16[4,1536]{1,0:T(4,128)(2,1)} %param.11) | copy-start | bytes 36868
  63.6 56.2 %copy-start.2 = (f32[772,48]{0,1:T(8,128)}, f32[772,48]{0,1:T(8,128)S(1)}, u32[]{:S(2)}) copy-start(f32[772,48]{0,1:T(8,128)S(1)} %get-tuple-element.70) | copy-start | bytes 444676
  63.6 56.2 %copy-start.3 = (f32[772,48]{0,1:T(8,128)}, f32[772,48]{0,1:T(8,128)S(1)}, u32[]{:S(2)}) copy-start(f32[772,48]{0,1:T(8,128)S(1)} %get-tuple-element.71) | copy-start | bytes 444676
  125.1 26.2 %copy-start.5 = (pred[4,512]{1,0:T(4,128)(4,1)S(1)}, pred[4,512]{1,0:T(4,128)(4,1)}, u32[]{:S(2)}) copy-start(pred[4,512]{1,0:T(4,128)(4,1)} %broadcast_compare_fusion) | copy-start | bytes 6148
  126.5 24.8 %copy-start.4 = (f32[4,8,2,512]{3,2,1,0:T(2,128)}, f32[4,8,2,512]{3,2,1,0:T(2,128)S(1)}, u32[]{:S(2)}) copy-start(f32[4,8,2,512]{3,2,1,0:T(2,128)S(1)} %get-tuple-element.73) | copy-start | bytes 393220
  155.1 0.9 copy-start
  156.0 27.2 %copy-start.1 = (bf16[772,8,48]{0,2,1:T(8,128)(2,1)S(1)}, bf16[772,8,48]{0,2,1:T(8,128)(2,1)}, u32[]{:S(2)}) copy-start(bf16[772,8,48]{0,2,1:T(8,128)(2,1)} %copy-done) | copy-start | bytes 1778692
Sparse Core Ops, SparseCore 0:
  10.9 85.5 all-gather.2
  99.4 62.4 all-gather.4
where the time goes:
time: 274 us; the launch traced here: 273 us
  matrix products  93.2 us (34%)
  blocking collectives  90.2 us (33%)
  waiting for transfers between devices  34.3 us (13%)
  local copies, waits for them, and re-layouts  27.7 us (10%)
  between operations  14.3 us (5%)
  other arithmetic  12.8 us (5%)
    unnamed x1, blocking collectives  42.5 us
    sub x8, matrix products, one_head(): expanded = jnp.exp(scores - highest)  39.4 us
    all_gather x1, waiting for transfers between devices, per_device(): weight_rows = lax.all_gather(wqkv, ('dp', 'shard'), axis=0, tiled=True)  33 us
    dot_general x8, matrix products, one_head(): jnp.einsum('gqs,sd->qgd', weights, value_head, preferred_element_type=jnp...  29.3 us
    pmax x1, blocking collectives, per_device(): group_top = lax.pmax(block_peaks, 'shard')  24.8 us
    psum x1, blocking collectives, per_device(): lax.psum((partial_sums * rescale[..., None], partial_totals * rescale), '...  22.9 us
    dot_general x1, matrix products, per_device(): jnp.dot(left_side, weight_rows, preferred_element_type=jnp.float32)  13.1 us
    unnamed x20, local copies, waits for them, and re-layouts  9.58 us
  transfers between devices with their start and end apart: 2, of which 1 were waited for; matrix products, arithmetic and copies ran while one was open for 45% of the time, Pallas kernels for 0%

commit v1 on v0

v1 whole, which is shorter than its diff:
```python
import functools

import jax
import jax.numpy as jnp
from jax import lax
from jax.experimental import pallas as pl
from jax.experimental.pallas import tpu as pltpu
from jax.sharding import PartitionSpec as P

H = 16
KV = 8
HD = 96
HALF = HD // 2
LANES = 128
PAD = H * LANES

THETA = 100000.0
EPS = 1e-05
NEGATIVE = -1e30
SCALE = HD ** (-0.5)
LOG2E = 1.4426950408889634

BF16 = jnp.bfloat16
F32 = jnp.float32
VMEM_BYTES = 56 * 1024 * 1024


def rope_tables(positions, width):
    lane = jnp.arange(width, dtype=jnp.int32)
    lane = lane % HD if width % HD == 0 else lane
    frequency = jnp.power(THETA, -(lane % HALF).astype(F32) * (2.0 / HD))
    angles = positions.astype(F32)[:, None] * frequency[None, :]
    cosine, sine = jnp.cos(angles), jnp.sin(angles)
    lane = lane[None, :]
    return jnp.stack(
        [
            jnp.where(lane < HD, cosine, 0.0),
            jnp.where((lane >= HALF) & (lane < HD), sine, 0.0),
            jnp.where(lane < HALF, -sine, 0.0),
        ]
    )


def normalize(rows, gain):
    widened = rows.astype(F32)
    factor = lax.rsqrt(jnp.mean(widened * widened, axis=-1, keepdims=True) + EPS)
    return (widened * factor * gain).astype(BF16)


def project_kernel(block_rows, plan, rope, offs_ref, *rest):
    count = 1 + max(source[0] for sources in plan for source in sources)
    w_refs, rest = rest[:count], rest[count:]
    if rope:
        xn_ref, table_ref, dtable_ref, heads_ref, dec_ref, w_ref, *u_refs, w_sem = rest
    else:
        x_ref, sib_ref, dx_ref, table_ref, dtable_ref, heads_ref, dec_ref, xn_ref, w_ref, *u_refs, gain_ref, w_sem = rest
    half = KV * HD // 2
    width = 2 * half
    rows_all = xn_ref.shape[0]
    main = heads_ref.shape[1]
    stretch = main // 2

    for t, sources in enumerate(plan):
        for ref, column, first, blocks in sources:
            for b in range(blocks):
                rows = pl.ds(pl.multiple_of(offs_ref[first + b], 16), block_rows)
                pltpu.make_async_copy(
                    w_refs[ref].at[pl.ds(b * block_rows, block_rows), pl.ds(column, half if t < 2 else LANES)],
                    w_ref.at[rows, pl.ds(t * half, half)] if t < 2 else gain_ref.at[rows],
                    w_sem.at[t // 2],
                ).start()

    if not rope:
        pltpu.make_async_copy(gain_ref, gain_ref, w_sem.at[1]).wait()
        pick = (lax.broadcasted_iota(jnp.int32, (8, LANES), 1) == 0).astype(BF16)
        gain = lax.dot_general(pick, gain_ref[...], (((1,), (1,)), ((), ())), preferred_element_type=F32)[0:1]

        def body(i, _):
            rows = pl.ds(pl.multiple_of(i * 64, 64), 64)
            xn_ref[rows, :] = normalize(x_ref[rows, :], gain)
            xn_ref[pl.ds(pl.multiple_of(i * 64 + stretch, 64), 64), :] = normalize(sib_ref[rows, :], gain)
            return 0

        lax.fori_loop(0, stretch // 64, body, 0)
        xn_ref[main:, :] = normalize(dx_ref[...], gain)

    pltpu.make_async_copy(w_ref, w_ref, w_sem.at[0]).wait()

    chunk = 256
    lane = lax.broadcasted_iota(jnp.int32, (chunk, LANES), 1)
    for i in range(main // chunk):
        u_ref = u_refs[i % 2]
        first, last = i * chunk, (i + 1) * chunk
        whole = slice(first, last if last < main else rows_all)
        for n in range(width // 256):
            u_ref[: whole.stop - first, n * 256 : (n + 1) * 256] = jnp.dot(
                xn_ref[whole, :], w_ref[:, n * 256 : (n + 1) * 256], preferred_element_type=F32
            )
        at = slice(first % stretch, first % stretch + chunk)
        for h in range(8):
            u = head_tile(u_ref, slice(0, chunk), h)
            if rope or h < 4:
                u = (
                    u * table_ref[0, at, :]
                    + pltpu.roll(u, HALF, 1) * table_ref[1, at, :]
                    + pltpu.roll(u, LANES - HALF, 1) * table_ref[2, at, :]
                )
            else:
                u = jnp.where(lane < HD, u, 1.0)
            heads_ref[h, first:last, :] = u.astype(BF16)
        if last == main:
            u = u_ref[chunk : chunk + rows_all - main, :]
            turned = (
                u * dtable_ref[0]
                + pltpu.roll(u, HALF, 1) * dtable_ref[1]
                + pltpu.roll(u, width - HALF, 1) * dtable_ref[2]
            )
            dec_ref[...] = turned.astype(BF16)


def project(rope, operands, tables, dtable, offs, w_pieces, block_rows, plan):
    depth = operands[0].shape[1]
    rows_all = sum(operand.shape[0] for operand in operands)
    width = KV * HD
    extra = dtable.shape[1]
    main = rows_all - extra
    smem = pl.BlockSpec(memory_space=pltpu.SMEM)
    vmem = pl.BlockSpec(memory_space=pltpu.VMEM)
    hbm = pl.BlockSpec(memory_space=pl.ANY)
    out_shape = [
        jax.ShapeDtypeStruct((8, main, LANES), BF16),
        jax.ShapeDtypeStruct((extra, width), BF16),
    ]
    scratch = [pltpu.VMEM((depth, width), BF16)] + [pltpu.VMEM((256 + extra, width), F32)] * 2
    if not rope:
        out_shape.append(jax.ShapeDtypeStruct((rows_all, depth), BF16))
        scratch.append(pltpu.VMEM((depth, LANES), BF16))
    return pl.pallas_call(
        functools.partial(project_kernel, block_rows, plan, rope),
        in_specs=[smem] + [hbm] * len(w_pieces) + [vmem] * (len(operands) + 2),
        out_specs=[vmem] * len(out_shape),
        out_shape=out_shape,
        scratch_shapes=scratch + [pltpu.SemaphoreType.DMA((2,))],
        compiler_params=pltpu.CompilerParams(vmem_limit_bytes=VMEM_BYTES),
        cost_estimate=pl.CostEstimate(
            flops=2 * rows_all * depth * width, bytes_accessed=12_000_000, transcendentals=0
        ),
        name="project_q" if rope else "project_kv",
    )(offs, *w_pieces, *operands, tables, dtable)


def head_tile(u_ref, rows, index):
    base, place = (index // 4) * 3 * LANES, index % 4
    lane = lax.broadcasted_iota(jnp.int32, (rows.stop - rows.start, LANES), 1)

    def tile(t):
        return u_ref[rows, base + t * LANES : base + (t + 1) * LANES]

    if place == 0:
        return tile(0)
    if place == 1:
        return pltpu.roll(jnp.where(lane >= 96, tile(0), tile(1)), 32, 1)
    if place == 2:
        return pltpu.roll(jnp.where(lane >= 64, tile(1), tile(2)), 64, 1)
    return pltpu.roll(tile(2), 96, 1)


def decode_kernel(core_ref, len_ref, start_ref, mine_ref, other_ref, k_ref, v_ref, part_ref, self_ref, query_ref):
    step = pl.program_id(0)
    requests, span, width = pl.num_programs(0), k_ref.shape[1], k_ref.shape[2]
    half = width // 2
    count = self_ref.shape[1] // 2

    @pl.when(step == 0)
    def _():
        mine, other = mine_ref[...].astype(F32), other_ref[...].astype(F32)
        mine_first = core_ref[0] == 0
        low, high = jnp.where(mine_first, mine, other), jnp.where(mine_first, other, mine)
        own_k = jnp.concatenate([low[:, width : width + half], high[:, width : width + half]], axis=1)
        own_v = jnp.concatenate([low[:, width + half :], high[:, width + half :]], axis=1)
        at_lane = lax.broadcasted_iota(jnp.int32, own_k.shape, 1) // HD
        for parity in range(2):
            query = jnp.concatenate(
                [side[:, h * HD : (h + 1) * HD] for side in (low, high) for h in range(parity, 8, 2)], axis=1
            )
            query_ref[parity] = query
            product = query * own_k
            own = jnp.zeros(own_k.shape, F32)
            for j in range(KV):
                here = at_lane == j
                own = own + jnp.where(
                    here, jnp.sum(jnp.where(here, product, 0.0), axis=-1, keepdims=True), 0.0
                )
            self_ref[0, parity * count : (parity + 1) * count, :] = own[:count] * SCALE
            self_ref[1, parity * count : (parity + 1) * count, :] = own_v[:count]

    diagonal = (
        lax.broadcasted_iota(jnp.int32, (KV, width), 1) // HD
        == lax.broadcasted_iota(jnp.int32, (KV, width), 0)
    )
    query = jnp.concatenate(
        [
            jnp.where(diagonal, jnp.broadcast_to(query_ref[p, pl.ds(step, 1), :], (KV, width)), 0.0)
            for p in range(2)
        ],
        axis=0,
    ).astype(BF16)
    scores = (
        lax.dot_general(query, k_ref[0], (((1,), (1,)), ((), ())), preferred_element_type=F32) * SCALE
    )
    live = lax.broadcasted_iota(jnp.int32, (H, span), 1) + start_ref[0] < len_ref[step]
    scores = jnp.where(live, scores, NEGATIVE)
    peak = jnp.max(scores, axis=-1, keepdims=True)
    expanded = jnp.where(live, jnp.exp(scores - peak), 0.0)
    total = jnp.sum(expanded, axis=-1, keepdims=True)
    sums = jnp.dot(expanded.astype(BF16), v_ref[0], preferred_element_type=F32)
    for slot, values in enumerate((sums, peak, total)):
        for parity in range(2):
            part_ref[slot, pl.ds(parity * requests + step, 1), :] = jnp.sum(
                jnp.where(diagonal, values[parity * KV : (parity + 1) * KV], 0.0), axis=0, keepdims=True
            )


def decode(core, cache_len, start, mine, other, k_cache, v_cache):
    requests, span, width = k_cache.shape
    smem = pl.BlockSpec(memory_space=pltpu.SMEM)
    vmem = pl.BlockSpec(memory_space=pltpu.VMEM)
    block = pl.BlockSpec((1, span, width), lambda r: (r, 0, 0))
    return pl.pallas_call(
        decode_kernel,
        grid=(requests,),
        in_specs=[smem] * 3 + [vmem] * 2 + [block] * 2,
        out_specs=[vmem] * 2,
        out_shape=[
            jax.ShapeDtypeStruct((3, 2 * requests, width), F32),
            jax.ShapeDtypeStruct((2, 2 * requests, width), F32),
        ],
        scratch_shapes=[pltpu.VMEM((2, mine.shape[0], width), F32)],
        compiler_params=pltpu.CompilerParams(
            dimension_semantics=("arbitrary",), vmem_limit_bytes=VMEM_BYTES
        ),
        cost_estimate=pl.CostEstimate(
            flops=2_000_000_000, bytes_accessed=2 * requests * span * width * 2, transcendentals=0
        ),
        name="decode",
    )(core, cache_len, start, mine, other, k_cache, v_cache)


def attend_kernel(block, q_ref, k_ref, v_ref, o_ref):
    stretch = o_ref.shape[0]
    causal = lax.broadcasted_iota(jnp.int32, (block, block), 1) <= lax.broadcasted_iota(
        jnp.int32, (block, block), 0
    )
    for parity in range(2):
        for i in range(stretch // block):
            rows = slice(i * block, (i + 1) * block)
            seen = (i + 1) * block
            scores = lax.dot_general(
                q_ref[parity, rows, :], k_ref[0, :seen, :], (((1,), (1,)), ((), ())),
                preferred_element_type=F32,
            )
            last = jnp.where(causal, scores[:, i * block :], NEGATIVE)
            scores = last if i == 0 else jnp.concatenate([scores[:, : i * block], last], axis=1)
            peak = jnp.max(scores, axis=-1, keepdims=True)
            weights = jnp.exp2((scores - peak) * (SCALE * LOG2E)).astype(BF16)
            mixed = jnp.dot(weights, v_ref[0, :seen, :], preferred_element_type=F32)
            o_ref[rows, parity * LANES : (parity + 1) * LANES] = (mixed / mixed[:, HD : HD + 1]).astype(BF16)


def attend(queries, keys_values, which):
    stretch = queries.shape[1] // 2
    return pl.pallas_call(
        functools.partial(attend_kernel, 256),
        grid=(KV // 2,),
        in_specs=[
            pl.BlockSpec((2, stretch, LANES), lambda j: (j, which, 0)),
            pl.BlockSpec((1, stretch, LANES), lambda j: (j, which, 0)),
            pl.BlockSpec((1, stretch, LANES), lambda j: (KV // 2 + j, which, 0)),
        ],
        out_specs=pl.BlockSpec((stretch, 2 * LANES), lambda j: (0, j)),
        out_shape=jax.ShapeDtypeStruct((stretch, PAD // 2), BF16),
        compiler_params=pltpu.CompilerParams(
            dimension_semantics=("arbitrary",), vmem_limit_bytes=VMEM_BYTES
        ),
        cost_estimate=pl.CostEstimate(
            flops=10_000_000_000, bytes_accessed=5_000_000, transcendentals=H // 2 * stretch * stretch
        ),
        name="attend",
    )(queries, keys_values, keys_values)


def output_kernel(requests, core_ref, wo_hbm, mine_hbm, other_hbm, part_ref, self_ref, out_ref, dec_ref, wo_ref, att_ref, w_sem, o_sem):
    step = pl.program_id(0)
    stretch = out_ref.shape[0]
    columns = out_ref.shape[1]
    steps = wo_ref.shape[0]
    half = PAD // 2

    @pl.when(step == 0)
    def _():
        core = core_ref[0]
        o_copies = [
            pltpu.make_async_copy(source, att_ref.at[place, pl.ds(0, stretch)], o_sem.at[n])
            for n, (source, place) in enumerate(((mine_hbm, core), (other_hbm, 1 - core)))
        ]
        for copy in o_copies:
            copy.start()
        for t in range(steps):
            for h in range(H):
                pltpu.make_async_copy(
                    wo_hbm.at[pl.ds(h * HD, HD), pl.ds(t * columns, columns)],
                    wo_ref.at[t, pl.ds(h * LANES, HD)],
                    w_sem.at[t],
                ).start()
        for t in range(steps):
            for h in range(H):
                wo_ref[t, h * LANES + HD : (h + 1) * LANES, :] = jnp.zeros((LANES - HD, columns), BF16)
        own, own_v = self_ref[0], self_ref[1]
        peak = part_ref[1]
        top = jnp.maximum(own, peak)
        rescale, own_weight = jnp.exp(peak - top), jnp.exp(own - top)
        mix = (part_ref[0] * rescale + own_weight * own_v) / (part_ref[2] * rescale + own_weight)
        extra = att_ref.shape[1] - stretch
        att_ref[:, stretch:, :] = jnp.zeros((2, extra, half), BF16)
        for parity in range(2):
            mine = mix[parity * requests : (parity + 1) * requests]
            mine = jnp.concatenate([mine, jnp.zeros((extra - requests, mine.shape[1]), F32)], axis=0)
            for j in range(KV):
                h = 2 * j + parity
                at = h % 8 * LANES
                att_ref[h // 8, stretch:, at : at + HD] = mine[:, j * HD : (j + 1) * HD].astype(BF16)
        for copy in o_copies:
            copy.wait()

    for t in range(steps):
        @pl.when(step == t)
        def _():
            whole = wo_ref.at[t, pl.ds(0, H * HD)]
            pltpu.make_async_copy(whole, whole, w_sem.at[t]).wait()

    projected = jnp.dot(att_ref[0], wo_ref[step, :half], preferred_element_type=F32) + jnp.dot(
        att_ref[1], wo_ref[step, half:], preferred_element_type=F32
    )
    out_ref[...] = projected[:stretch].astype(BF16)
    dec_ref[...] = projected[stretch : stretch + requests].astype(BF16)


def output(mine, other, part, own, core, wo_all, requests):
    stretch = mine.shape[0]
    width = wo_all.shape[1]
    steps, extra = 3, 16
    smem = pl.BlockSpec(memory_space=pltpu.SMEM)
    vmem = pl.BlockSpec(memory_space=pltpu.VMEM)
    hbm = pl.BlockSpec(memory_space=pl.ANY)
    return pl.pallas_call(
        functools.partial(output_kernel, requests),
        grid=(steps,),
        in_specs=[smem] + [hbm] * 3 + [vmem] * 2,
        out_specs=[
            pl.BlockSpec((stretch, width // steps), lambda t: (0, t)),
            pl.BlockSpec((requests, width // steps), lambda t: (0, t)),
        ],
        out_shape=[
            jax.ShapeDtypeStruct((stretch, width), BF16),
            jax.ShapeDtypeStruct((requests, width), BF16),
        ],
        scratch_shapes=[
            pltpu.VMEM((steps, PAD, width // steps), BF16),
            pltpu.VMEM((2, stretch + extra, PAD // 2), BF16),
            pltpu.SemaphoreType.DMA((steps,)),
            pltpu.SemaphoreType.DMA((2,)),
        ],
        compiler_params=pltpu.CompilerParams(
            dimension_semantics=("arbitrary",), vmem_limit_bytes=VMEM_BYTES
        ),
        cost_estimate=pl.CostEstimate(
            flops=2 * stretch * PAD * width, bytes_accessed=12_000_000, transcendentals=0
        ),
        name="output",
    )(core, wo_all, mine, other, part, own)


def swap(array, mask, n_shard):
    return lax.ppermute(array, "shard", [(i, i ^ mask) for i in range(n_shard)])


def spread(local, cut, n_dp, n_shard):
    along = [local]
    for shift in range(1, n_dp):
        along.append(lax.ppermute(local, "dp", [((i + shift) % n_dp, i) for i in range(n_dp)]))
    here = jnp.concatenate(along, axis=0)
    whole = local.shape[1]
    beside, above = swap(here, 2, n_shard), swap(here, 4, n_shard)
    left, right = swap(beside[:, :cut], 4, n_shard), swap(above[:, cut:], 2, n_shard)
    return [(here, 0, 0, whole), (beside, 1, 0, whole), (above, 2, 0, whole), (left, 3, 0, cut), (right, 3, cut, whole)]


def merge(first, second):
    top = jnp.maximum(first[1], second[1])
    one, two = jnp.exp(first[1] - top), jnp.exp(second[1] - top)
    return jnp.stack([first[0] * one + second[0] * two, top, first[2] * one + second[2] * two])


def per_device(n_dp, n_shard, prefill_x, decode_x, norm_gain, wqkv, wo, k_cache, v_cache, cache_len):
    stretch = prefill_x.shape[0]
    requests, span, width = k_cache.shape
    half = width // 2
    me, me_dp = lax.axis_index("shard"), lax.axis_index("dp")
    core = me % 2
    everyone = ("dp", "shard")
    block_rows = wqkv.shape[0]
    low = [wqkv[:, 2 * width : 2 * width + half], wqkv[:, 3 * width : 3 * width + half], wqkv[:, :width]]
    high = [wqkv[:, 2 * width + half : 3 * width], wqkv[:, 3 * width + half :], wqkv[:, width : 2 * width]]
    low, high = jnp.concatenate(low, axis=1), jnp.concatenate(high, axis=1)
    gain_columns = jnp.broadcast_to(norm_gain[:, None], (block_rows, LANES))
    head = LANES + width
    split = n_shard == 8 and block_rows == HALF

    wo_all = lax.all_gather(wo, everyone, axis=0, tiled=True)
    sib_x = swap(prefill_x, 1, n_shard)
    kv_plan, q_plan = [[], [], []], [[], []]
    if split:
        first = core == 0
        mine = jnp.concatenate([gain_columns, jnp.where(first, low, high)], axis=1)
        theirs = jnp.concatenate([gain_columns, jnp.where(first, high, low)], axis=1)
        theirs = swap(theirs, 1, n_shard)
        pair = jnp.concatenate([jnp.where(first, mine, theirs), jnp.where(first, theirs, mine)], axis=0)
        order = jnp.arange(n_shard // 2 * n_dp, dtype=jnp.int32)
        chip = (me_dp + order % n_dp) % n_dp * (n_shard // 2) + (me // 2 ^ (order // n_dp))
        block_rows = 2 * block_rows
        offs = chip * block_rows
        kv_pieces = spread(pair[:, :head], LANES + half, n_dp, n_shard)
        later, _ = lax.optimization_barrier((pair[:, head:], kv_pieces[0][0]))
        q_pieces = spread(later, half, n_dp, n_shard)
        for pieces, plan, starts in (
            (kv_pieces, kv_plan, {LANES: 0, LANES + half: 1, 0: 2}),
            (q_pieces, q_plan, {0: 0, half: 1}),
        ):
            for index, (_, mask, left, right) in enumerate(pieces):
                for column, t in starts.items():
                    if left <= column < right:
                        plan[t].append((index, column - left, mask * n_dp, n_dp))
        kv_pieces, q_pieces = [piece[0] for piece in kv_pieces], [piece[0] for piece in q_pieces]
    else:
        offs = jnp.zeros((1,), jnp.int32)
        every = lax.all_gather(jnp.concatenate([gain_columns, low, high], axis=1), everyone, axis=0, tiled=True)
        block_rows = every.shape[0]
        chosen = jnp.where(core == 0, every[:, LANES : LANES + 2 * width], every[:, LANES + 2 * width :])
        kv_pieces = [jnp.concatenate([every[:, :LANES], chosen[:, :width]], axis=1)]
        q_pieces = [chosen[:, width:]]
        kv_plan = [[(0, LANES, 0, 1)], [(0, LANES + half, 0, 1)], [(0, 0, 0, 1)]]
        q_plan = [[(0, 0, 0, 1)], [(0, half, 0, 1)]]

    extra = 16
    dx = jnp.pad(decode_x, ((0, extra - requests), (0, 0)))
    decode_positions = jnp.concatenate([cache_len, jnp.zeros((extra - requests,), jnp.int32)])
    tables = rope_tables(jnp.arange(stretch, dtype=jnp.int32), LANES)
    q_table = rope_tables(decode_positions, width)
    plain = jnp.stack([jnp.ones((extra, half), F32)] + [jnp.zeros((extra, half), F32)] * 2)
    kv_table = jnp.concatenate([q_table[:, :, :half], plain], axis=2)
    keys_values, dec_kv, xn = project(
        False, [prefill_x, sib_x, dx], tables, kv_table, offs, kv_pieces, block_rows, kv_plan
    )
    queries, dec_q = project(True, [xn], tables, q_table, offs, q_pieces, block_rows, q_plan)
    dec = jnp.concatenate([dec_q, dec_kv], axis=1)
    dec_other = swap(dec, 1, n_shard)
    core = core.astype(jnp.int32).reshape(1)
    theirs = attend(queries, keys_values, 1)
    other = swap(theirs, 1, n_shard)
    part, own = decode(core, cache_len, (me * span).reshape(1), dec, dec_other, k_cache, v_cache)
    mask = 1
    while mask < n_shard:
        received = swap(part, mask, n_shard)
        lower = (me & mask) == 0
        part = merge(jnp.where(lower, part, received), jnp.where(lower, received, part))
        mask *= 2
    mine = attend(queries, keys_values, 0)
    return output(mine, other, part, own, core, wo_all, requests)


def solution(mesh):
    in_specs = (
        P(("dp", "shard"), None),
        P("dp", None),
        P(("dp", "shard")),
        P(("dp", "shard"), None),
        P(("dp", "shard"), None),
        P("dp", "shard", None),
        P("dp", "shard", None),
        P("dp"),
    )
    out_specs = (P(("dp", "shard"), None), P("dp", None))
    return jax.shard_map(
        functools.partial(per_device, mesh.shape["dp"], mesh.shape["shard"]),
        mesh=mesh, in_specs=in_specs, out_specs=out_specs, check_vma=False,
    )
```

time: 274 us -> 169 us (0.62)
  matrix products: 93.2 us -> 0 us
  blocking collectives: 90.2 us -> 0 us
  Pallas kernels: 0 us -> 63.3 us
  starting transfers between devices: 0.08 us -> 30 us
  local copies, waits for them, and re-layouts: 27.7 us -> 12.2 us
  waiting for transfers between devices: 34.3 us -> 41.2 us
  other arithmetic: 12.8 us -> 6.05 us
    pallas_call x0 -> x6, Pallas kernels: none -> 63.3 us  [the longest x2 26.1 us: project(): pl.pallas_call(functools.partial(project_kernel, block_rows, plan, rope),...]
    dot_general x13 -> x0, matrix products: 53.8 us -> none  [the longest x8 29.3 us: one_head(): jnp.einsum('gqs,sd->qgd', weights, value_head, preferred_element_type=jnp...]
    unnamed x1 -> x0, blocking collectives: 42.5 us -> none
    ppermute x0 -> x21, waiting for transfers between devices: none -> 40.5 us  [the longest x6 22.8 us: spread(): lax.ppermute(local, 'dp', [((i + shift) % n_dp, i) for i in range(n_dp)])]
    sub x8 -> x0, matrix products: 39.4 us -> none  [one_head(): expanded = jnp.exp(scores - highest)]
    all_gather x2 -> x1, waiting for transfers between devices: 33 us -> 0.01 us  [per_device(): wo_all = lax.all_gather(wo, everyone, axis=0, tiled=True)]
    ppermute x0 -> x21, starting transfers between devices: none -> 29.9 us  [the longest x15 18.6 us: swap(): return lax.ppermute(array, 'shard', [(i, i ^ mask) for i in range(n_shard)])]
    pmax x1 -> x0, blocking collectives: 24.8 us -> none  [per_device(): group_top = lax.pmax(block_peaks, 'shard')]
  transfers between devices with their start and end apart: 2 -> 22, of which waited for: 1 -> 8; matrix products, arithmetic and copies ran while one was open for 45% -> 9% of each run, Pallas kernels for 0% -> 32%
where the time goes in v1:
time: 169 us; the launch traced here: 167 us
  Pallas kernels  63.3 us (37%)
  waiting for transfers between devices  41.2 us (24%)
  starting transfers between devices  30 us (18%)
  between operations  14.4 us (9%)
  local copies, waits for them, and re-layouts  12.2 us (7%)
  other arithmetic  6.05 us (4%)
    pallas_call x2, Pallas kernels, project(): pl.pallas_call(functools.partial(project_kernel, block_rows, plan, rope),...  26.1 us
    ppermute x6, waiting for transfers between devices, spread(): lax.ppermute(local, 'dp', [((i + shift) % n_dp, i) for i in range(n_dp)])  22.8 us
    pallas_call x2, Pallas kernels, attend(): pl.pallas_call(functools.partial(attend_kernel, 256), grid=(KV // 2,), in...  21.9 us
    ppermute x15, starting transfers between devices, swap(): return lax.ppermute(array, 'shard', [(i, i ^ mask) for i in range(n_shard)])  18.6 us
    ppermute x15, waiting for transfers between devices, swap(): return lax.ppermute(array, 'shard', [(i, i ^ mask) for i in range(n_shard)])  17.7 us
    ppermute x6, starting transfers between devices, spread(): lax.ppermute(local, 'dp', [((i + shift) % n_dp, i) for i in range(n_dp)])  11.3 us
    pallas_call x1, Pallas kernels, output(): pl.pallas_call(functools.partial(output_kernel, requests), grid=(steps,),...  9.7 us
    pallas_call x1, Pallas kernels, decode(): pl.pallas_call(decode_kernel, grid=(requests,), in_specs=[smem] * 3 + [vm...  5.59 us
  transfers between devices with their start and end apart: 22, of which 8 were waited for; matrix products, arithmetic and copies ran while one was open for 9% of the time, Pallas kernels for 32%

profile of v1, /device:TPU:0, one launch (start us, length us, event | category | flops | bytes accessed | tf_op | source)
XLA Modules:
  0.0 167.1 jit_solution(10825503295187919801)
XLA Ops:
  11.2 1.5 fusion.3
  12.8 5.1 %collective-permute-start.1 = (bf16[96,896]{1,0:T(8,128)(2,1)S(1)}, bf16[96,896]{1,0:T(8,128)(2,1)S(1)}, u32[]{:S(2)}, u32[]{:S(2)}) collective-permute-start(bf16[96,896]{1,0:T(8,128)(2,1)S(1)} %pad_maximum_fusion.4), channel_id=1, source_target_pairs={{8,0},{16,8},{24,16},{0,24},{9,1},{17,9},{25,17},{1,25},{10,2},{18... | collective-permute-start | bytes 516104 | tf_op jit(solution)/shard_map/ppermute | solution.py:390
  17.9 1.0 collective-permute-start.3
  18.9 3.8 %collective-permute-done.1 = bf16[96,896]{1,0:T(8,128)(2,1)S(1)} collective-permute-done((bf16[96,896]{1,0:T(8,128)(2,1)S(1)}, bf16[96,896]{1,0:T(8,128)(2,1)S(1)}, u32[]{:S(2)}, u32[]{:S(2)}) %collective-permute-start.1) | collective-permute-done | bytes 172064 | tf_op jit(solution)/shard_map/ppermute | solution.py:390
  22.7 12.7 %collective-permute-done.2 = bf16[96,896]{1,0:T(8,128)(2,1)S(1)} collective-permute-done((bf16[96,896]{1,0:T(8,128)(2,1)S(1)}, bf16[96,896]{1,0:T(8,128)(2,1)S(1)}, u32[]{:S(2)}, u32[]{:S(2)}) %collective-permute-start.2) | collective-permute-done | bytes 172064 | tf_op jit(solution)/shard_map/ppermute | solution.py:390
  35.6 1.5 collective-permute-start.11
  37.1 1.6 collective-permute-start.12
  38.7 3.2 %collective-permute-start.5 = (bf16[96,768]{1,0:T(8,128)(2,1)S(1)}, bf16[96,768]{1,0:T(8,128)(2,1)S(1)}, u32[]{:S(2)}, u32[]{:S(2)}) collective-permute-start(bf16[96,768]{1,0:T(8,128)(2,1)S(1)} %pad_maximum_fusion.5), channel_id=1, source_target_pairs={{16,0},{24,8},{0,16},{8,24},{17,1},{25,9},{1,17},{9,25},{18,2},{26... | collective-permute-start | bytes 442376 | tf_op jit(solution)/shard_map/ppermute | solution.py:390
  42.5 1.9 %collective-permute-start.6 = (bf16[96,768]{1,0:T(8,128)(2,1)S(1)}, bf16[96,768]{1,0:T(8,128)(2,1)S(1)}, u32[]{:S(2)}, u32[]{:S(2)}) collective-permute-start(bf16[96,768]{1,0:T(8,128)(2,1)S(1)} %pad_maximum_fusion.5), channel_id=1, source_target_pairs={{24,0},{0,8},{8,16},{16,24},{25,1},{1,9},{9,17},{17,25},{26,2},{2,... | collective-permute-start | bytes 442376 | tf_op jit(solution)/shard_map/ppermute | solution.py:390
  45.1 6.3 %collective-permute-done.5 = bf16[96,768]{1,0:T(8,128)(2,1)S(1)} collective-permute-done((bf16[96,768]{1,0:T(8,128)(2,1)S(1)}, bf16[96,768]{1,0:T(8,128)(2,1)S(1)}, u32[]{:S(2)}, u32[]{:S(2)}) %collective-permute-start.5) | collective-permute-done | bytes 147488 | tf_op jit(solution)/shard_map/ppermute | solution.py:390
  52.7 2.4 %collective-permute-start.8 = (bf16[384,768]{1,0:T(8,128)(2,1)}, bf16[384,768]{1,0:T(8,128)(2,1)}, u32[]{:S(2)}, u32[]{:S(2)}) collective-permute-start(bf16[384,768]{1,0:T(8,128)(2,1)} %constant_dynamic-update-slice_fusion.rest_0_), channel_id=1, source_target_pairs={{0,4},{1,5},{2,6},{3,7},{4,0},{5,1},{6,2},{7,3},{8,12},{9,13},{10,... | collective-permute-start | bytes 1769480 | tf_op jit(solution)/shard_map/ppermute | solution.py:384
  55.1 1.4 collective-permute-start.7
  56.8 1.6 collective-permute-start.13
  58.5 1.0 slice.133
  59.6 2.5 %collective-permute-start.14 = (bf16[384,384]{1,0:T(8,128)(2,1)S(1)}, bf16[384,384]{1,0:T(8,128)(2,1)S(1)}, u32[]{:S(2)}, u32[]{:S(2)}) collective-permute-start(bf16[384,384]{1,0:T(8,128)(2,1)S(1)} %slice.133), channel_id=1, source_target_pairs={{0,2},{1,3},{2,0},{3,1},{4,6},{5,7},{6,4},{7,5},{8,10},{9,11},{10,... | collective-permute-start | bytes 884744 | tf_op jit(solution)/shard_map/ppermute | solution.py:384
  63.9 1.1 pad_maximum_fusion.rest_8_.rest_6_
  65.0 4.9 %collective-permute-done.8.rest_2_ = bf16[384,768]{1,0:T(8,128)(2,1)} collective-permute-done((bf16[384,768]{1,0:T(8,128)(2,1)}, bf16[384,768]{1,0:T(8,128)(2,1)}, u32[]{:S(2)}, u32[]{:S(2)}) %collective-permute-start.8) | collective-permute-done | bytes 589856 | tf_op jit(solution)/shard_map/ppermute | solution.py:384
  70.9 1.8 %collective-permute-start.10 = (bf16[384,384]{1,0:T(8,128)(2,1)S(1)}, bf16[384,384]{1,0:T(8,128)(2,1)S(1)}, u32[]{:S(2)}, u32[]{:S(2)}) collective-permute-start(bf16[384,384]{1,0:T(8,128)(2,1)S(1)} %slice.131), channel_id=1, source_target_pairs={{0,2},{1,3},{2,0},{3,1},{4,6},{5,7},{6,4},{7,5},{8,10},{9,11},{10,... | collective-permute-start | bytes 884744 | tf_op jit(solution)/shard_map/ppermute | solution.py:384
  73.8 1.5 collective-permute-start.9
  75.2 8.5 %collective-permute-done.14.rest_4_ = bf16[384,384]{1,0:T(8,128)(2,1)S(1)} collective-permute-done((bf16[384,384]{1,0:T(8,128)(2,1)S(1)}, bf16[384,384]{1,0:T(8,128)(2,1)S(1)}, u32[]{:S(2)}, u32[]{:S(2)}) %collective-permute-start.14) | collective-permute-done | bytes 294944 | tf_op jit(solution)/shard_map/ppermute | solution.py:384
  83.8 1.7 %collective-permute-done.13.rest_3_ = bf16[384,512]{1,0:T(8,128)(2,1)} collective-permute-done((bf16[384,512]{1,0:T(8,128)(2,1)S(1)}, bf16[384,512]{1,0:T(8,128)(2,1)}, u32[]{:S(2)}, u32[]{:S(2)}) %collective-permute-start.13) | collective-permute-done | bytes 393248 | tf_op jit(solution)/shard_map/ppermute | solution.py:384
  85.5 14.3 %project_kv.1 = (bf16[8,1536,128]{2,1,0:T(8,128)(2,1)}, bf16[16,768]{1,0:T(8,128)(2,1)}, bf16[1552,1536]{1,0:T(8,128)(2,1)}) custom-call(s32[16]{0:T(128)} %fusion.38.offs_ref, bf16[384,896]{1,0:T(8,128)(2,1)} %copy-done, bf16[384,896]{1,0:T(8,128)(2,1)} %copy-done.2, bf16[384,896]{1,0:T(8,128)(2,1)} %collective-permute-done.12.rest_2_, ...), custom_call_target="tpu_custom_call" | custom-call | flops 3661627392 | bytes 12000000 | tf_op jit(solution)/shard_map/project_kv/pallas_call | solution.py:138
  100.7 11.7 %project_q.1 = (bf16[8,1536,128]{2,1,0:T(8,128)(2,1)}, bf16[16,768]{1,0:T(8,128)(2,1)}) custom-call(s32[16]{0:T(128)} %fusion.38.offs_ref, bf16[384,768]{1,0:T(8,128)(2,1)} %constant_dynamic-update-slice_fusion.rest_0_, bf16[384,768]{1,0:T(8,128)(2,1)} %collective-permute-done.7.rest_1_, bf16[384,768]{1,0:T(8,128)(2,1)} %collective-permute-done.8.rest_2_, ...), custom_call_target="tpu_custom_call" | custom-call | flops 3661627392 | bytes 12000000 | tf_op jit(solution)/shard_map/project_q/pallas_call | solution.py:138
  113.3 1.2 collective-permute-done.17.other_ref
  115.1 5.6 %decode.1 = (f32[3,8,768]{2,1,0:T(8,128)}, f32[2,8,768]{2,1,0:T(8,128)}) custom-call(s32[1]{0:T(128)} %bitcast.core_ref, s32[4]{0:T(128)} %len_ref.1, s32[1]{0:T(128)} %bitcast.1.start_ref, bf16[16,1536]{1,0:T(8,128)(2,1)} %copy-done.5, bf16[16,1536]{1,0:T(8,128)(2,1)} %copy-done.11, bf16[4,512,768]{2,1,0:T(8,128)(2,1)} %k_ref.1, bf16[4,512,768]{2,1,0:T(8,128)(2,1)} %v_ref.1), custom_call_target="tpu_custom_call" | custom-call | flops 2000000000 | bytes 6291456 | tf_op jit(solution)/shard_map/decode/pallas_call | solution.py:229
  120.9 1.3 collective-permute-done.18
  123.2 1.5 collective-permute-start.19
  124.6 10.9 %attend.3 = bf16[768,1024]{1,0:T(8,128)(2,1)} custom-call(bf16[8,1536,128]{2,1,0:T(8,128)(2,1)} %get-tuple-element.12.q_ref, bf16[8,1536,128]{2,1,0:T(8,128)(2,1)} %get-tuple-element.13.k_ref.v_ref, bf16[8,1536,128]{2,1,0:T(8,128)(2,1)} %get-tuple-element.13.k_ref.v_ref), custom_call_target="tpu_custom_call" | custom-call | flops 10000000000 | bytes 5000000 | tf_op jit(solution)/shard_map/attend/pallas_call | solution.py:272
  135.7 2.0 %collective-permute-start.20 = (f32[3,8,768]{2,1,0:T(8,128)S(1)}, f32[3,8,768]{2,1,0:T(8,128)S(1)}, u32[]{:S(2)}, u32[]{:S(2)}) collective-permute-start(f32[3,8,768]{2,1,0:T(8,128)S(1)} %pad_maximum_fusion.11), channel_id=1, source_target_pairs={{0,4},{1,5},{2,6},{3,7},{4,0},{5,1},{6,2},{7,3},{8,12},{9,13},{10,... | collective-permute-start | bytes 221192 | tf_op jit(solution)/shard_map/ppermute | solution.py:384
  137.7 11.0 %attend.2.mine_hbm = bf16[768,1024]{1,0:T(8,128)(2,1)} custom-call(bf16[8,1536,128]{2,1,0:T(8,128)(2,1)} %get-tuple-element.12.q_ref, bf16[8,1536,128]{2,1,0:T(8,128)(2,1)} %get-tuple-element.13.k_ref.v_ref, bf16[8,1536,128]{2,1,0:T(8,128)(2,1)} %get-tuple-element.13.k_ref.v_ref), custom_call_target="tpu_custom_call" | custom-call | flops 10000000000 | bytes 5000000 | tf_op jit(solution)/shard_map/attend/pallas_call | solution.py:272
  149.4 1.1 copy-done.7
  150.5 9.7 %output.1 = (bf16[768,1536]{1,0:T(8,128)(2,1)}, bf16[4,1536]{1,0:T(4,128)(2,1)}) custom-call(s32[1]{0:T(128)} %bitcast.core_ref, bf16[1536,1536]{1,0:T(8,128)(2,1)} %all-gather.2.cloned.1.call-done.wo_hbm, bf16[768,1024]{1,0:T(8,128)(2,1)} %attend.2.mine_hbm, bf16[768,1024]{1,0:T(8,128)(2,1)} %copy-done.7, f32[3,8,768]{2,1,0:T(8,128)} %pad_maximum_fusion.12.part_ref, ...), custom_call_target="tpu_custom_call" | custom-call | flops 4831838208 | bytes 12000000 | tf_op jit(solution)/shard_map/output/pallas_call | solution.py:355
  (92 shorter events, 15.2 us)
Async XLA Ops:
  7.2 142.3 %all-gather.2.cloned.1.call-start = ((), (), s32[]{:S(2)}) async-start(), calls=%async_computation | async-start | bytes 4866048 | tf_op jit(solution)/shard_map/all_gather | solution.py:419
  10.5 2.2 %collective-permute-start = (bf16[48,1664]{1,0:T(8,128)(2,1)S(1)}, bf16[48,1664]{1,0:T(8,128)(2,1)S(1)}, u32[]{:S(2)}, u32[]{:S(2)}) collective-permute-start(bf16[48,1664]{1,0:T(8,128)(2,1)S(1)} %pad_maximum_fusion.2), channel_id=1, source_target_pairs={{0,1},{1,0},{2,3},{3,2},{4,5},{5,4},{6,7},{7,6},{8,9},{9,8},{10,11... | collective-permute-start | bytes 479240 | tf_op jit(solution)/shard_map/ppermute | solution.py:384
  11.0 74.5 %collective-permute-start.15 = (bf16[768,1536]{1,0:T(8,128)(2,1)}, bf16[768,1536]{1,0:T(8,128)(2,1)}, u32[]{:S(2)}, u32[]{:S(2)}) collective-permute-start(bf16[768,1536]{1,0:T(8,128)(2,1)} %rest_5_.1), channel_id=1, source_target_pairs={{0,1},{1,0},{2,3},{3,2},{4,5},{5,4},{6,7},{7,6},{8,9},{9,8},{10,11... | collective-permute-start | bytes 7077896 | tf_op jit(solution)/shard_map/ppermute | solution.py:384
  12.7 22.9 %copy-start.12 = (s32[4]{0:T(128)S(1)}, s32[4]{0:T(128)}, u32[]{:S(2)}) copy-start(s32[4]{0:T(128)} %len_ref.1) | copy-start | bytes 52
  12.8 9.9 %collective-permute-start.1 = (bf16[96,896]{1,0:T(8,128)(2,1)S(1)}, bf16[96,896]{1,0:T(8,128)(2,1)S(1)}, u32[]{:S(2)}, u32[]{:S(2)}) collective-permute-start(bf16[96,896]{1,0:T(8,128)(2,1)S(1)} %pad_maximum_fusion.4), channel_id=1, source_target_pairs={{8,0},{16,8},{24,16},{0,24},{9,1},{17,9},{25,17},{1,25},{10,2},{18... | collective-permute-start | bytes 516104 | tf_op jit(solution)/shard_map/ppermute | solution.py:390
  17.9 17.5 %collective-permute-start.2 = (bf16[96,896]{1,0:T(8,128)(2,1)S(1)}, bf16[96,896]{1,0:T(8,128)(2,1)S(1)}, u32[]{:S(2)}, u32[]{:S(2)}) collective-permute-start(bf16[96,896]{1,0:T(8,128)(2,1)S(1)} %pad_maximum_fusion.4), channel_id=1, source_target_pairs={{16,0},{24,8},{0,16},{8,24},{17,1},{25,9},{1,17},{9,25},{18,2},{26... | collective-permute-start | bytes 516104 | tf_op jit(solution)/shard_map/ppermute | solution.py:390
  17.9 17.5 %collective-permute-start.3 = (bf16[96,896]{1,0:T(8,128)(2,1)S(1)}, bf16[96,896]{1,0:T(8,128)(2,1)S(1)}, u32[]{:S(2)}, u32[]{:S(2)}) collective-permute-start(bf16[96,896]{1,0:T(8,128)(2,1)S(1)} %pad_maximum_fusion.4), channel_id=1, source_target_pairs={{24,0},{0,8},{8,16},{16,24},{25,1},{1,9},{9,17},{17,25},{26,2},{2,... | collective-permute-start | bytes 516104 | tf_op jit(solution)/shard_map/ppermute | solution.py:390
  35.5 24.1 %copy-start = (bf16[384,896]{1,0:T(8,128)(2,1)}, bf16[384,896]{1,0:T(8,128)(2,1)S(1)}, u32[]{:S(2)}) copy-start(bf16[384,896]{1,0:T(8,128)(2,1)S(1)} %pad_maximum_fusion.1.rest_0_) | copy-start | bytes 2064388
  35.5 7.0 %collective-permute-start.4 = (bf16[96,768]{1,0:T(8,128)(2,1)S(1)}, bf16[96,768]{1,0:T(8,128)(2,1)S(1)}, u32[]{:S(2)}, u32[]{:S(2)}) collective-permute-start(bf16[96,768]{1,0:T(8,128)(2,1)S(1)} %pad_maximum_fusion.5), channel_id=1, source_target_pairs={{8,0},{16,8},{24,16},{0,24},{9,1},{17,9},{25,17},{1,25},{10,2},{18... | collective-permute-start | bytes 442376 | tf_op jit(solution)/shard_map/ppermute | solution.py:390
  35.6 21.2 %collective-permute-start.11 = (bf16[384,896]{1,0:T(8,128)(2,1)S(1)}, bf16[384,896]{1,0:T(8,128)(2,1)S(1)}, u32[]{:S(2)}, u32[]{:S(2)}) collective-permute-start(bf16[384,896]{1,0:T(8,128)(2,1)S(1)} %pad_maximum_fusion.1.rest_0_), channel_id=1, source_target_pairs={{0,2},{1,3},{2,0},{3,1},{4,6},{5,7},{6,4},{7,5},{8,10},{9,11},{10,... | collective-permute-start | bytes 2064392 | tf_op jit(solution)/shard_map/ppermute | solution.py:384
  37.1 21.4 %collective-permute-start.12 = (bf16[384,896]{1,0:T(8,128)(2,1)S(1)}, bf16[384,896]{1,0:T(8,128)(2,1)}, u32[]{:S(2)}, u32[]{:S(2)}) collective-permute-start(bf16[384,896]{1,0:T(8,128)(2,1)S(1)} %pad_maximum_fusion.1.rest_0_), channel_id=1, source_target_pairs={{0,4},{1,5},{2,6},{3,7},{4,0},{5,1},{6,2},{7,3},{8,12},{9,13},{10,... | collective-permute-start | bytes 2064392 | tf_op jit(solution)/shard_map/ppermute | solution.py:384
  38.7 12.7 %collective-permute-start.5 = (bf16[96,768]{1,0:T(8,128)(2,1)S(1)}, bf16[96,768]{1,0:T(8,128)(2,1)S(1)}, u32[]{:S(2)}, u32[]{:S(2)}) collective-permute-start(bf16[96,768]{1,0:T(8,128)(2,1)S(1)} %pad_maximum_fusion.5), channel_id=1, source_target_pairs={{16,0},{24,8},{0,16},{8,24},{17,1},{25,9},{1,17},{9,25},{18,2},{26... | collective-permute-start | bytes 442376 | tf_op jit(solution)/shard_map/ppermute | solution.py:390
  42.5 20.2 %copy-start.6 = (bf16[4,1536]{1,0:T(4,128)(2,1)S(1)}, bf16[4,1536]{1,0:T(4,128)(2,1)}, u32[]{:S(2)}) copy-start(bf16[4,1536]{1,0:T(4,128)(2,1)} %param.9) | copy-start | bytes 36868
  42.5 9.6 %collective-permute-start.6 = (bf16[96,768]{1,0:T(8,128)(2,1)S(1)}, bf16[96,768]{1,0:T(8,128)(2,1)S(1)}, u32[]{:S(2)}, u32[]{:S(2)}) collective-permute-start(bf16[96,768]{1,0:T(8,128)(2,1)S(1)} %pad_maximum_fusion.5), channel_id=1, source_target_pairs={{24,0},{0,8},{8,16},{16,24},{25,1},{1,9},{9,17},{17,25},{26,2},{2,... | collective-permute-start | bytes 442376 | tf_op jit(solution)/shard_map/ppermute | solution.py:390
  45.1 18.2 %copy-start.3 = (f32[3,16,384]{2,1,0:T(8,128)S(1)}, f32[3,16,384]{2,1,0:T(8,128)}, u32[]{:S(2)}) copy-start(f32[3,16,384]{2,1,0:T(8,128)} %constant.110.clone.1) | copy-start | bytes 221188
  52.7 17.2 %collective-permute-start.8 = (bf16[384,768]{1,0:T(8,128)(2,1)}, bf16[384,768]{1,0:T(8,128)(2,1)}, u32[]{:S(2)}, u32[]{:S(2)}) collective-permute-start(bf16[384,768]{1,0:T(8,128)(2,1)} %constant_dynamic-update-slice_fusion.rest_0_), channel_id=1, source_target_pairs={{0,4},{1,5},{2,6},{3,7},{4,0},{5,1},{6,2},{7,3},{8,12},{9,13},{10,... | collective-permute-start | bytes 1769480 | tf_op jit(solution)/shard_map/ppermute | solution.py:384
  55.1 17.7 %collective-permute-start.7 = (bf16[384,768]{1,0:T(8,128)(2,1)}, bf16[384,768]{1,0:T(8,128)(2,1)}, u32[]{:S(2)}, u32[]{:S(2)}) collective-permute-start(bf16[384,768]{1,0:T(8,128)(2,1)} %constant_dynamic-update-slice_fusion.rest_0_), channel_id=1, source_target_pairs={{0,2},{1,3},{2,0},{3,1},{4,6},{5,7},{6,4},{7,5},{8,10},{9,11},{10,... | collective-permute-start | bytes 1769480 | tf_op jit(solution)/shard_map/ppermute | solution.py:384
  56.8 8.2 %copy-start.2 = (bf16[384,896]{1,0:T(8,128)(2,1)}, bf16[384,896]{1,0:T(8,128)(2,1)S(1)}, u32[]{:S(2)}) copy-start(bf16[384,896]{1,0:T(8,128)(2,1)S(1)} %collective-permute-done.11.rest_1_) | copy-start | bytes 2064388
  56.8 28.7 %collective-permute-start.13 = (bf16[384,512]{1,0:T(8,128)(2,1)S(1)}, bf16[384,512]{1,0:T(8,128)(2,1)}, u32[]{:S(2)}, u32[]{:S(2)}) collective-permute-start(bf16[384,512]{1,0:T(8,128)(2,1)S(1)} %slice.132), channel_id=1, source_target_pairs={{0,4},{1,5},{2,6},{3,7},{4,0},{5,1},{6,2},{7,3},{8,12},{9,13},{10,... | collective-permute-start | bytes 1179656 | tf_op jit(solution)/shard_map/ppermute | solution.py:384
  58.5 6.5 %copy-start.1 = (f32[3,16,768]{2,1,0:T(8,128)}, f32[3,16,768]{2,1,0:T(8,128)S(1)}, u32[]{:S(2)}) copy-start(f32[3,16,768]{2,1,0:T(8,128)S(1)} %pad_maximum_fusion.8.rest_7_) | copy-start | bytes 442372
  59.6 24.2 %collective-permute-start.14 = (bf16[384,384]{1,0:T(8,128)(2,1)S(1)}, bf16[384,384]{1,0:T(8,128)(2,1)S(1)}, u32[]{:S(2)}, u32[]{:S(2)}) collective-permute-start(bf16[384,384]{1,0:T(8,128)(2,1)S(1)} %slice.133), channel_id=1, source_target_pairs={{0,2},{1,3},{2,0},{3,1},{4,6},{5,7},{6,4},{7,5},{8,10},{9,11},{10,... | collective-permute-start | bytes 884744 | tf_op jit(solution)/shard_map/ppermute | solution.py:384
  70.9 28.9 %collective-permute-start.10 = (bf16[384,384]{1,0:T(8,128)(2,1)S(1)}, bf16[384,384]{1,0:T(8,128)(2,1)S(1)}, u32[]{:S(2)}, u32[]{:S(2)}) collective-permute-start(bf16[384,384]{1,0:T(8,128)(2,1)S(1)} %slice.131), channel_id=1, source_target_pairs={{0,2},{1,3},{2,0},{3,1},{4,6},{5,7},{6,4},{7,5},{8,10},{9,11},{10,... | collective-permute-start | bytes 884744 | tf_op jit(solution)/shard_map/ppermute | solution.py:384
  73.8 26.1 %collective-permute-start.9 = (bf16[384,384]{1,0:T(8,128)(2,1)S(1)}, bf16[384,384]{1,0:T(8,128)(2,1)S(1)}, u32[]{:S(2)}, u32[]{:S(2)}) collective-permute-start(bf16[384,384]{1,0:T(8,128)(2,1)S(1)} %slice.130), channel_id=1, source_target_pairs={{0,4},{1,5},{2,6},{3,7},{4,0},{5,1},{6,2},{7,3},{8,12},{9,13},{10,... | collective-permute-start | bytes 884744 | tf_op jit(solution)/shard_map/ppermute | solution.py:384
  83.8 1.8 %copy-start.8 = (bf16[384,384]{1,0:T(8,128)(2,1)}, bf16[384,384]{1,0:T(8,128)(2,1)S(1)}, u32[]{:S(2)}) copy-start(bf16[384,384]{1,0:T(8,128)(2,1)S(1)} %collective-permute-done.14.rest_4_) | copy-start | bytes 884740
  100.7 12.5 %copy-start.4 = (bf16[16,768]{1,0:T(8,128)(2,1)S(1)}, bf16[16,768]{1,0:T(8,128)(2,1)}, u32[]{:S(2)}) copy-start(bf16[16,768]{1,0:T(8,128)(2,1)} %get-tuple-element.15) | copy-start | bytes 73732
  113.2 1.3 copy-start.5
  113.2 1.3 collective-permute-start.17
  120.7 1.5 collective-permute-start.18
  123.2 12.4 %collective-permute-start.19 = (f32[3,8,768]{2,1,0:T(8,128)S(1)}, f32[3,8,768]{2,1,0:T(8,128)S(1)}, u32[]{:S(2)}, u32[]{:S(2)}) collective-permute-start(f32[3,8,768]{2,1,0:T(8,128)S(1)} %pad_maximum_fusion.10), channel_id=1, source_target_pairs={{0,2},{1,3},{2,0},{3,1},{4,6},{5,7},{6,4},{7,5},{8,10},{9,11},{10,... | collective-permute-start | bytes 221192 | tf_op jit(solution)/shard_map/ppermute | solution.py:384
  135.6 13.8 %collective-permute-start.16 = (bf16[768,1024]{1,0:T(8,128)(2,1)}, bf16[768,1024]{1,0:T(8,128)(2,1)S(1)}, u32[]{:S(2)}, u32[]{:S(2)}) collective-permute-start(bf16[768,1024]{1,0:T(8,128)(2,1)} %attend.3), channel_id=1, source_target_pairs={{0,1},{1,0},{2,3},{3,2},{4,5},{5,4},{6,7},{7,6},{8,9},{9,8},{10,11... | collective-permute-start | bytes 4718600 | tf_op jit(solution)/shard_map/ppermute | solution.py:384
  135.7 13.0 %collective-permute-start.20 = (f32[3,8,768]{2,1,0:T(8,128)S(1)}, f32[3,8,768]{2,1,0:T(8,128)S(1)}, u32[]{:S(2)}, u32[]{:S(2)}) collective-permute-start(f32[3,8,768]{2,1,0:T(8,128)S(1)} %pad_maximum_fusion.11), channel_id=1, source_target_pairs={{0,4},{1,5},{2,6},{3,7},{4,0},{5,1},{6,2},{7,3},{8,12},{9,13},{10,... | collective-permute-start | bytes 221192 | tf_op jit(solution)/shard_map/ppermute | solution.py:384
  149.4 1.1 copy-start.7
  (3 other events, 2.2 us)
Sparse Core Ops, SparseCore 0:
  10.9 87.1 all-gather.1

commit v2 on v0

v2 whole, which is shorter than its diff:
```python
import functools

import jax
import jax.numpy as jnp
from jax import lax
from jax.experimental import pallas as pl
from jax.experimental.pallas import tpu as pltpu
from jax.sharding import PartitionSpec as P

H = 16
KV = 8
HD = 96
HALF = HD // 2
LANES = 128
PAD = H * LANES

THETA = 100000.0
EPS = 1e-05
NEGATIVE = -1e30
SCALE = HD ** (-0.5)
LOG2E = 1.4426950408889634

BF16 = jnp.bfloat16
F32 = jnp.float32
VMEM_BYTES = 56 * 1024 * 1024


def cost(microseconds):
    return pl.CostEstimate(flops=int(microseconds * 1.1e9), bytes_accessed=100_000, transcendentals=0)


def rope_tables(positions, width):
    lane = jnp.arange(width, dtype=jnp.int32)
    lane = lane % HD if width % HD == 0 else lane
    frequency = jnp.power(THETA, -(lane % HALF).astype(F32) * (2.0 / HD))
    angles = positions.astype(F32)[:, None] * frequency[None, :]
    cosine, sine = jnp.cos(angles), jnp.sin(angles)
    lane = lane[None, :]
    return jnp.stack(
        [
            jnp.where(lane < HD, cosine, 0.0),
            jnp.where((lane >= HALF) & (lane < HD), sine, 0.0),
            jnp.where(lane < HALF, -sine, 0.0),
        ]
    )


def normalize(rows, gain):
    widened = rows.astype(F32)
    factor = lax.rsqrt(jnp.mean(widened * widened, axis=-1, keepdims=True) + EPS)
    return (widened * factor * gain).astype(BF16)


def head_tile(u_ref, rows, index):
    base, place = (index // 4) * 3 * LANES, index % 4
    lane = lax.broadcasted_iota(jnp.int32, (rows.stop - rows.start, LANES), 1)

    def tile(t):
        return u_ref[rows, base + t * LANES : base + (t + 1) * LANES]

    if place == 0:
        return tile(0)
    if place == 1:
        return pltpu.roll(jnp.where(lane >= 96, tile(0), tile(1)), 32, 1)
    if place == 2:
        return pltpu.roll(jnp.where(lane >= 64, tile(1), tile(2)), 64, 1)
    return pltpu.roll(tile(2), 96, 1)


def fetch(sources, refs, offs_ref, block_rows, columns, target, sem):
    for ref, column, first, blocks in sources:
        for b in range(blocks):
            to = pl.ds(pl.multiple_of(offs_ref[first + b], 16), block_rows)
            source = refs[ref].at[pl.ds(b * block_rows, block_rows), pl.ds(column, columns)]
            pltpu.make_async_copy(source, target(to), sem).start()


def fetch_weights(plan, refs, offs_ref, block_rows, w_ref, sem):
    half = w_ref.shape[1] // len(plan)
    for t, sources in enumerate(plan):
        fetch(sources, refs, offs_ref, block_rows, half, lambda rows: w_ref.at[rows, pl.ds(t * half, half)], sem)


def multiply(x, w_ref, u_ref, rows):
    for n in range(w_ref.shape[1] // 256):
        cols = slice(n * 256, (n + 1) * 256)
        u_ref[:rows, cols] = jnp.dot(x, w_ref[:, cols], preferred_element_type=F32)


def store_heads(u_ref, table_ref, heads_ref, first):
    rows = table_ref.shape[1]
    lane = lax.broadcasted_iota(jnp.int32, (rows, LANES), 1)
    for h in range(8):
        u = head_tile(u_ref, slice(0, rows), h)
        if h in (2, 3):
            u = jnp.where(lane < HD, u, 1.0)
        else:
            u = (
                u * table_ref[0]
                + pltpu.roll(u, HALF, 1) * table_ref[1]
                + pltpu.roll(u, LANES - HALF, 1) * table_ref[2]
            )
        heads_ref[h, first : first + rows, :] = u.astype(BF16)


def turn_decode(u, dtable_ref):
    return (
        u * dtable_ref[0]
        + pltpu.roll(u, HALF, 1) * dtable_ref[1]
        + pltpu.roll(u, u.shape[1] - HALF, 1) * dtable_ref[2]
    ).astype(BF16)


def attend(heads_ref, o_ref, block):
    stretch = o_ref.shape[0]
    causal = lax.broadcasted_iota(jnp.int32, (block, block), 1) <= lax.broadcasted_iota(
        jnp.int32, (block, block), 0
    )
    causal = jnp.concatenate([causal, causal], axis=0)
    for j in range(2):
        for i in range(stretch // block):
            rows = slice(i * block, (i + 1) * block)
            seen = (i + 1) * block
            both = heads_ref[4 + 2 * j : 6 + 2 * j, rows, :].reshape(2 * block, LANES)
            scores = lax.dot_general(
                both, heads_ref[j, :seen, :], (((1,), (1,)), ((), ())), preferred_element_type=F32
            )
            last = jnp.where(causal, scores[:, i * block :], NEGATIVE)
            scores = last if i == 0 else jnp.concatenate([scores[:, : i * block], last], axis=1)
            peak = jnp.max(scores, axis=-1, keepdims=True)
            weights = jnp.exp2((scores - peak) * (SCALE * LOG2E)).astype(BF16)
            mixed = jnp.dot(weights, heads_ref[2 + j, :seen, :], preferred_element_type=F32)
            mixed = (mixed / mixed[:, HD : HD + 1]).astype(BF16)
            for parity in range(2):
                lanes = slice((2 * j + parity) * LANES, (2 * j + parity + 1) * LANES)
                o_ref[rows, lanes] = mixed[parity * block : (parity + 1) * block]


def decode(turned, requests, offset, k_ref, v_ref, len_ref, start_ref, part_ref):
    turned = turned.astype(F32)
    extra = turned.shape[0]
    window, span = k_ref.shape[3], k_ref.shape[2]
    two = 2 * HD

    def widen(values):
        sides = [jnp.zeros((extra, offset), F32)] if offset else []
        sides += [values]
        sides += [jnp.zeros((extra, window - two - offset), F32)] if window - two - offset else []
        return jnp.concatenate(sides, axis=1)

    own_k, own_v = widen(turned[:, :two]), widen(turned[:, two : 2 * two])
    queries = []
    for parity in range(2):
        at = 2 * two + parity * HD
        queries.append(
            widen(jnp.concatenate([turned[:, at : at + HD], turned[:, at + two : at + two + HD]], axis=1))
        )

    def here(i, rows):
        lane = lax.broadcasted_iota(jnp.int32, (rows, window), 1)
        return (lane >= offset + i * HD) & (lane < offset + (i + 1) * HD)

    for parity in range(2):
        product = queries[parity] * own_k
        own = jnp.zeros((extra, window), F32)
        for i in range(2):
            mask = here(i, extra)
            own = own + jnp.where(mask, jnp.sum(jnp.where(mask, product, 0.0), axis=-1, keepdims=True), 0.0)
        rows = slice(parity * requests, (parity + 1) * requests)
        part_ref[2, 0, rows, :] = own_v[:requests]
        part_ref[2, 1, rows, :] = own[:requests] * SCALE
        part_ref[2, 2, rows, :] = jnp.ones((requests, window), F32)

    for r in range(requests):
        query = [
            jnp.where(here(i, 1), queries[parity][r : r + 1], 0.0) for parity in range(2) for i in range(2)
        ]
        query = jnp.concatenate(query + [jnp.zeros((4, window), F32)], axis=0).astype(BF16)
        for b in range(2):
            scores = (
                lax.dot_general(query, k_ref[b, r], (((1,), (1,)), ((), ())), preferred_element_type=F32)
                * SCALE
            )
            live = lax.broadcasted_iota(jnp.int32, scores.shape, 1) + start_ref[b] < len_ref[r]
            scores = jnp.where(live, scores, NEGATIVE)
            peak = jnp.max(scores, axis=-1, keepdims=True)
            expanded = jnp.where(live, jnp.exp(scores - peak), 0.0)
            total = jnp.sum(expanded, axis=-1, keepdims=True)
            sums = jnp.dot(expanded.astype(BF16), v_ref[b, r], preferred_element_type=F32)
            for slot, values in enumerate((sums, peak, total)):
                for parity in range(2):
                    row = parity * requests + r
                    part_ref[b, slot, row : row + 1, :] = sum(
                        jnp.where(here(i, 1), values[2 * parity + i : 2 * parity + i + 1], 0.0) for i in range(2)
                    )


def group_kernel(block_rows, plan, norm, offset, stretches, *refs):
    refs = list(refs)

    def take(count=1):
        taken, refs[:count] = refs[:count], []
        return taken

    with_decode = offset is not None
    (offs_ref,) = take()
    if with_decode:
        lane_ref, len_ref, start_ref = take(3)
    w_refs = take(1 + max(source[0] for sources in plan for source in sources))
    x_hbm = take(stretches)
    (table_ref,) = take()
    if with_decode:
        dx_ref, dtable_ref = take(2)
        caches = take(4)
    o_refs = take(stretches)
    if with_decode:
        (part_ref,) = take()
    if norm:
        xn_hbm = take(stretches)
        (dxn_ref,) = take()
    x_refs, u_refs, heads_refs = take(stretches), take(stretches), take(stretches)
    (w_ref,) = take()
    if with_decode:
        k_ref, v_ref = take(2)
    if norm:
        (gain_ref,) = take()
    (sem,) = take()
    stretch = table_ref.shape[1]
    main = pl.ds(0, stretch)

    if norm:
        fetch(plan[2], w_refs, offs_ref, block_rows, LANES, lambda rows: gain_ref.at[rows], sem.at[1])
    loads = [pltpu.make_async_copy(x_hbm[n], x_refs[n].at[main], sem.at[2 + n]) for n in range(stretches)]
    loads[0].start()
    fetch_weights(plan[:2], w_refs, offs_ref, block_rows, w_ref, sem.at[0])
    for load in loads[1:]:
        load.start()
    if with_decode:
        window = k_ref.shape[3]
        for n, source in enumerate(caches):
            lane = pl.multiple_of(lane_ref[0], LANES) if n < 2 else 0 if offset == 0 else LANES
            pltpu.make_async_copy(
                source.at[:, :, pl.ds(lane, window)], (k_ref, v_ref)[n % 2].at[n // 2], sem.at[4 + n]
            ).start()
    if norm:
        pltpu.make_async_copy(gain_ref, gain_ref, sem.at[1]).wait()
        pick = (lax.broadcasted_iota(jnp.int32, (8, LANES), 1) == 0).astype(BF16)
        gain = lax.dot_general(pick, gain_ref[...], (((1,), (1,)), ((), ())), preferred_element_type=F32)[0:1]
        dxn_ref[...] = normalize(dx_ref[...], gain)
    saves = []
    for n in range(stretches):
        loads[n].wait()
        if norm:
            def body(i, _):
                rows = pl.ds(pl.multiple_of(i * 64, 64), 64)
                x_refs[n][rows, :] = normalize(x_refs[n][rows, :], gain)
                return 0

            lax.fori_loop(0, stretch // 64, body, 0)
            saves.append(pltpu.make_async_copy(x_refs[n].at[main], xn_hbm[n], sem.at[8 + n]))
            saves[-1].start()
        if n == 0:
            pltpu.make_async_copy(w_ref, w_ref, sem.at[0]).wait()
            if with_decode:
                x_refs[0][stretch:, :] = dxn_ref[...] if norm else dx_ref[...]
        multiply(x_refs[n][...], w_ref, u_refs[n], x_refs[n].shape[0])
        store_heads(u_refs[n], table_ref, heads_refs[n], 0)
        if n == 0 and with_decode:
            turned = turn_decode(u_refs[0][stretch:, :], dtable_ref)
            for m, source in enumerate(caches):
                target = (k_ref, v_ref)[m % 2].at[m // 2]
                pltpu.make_async_copy(target, target, sem.at[4 + m]).wait()
            decode(turned, k_ref.shape[1], offset, k_ref, v_ref, len_ref, start_ref, part_ref)
        attend(heads_refs[n], o_refs[n], 256)
    for save in saves:
        save.wait()


def run_group(rows, tables, offs, w_pieces, block_rows, plan, norm=False, decoding=None):
    stretch, depth = rows[0].shape
    stretches = len(rows)
    width = KV * HD
    smem = pl.BlockSpec(memory_space=pltpu.SMEM)
    vmem = pl.BlockSpec(memory_space=pltpu.VMEM)
    hbm = pl.BlockSpec(memory_space=pl.ANY)
    operands, in_specs, offset, extra = [offs], [smem], None, 0
    if decoding:
        offset, lane, cache_len, starts, dx, dtable, caches = decoding
        requests, span = caches[0].shape[:2]
        extra, window = dx.shape[0], 2 * LANES
        operands += [lane, cache_len, starts]
        in_specs += [smem] * 3
    operands += [*w_pieces, *rows, tables]
    in_specs += [hbm] * (len(w_pieces) + stretches) + [vmem]
    out_shape = [jax.ShapeDtypeStruct((stretch, 4 * LANES), BF16)] * stretches
    out_specs = [vmem] * stretches
    if decoding:
        operands += [dx, dtable, *caches]
        in_specs += [vmem] * 2 + [hbm] * 4
        out_shape.append(jax.ShapeDtypeStruct((3, 3, 2 * requests, window), F32))
        out_specs.append(vmem)
    if norm:
        out_shape += [jax.ShapeDtypeStruct((stretch, depth), BF16)] * stretches
        out_shape.append(jax.ShapeDtypeStruct((extra, depth), BF16))
        out_specs += [hbm] * stretches + [vmem]
    rows_all = [stretch + (extra if n == 0 else 0) for n in range(stretches)]
    scratch = [pltpu.VMEM((count, depth), BF16) for count in rows_all]
    scratch += [pltpu.VMEM((count, width), F32) for count in rows_all]
    scratch += [pltpu.VMEM((8, stretch, LANES), BF16)] * stretches
    scratch.append(pltpu.VMEM((depth, width), BF16))
    if decoding:
        scratch += [pltpu.VMEM((2, requests, span, window), BF16)] * 2
    if norm:
        scratch.append(pltpu.VMEM((depth, LANES), BF16))
    scratch.append(pltpu.SemaphoreType.DMA((10,)))
    return pl.pallas_call(
        functools.partial(group_kernel, block_rows, plan, norm, offset, stretches),
        in_specs=in_specs,
        out_specs=out_specs,
        out_shape=out_shape,
        scratch_shapes=scratch,
        compiler_params=pltpu.CompilerParams(vmem_limit_bytes=VMEM_BYTES),
        cost_estimate=cost(10 * stretches),
        name="group",
    )(*operands)


def output_kernel(requests, block_rows, plan, o_plan, core_ref, offs_ref, *rest):
    count = 1 + max(source[0] for sources in plan for source in sources)
    wo_refs = rest[:count]
    o_refs, rest = rest[count : count + len(o_plan)], rest[count + len(o_plan) :]
    parts_ref, other_ref, out_ref, dec_ref, wo_ref, att_ref, w_sem, o_sem = rest
    step = pl.program_id(0)
    stretch = out_ref.shape[0]
    columns = out_ref.shape[1]
    steps = wo_ref.shape[0]
    half = PAD // 2

    @pl.when(step == 0)
    def _():
        me, core = core_ref[0], core_ref[1]
        o_copies = [
            pltpu.make_async_copy(
                source,
                att_ref.at[core if mine else 1 - core, pl.ds(0, stretch), pl.ds(lane, source.shape[1])],
                o_sem.at[n],
            )
            for n, (source, (mine, lane)) in enumerate(zip(o_refs, o_plan))
        ]
        for copy in o_copies:
            copy.start()
        for t, sources in enumerate(plan):
            for ref, column, first, blocks in sources:
                for b in range(blocks):
                    to = pl.multiple_of(offs_ref[first + b], 16)
                    pltpu.make_async_copy(
                        wo_refs[ref].at[pl.ds(b * block_rows, block_rows), pl.ds(column, columns)],
                        wo_ref.at[t, pl.ds(to, block_rows)],
                        w_sem.at[t],
                    ).start()
        for t in range(steps):
            for h in range(H):
                wo_ref[t, h * LANES + HD : (h + 1) * LANES, :] = jnp.zeros((LANES - HD, columns), BF16)
        extra = att_ref.shape[1] - stretch
        att_ref[:, stretch:, :] = jnp.zeros((2, extra, half), BF16)
        chips = parts_ref.shape[0]
        for parts, place in ((parts_ref, core), (other_ref, 1 - core)):
            blocks = [(jnp.bitwise_xor(me // 2, chip), b) for chip in range(chips) for b in range(2)] + [(0, 2)]
            top = parts[0, 2, 1]
            for slot, b in blocks:
                top = jnp.maximum(top, parts[slot, b, 1])
            numerator, denominator = jnp.zeros_like(top), jnp.zeros_like(top)
            for slot, b in blocks:
                rescale = jnp.exp(parts[slot, b, 1] - top)
                numerator = numerator + rescale * parts[slot, b, 0]
                denominator = denominator + rescale * parts[slot, b, 2]
            mix = numerator / jnp.where(denominator > 0.0, denominator, 1.0)
            window = mix.shape[1] // 2
            for parity in range(2):
                rows = mix[parity * requests : (parity + 1) * requests]
                rows = jnp.concatenate([rows, jnp.zeros((extra - requests, mix.shape[1]), F32)], axis=0)
                for g in range(2):
                    for i in range(2):
                        at = g * window + g * (window - 2 * HD) + i * HD
                        to = (4 * g + 2 * i + parity) * LANES
                        att_ref[place, stretch:, to : to + HD] = rows[:, at : at + HD].astype(BF16)
        for copy in o_copies:
            copy.wait()

    for t in range(steps):
        @pl.when(step == t)
        def _():
            whole = wo_ref.at[t, pl.ds(0, H * HD)]
            pltpu.make_async_copy(whole, whole, w_sem.at[t]).wait()

    projected = jnp.dot(att_ref[0], wo_ref[step, :half], preferred_element_type=F32) + jnp.dot(
        att_ref[1], wo_ref[step, half:], preferred_element_type=F32
    )
    out_ref[...] = projected[:stretch].astype(BF16)
    dec_ref[...] = projected[stretch : stretch + requests].astype(BF16)


def output(attended, parts, other_parts, core, offs, wo_pieces, block_rows, plan, requests):
    stretch = attended[0][0].shape[0]
    width = H * HD
    steps, extra = 2, 16
    smem = pl.BlockSpec(memory_space=pltpu.SMEM)
    vmem = pl.BlockSpec(memory_space=pltpu.VMEM)
    hbm = pl.BlockSpec(memory_space=pl.ANY)
    return pl.pallas_call(
        functools.partial(output_kernel, requests, block_rows, plan, [piece[1:] for piece in attended]),
        grid=(steps,),
        in_specs=[smem] * 2 + [hbm] * (len(wo_pieces) + len(attended)) + [vmem] * 2,
        out_specs=[
            pl.BlockSpec((stretch, width // steps), lambda t: (0, t)),
            pl.BlockSpec((requests, width // steps), lambda t: (0, t)),
        ],
        out_shape=[
            jax.ShapeDtypeStruct((stretch, width), BF16),
            jax.ShapeDtypeStruct((requests, width), BF16),
        ],
        scratch_shapes=[
            pltpu.VMEM((steps, PAD, width // steps), BF16),
            pltpu.VMEM((2, stretch + extra, PAD // 2), BF16),
            pltpu.SemaphoreType.DMA((steps,)),
            pltpu.SemaphoreType.DMA((len(attended),)),
        ],
        compiler_params=pltpu.CompilerParams(
            dimension_semantics=("arbitrary",), vmem_limit_bytes=VMEM_BYTES
        ),
        cost_estimate=cost(9),
        name="output",
    )(core, offs, *wo_pieces, *[piece[0] for piece in attended], parts, other_parts)


def swap(array, mask, n_shard):
    return lax.ppermute(array, "shard", [(i, i ^ mask) for i in range(n_shard)])


def after(array, *others):
    return lax.optimization_barrier((array, *others))[0]


def along_dp(local, n_dp):
    found = [local]
    for shift in range(1, n_dp):
        found.append(lax.ppermute(local, "dp", [((i + shift) % n_dp, i) for i in range(n_dp)]))
    return jnp.concatenate(found, axis=0)


def pieces_of(here, beside, above, cut, n_shard):
    whole = here.shape[1]
    left, right = swap(beside[:, :cut], 4, n_shard), swap(above[:, cut:], 2, n_shard)
    return [(here, 0, 0, whole), (beside, 1, 0, whole), (above, 2, 0, whole), (left, 3, 0, cut), (right, 3, cut, whole)]


def lay_out(pieces, starts, n_dp, first=0):
    plan = [[] for _ in starts]
    for index, (_, mask, left, right) in enumerate(pieces):
        for column, t in starts.items():
            if left <= column < right:
                plan[t].append((index, column - left, mask * n_dp, n_dp))
    return plan


def group_columns(wqkv, core, width):
    quarter = width // 4
    found = []
    for g in range(2):
        at = (2 * core + g) * quarter
        found += [
            wqkv[:, 2 * width + at : 2 * width + at + quarter],
            wqkv[:, 3 * width + at : 3 * width + at + quarter],
            wqkv[:, 2 * at : 2 * at + 2 * quarter],
        ]
    return jnp.concatenate(found, axis=1)


def per_device(n_dp, n_shard, prefill_x, decode_x, norm_gain, wqkv, wo, k_cache, v_cache, cache_len):
    stretch = prefill_x.shape[0]
    requests, span, width = k_cache.shape
    half = width // 2
    me, me_dp = lax.axis_index("shard"), lax.axis_index("dp")
    core = me % 2
    everyone = ("dp", "shard")
    block_rows = wqkv.shape[0]
    low, high = group_columns(wqkv, 0, width), group_columns(wqkv, 1, width)
    gain_columns = jnp.broadcast_to(norm_gain[:, None], (block_rows, LANES))
    head = LANES + width
    split = n_shard == 8 and block_rows == HALF

    wo_all = lax.all_gather(wo, everyone, axis=0, tiled=True)
    wo_plan = [[(0, 0, 0, H)], [(0, width, 0, H)]]
    wo_offs = jnp.arange(H, dtype=jnp.int32) * LANES
    sib_x = swap(prefill_x, 1, n_shard)
    sib_caches = [
        swap(jnp.where(core == 0, cache[:, :, half:], cache[:, :, :half]), 1, n_shard) for cache in (k_cache, v_cache)
    ]
    extra = 16
    dx = jnp.pad(decode_x, ((0, extra - requests), (0, 0)))
    decode_positions = jnp.concatenate([cache_len, jnp.zeros((extra - requests,), jnp.int32)])
    tables = rope_tables(jnp.arange(stretch, dtype=jnp.int32), LANES)
    turning = rope_tables(decode_positions, half)
    quarter = half // 2
    plain = jnp.stack([jnp.ones((extra, quarter), F32)] + [jnp.zeros((extra, quarter), F32)] * 2)
    dtable = jnp.concatenate([turning[:, :, :quarter], plain, turning], axis=2)
    if split:
        first = core == 0
        mine = jnp.concatenate([gain_columns, jnp.where(first, low, high)], axis=1)
        theirs = jnp.concatenate([gain_columns, jnp.where(first, high, low)], axis=1)
        theirs = swap(theirs, 1, n_shard)
        pair = jnp.concatenate([jnp.where(first, mine, theirs), jnp.where(first, theirs, mine)], axis=0)
        order = jnp.arange(n_shard // 2 * n_dp, dtype=jnp.int32)
        chip = (me_dp + order % n_dp) % n_dp * (n_shard // 2) + (me // 2 ^ (order // n_dp))
        block_rows = 2 * block_rows
        offs = chip * block_rows
        here = along_dp(pair[:, :head], n_dp)
        beside, above = swap(here, 2, n_shard), swap(here, 4, n_shard)
        later_here = along_dp(after(pair[:, head:], beside, above), n_dp)
        pieces = pieces_of(here, beside, above, LANES + half, n_shard)
        plan = lay_out(pieces, {LANES: 0, LANES + half: 1, 0: 2}, n_dp)
        pieces = [piece[0] for piece in pieces]
        later_here = after(later_here, *pieces)
        beside, above = swap(later_here, 2, n_shard), swap(later_here, 4, n_shard)
    else:
        offs = jnp.zeros((1,), jnp.int32)
        every = lax.all_gather(jnp.concatenate([gain_columns, low, high], axis=1), everyone, axis=0, tiled=True)
        block_rows = every.shape[0]
        chosen = jnp.where(core == 0, every[:, LANES : LANES + 2 * width], every[:, LANES + 2 * width :])
        pieces = [jnp.concatenate([every[:, :LANES], chosen[:, :width]], axis=1)]
        plan = [[(0, LANES, 0, 1)], [(0, LANES + half, 0, 1)], [(0, 0, 0, 1)]]

    lane = core.astype(jnp.int32).reshape(1) * half
    starts = jnp.stack([me * span, (me ^ 1) * span]).astype(jnp.int32)
    caches = [k_cache, v_cache, *sib_caches]
    own_o, sib_o, part, xn, sib_xn, dxn = run_group(
        [prefill_x, sib_x], tables, offs, pieces, block_rows, plan, norm=True,
        decoding=(0, lane, cache_len, starts, dx, dtable, caches),
    )
    mine, theirs = [own_o], [sib_o]
    if split:
        pieces = pieces_of(later_here, after(beside, sib_o), after(above, sib_o), half, n_shard)
        plan = lay_out(pieces, {0: 0, half: 1}, n_dp)
        pieces = [piece[0] for piece in pieces]
    else:
        pieces = [chosen[:, width:]]
        plan = [[(0, 0, 0, 1)], [(0, half, 0, 1)]]
    sib_o, later_part = run_group(
        [sib_xn], tables, offs, pieces, block_rows, plan,
        decoding=(LANES // 2, lane + LANES, cache_len, starts, dxn, dtable, caches),
    )
    theirs.append(sib_o)
    part = jnp.concatenate([part, later_part], axis=-1)
    parts = jnp.stack([part] + [swap(part, 2 * chip, n_shard) for chip in range(1, n_shard // 2)])
    mine += run_group([after(xn, sib_o)], tables, offs, pieces, block_rows, plan)
    other_parts = swap(after(parts, mine[1]), 1, n_shard)
    group_lanes = PAD // 4
    attended = [(piece, True, g * group_lanes) for g, piece in enumerate(mine)]
    attended += [(swap(piece, 1, n_shard), False, g * group_lanes) for g, piece in enumerate(theirs)]
    me_and_core = jnp.stack([me, core]).astype(jnp.int32)
    return output(attended, parts, other_parts, me_and_core, wo_offs, [wo_all], HD, wo_plan, requests)


def solution(mesh):
    in_specs = (
        P(("dp", "shard"), None),
        P("dp", None),
        P(("dp", "shard")),
        P(("dp", "shard"), None),
        P(("dp", "shard"), None),
        P("dp", "shard", None),
        P("dp", "shard", None),
        P("dp"),
    )
    out_specs = (P(("dp", "shard"), None), P("dp", None))
    return jax.shard_map(
        functools.partial(per_device, mesh.shape["dp"], mesh.shape["shard"]),
        mesh=mesh, in_specs=in_specs, out_specs=out_specs, check_vma=False,
    )
```

time: 274 us -> 180 us (0.66)
  matrix products: 93.2 us -> 0 us
  blocking collectives: 90.2 us -> 0 us
  Pallas kernels: 0 us -> 57.1 us
  starting transfers between devices: 0.08 us -> 33 us
  waiting for transfers between devices: 34.3 us -> 55.9 us
  local copies, waits for them, and re-layouts: 27.7 us -> 7.98 us
    pallas_call x0 -> x4, Pallas kernels: none -> 57.1 us  [the longest x3 46.9 us: run_group(): pl.pallas_call(functools.partial(group_kernel, block_rows, plan, norm, of...]
    ppermute x0 -> x24, waiting for transfers between devices: none -> 55.2 us  [the longest x18 28.6 us: swap(): return lax.ppermute(array, 'shard', [(i, i ^ mask) for i in range(n_shard)])]
    dot_general x13 -> x0, matrix products: 53.8 us -> none  [the longest x8 29.3 us: one_head(): jnp.einsum('gqs,sd->qgd', weights, value_head, preferred_element_type=jnp...]
    unnamed x1 -> x0, blocking collectives: 42.5 us -> none
    sub x8 -> x0, matrix products: 39.4 us -> none  [one_head(): expanded = jnp.exp(scores - highest)]
    all_gather x2 -> x1, waiting for transfers between devices: 33 us -> 0.01 us  [per_device(): wo_all = lax.all_gather(wo, everyone, axis=0, tiled=True)]
    ppermute x0 -> x24, starting transfers between devices: none -> 32.9 us  [the longest x6 18.9 us: along_dp(): lax.ppermute(local, 'dp', [((i + shift) % n_dp, i) for i in range(n_dp)])]
    pmax x1 -> x0, blocking collectives: 24.8 us -> none  [per_device(): group_top = lax.pmax(block_peaks, 'shard')]
  transfers between devices with their start and end apart: 2 -> 25, of which waited for: 1 -> 9; matrix products, arithmetic and copies ran while one was open for 45% -> 9% of each run, Pallas kernels for 0% -> 26%
where the time goes in v2:
time: 180 us; the launch traced here: 179 us
  Pallas kernels  57.1 us (32%)
  waiting for transfers between devices  55.9 us (31%)
  starting transfers between devices  33 us (18%)
  between operations  14.4 us (8%)
  other arithmetic  10.9 us (6%)
  local copies, waits for them, and re-layouts  7.98 us (4%)
    pallas_call x3, Pallas kernels, run_group(): pl.pallas_call(functools.partial(group_kernel, block_rows, plan, norm, of...  46.9 us
    ppermute x18, waiting for transfers between devices, swap(): return lax.ppermute(array, 'shard', [(i, i ^ mask) for i in range(n_shard)])  28.6 us
    ppermute x6, waiting for transfers between devices, along_dp(): lax.ppermute(local, 'dp', [((i + shift) % n_dp, i) for i in range(n_dp)])  26.6 us
    ppermute x6, starting transfers between devices, along_dp(): lax.ppermute(local, 'dp', [((i + shift) % n_dp, i) for i in range(n_dp)])  18.9 us
    ppermute x18, starting transfers between devices, swap(): return lax.ppermute(array, 'shard', [(i, i ^ mask) for i in range(n_shard)])  14.1 us
    pallas_call x1, Pallas kernels, output(): pl.pallas_call(functools.partial(output_kernel, requests, block_rows, pla...  10.3 us
    select_n x2, other arithmetic, per_device(): jnp.where(core == 0, cache[:, :, half:], cache[:, :, :half])  4.89 us
  transfers between devices with their start and end apart: 25, of which 9 were waited for; matrix products, arithmetic and copies ran while one was open for 9% of the time, Pallas kernels for 26%

profile of v2, /device:TPU:0, one launch (start us, length us, event | category | flops | bytes accessed | tf_op | source)
XLA Modules:
  0.0 179.4 jit_solution(12107467475483321589)
XLA Ops:
  7.9 1.0 fusion.34
  8.9 0.8 fusion.33
  10.6 3.6 %slice_select_fusion = bf16[4,512,384]{2,1,0:T(8,128)(2,1)} fusion(bf16[4,512,768]{2,1,0:T(8,128)(2,1)} %refs_14_.3, pred[]{:T(512)S(6)} %eq.15), kind=kLoop, calls=%fused_computation | loop fusion | flops 786432 | bytes 4718593 | tf_op jit(solution)/shard_map/jit(_where)/select_n | solution.py:497
  14.7 1.3 slice_select_fusion.1
  16.2 4.6 %collective-permute-start.1 = (bf16[96,896]{1,0:T(8,128)(2,1)S(1)}, bf16[96,896]{1,0:T(8,128)(2,1)S(1)}, u32[]{:S(2)}, u32[]{:S(2)}) collective-permute-start(bf16[96,896]{1,0:T(8,128)(2,1)S(1)} %fusion.4), channel_id=1, source_target_pairs={{8,0},{16,8},{24,16},{0,24},{9,1},{17,9},{25,17},{1,25},{10,2},{18... | collective-permute-start | bytes 516104 | tf_op jit(solution)/shard_map/ppermute | solution.py:447
  20.8 1.0 collective-permute-start.3
  21.8 4.8 %collective-permute-done.1 = bf16[96,896]{1,0:T(8,128)(2,1)S(1)} collective-permute-done((bf16[96,896]{1,0:T(8,128)(2,1)S(1)}, bf16[96,896]{1,0:T(8,128)(2,1)S(1)}, u32[]{:S(2)}, u32[]{:S(2)}) %collective-permute-start.1) | collective-permute-done | bytes 172064 | tf_op jit(solution)/shard_map/ppermute | solution.py:447
  26.6 12.4 %collective-permute-done.2 = bf16[96,896]{1,0:T(8,128)(2,1)S(1)} collective-permute-done((bf16[96,896]{1,0:T(8,128)(2,1)S(1)}, bf16[96,896]{1,0:T(8,128)(2,1)S(1)}, u32[]{:S(2)}, u32[]{:S(2)}) %collective-permute-start.2) | collective-permute-done | bytes 172064 | tf_op jit(solution)/shard_map/ppermute | solution.py:447
  39.1 1.6 collective-permute-start.4
  40.7 1.5 collective-permute-start.5
  42.2 1.5 fusion.3
  43.8 16.6 %collective-permute-done.4.refs_5_ = bf16[384,896]{1,0:T(8,128)(2,1)S(1)} collective-permute-done((bf16[384,896]{1,0:T(8,128)(2,1)S(1)}, bf16[384,896]{1,0:T(8,128)(2,1)S(1)}, u32[]{:S(2)}, u32[]{:S(2)}) %collective-permute-start.4) | collective-permute-done | bytes 688160 | tf_op jit(solution)/shard_map/ppermute | solution.py:437
  60.5 2.5 %collective-permute-start.12 = (bf16[96,768]{1,0:T(8,128)(2,1)S(1)}, bf16[96,768]{1,0:T(8,128)(2,1)S(1)}, u32[]{:S(2)}, u32[]{:S(2)}) collective-permute-start(bf16[96,768]{1,0:T(8,128)(2,1)S(1)} %pad_maximum_fusion.6), channel_id=1, source_target_pairs={{16,0},{24,8},{0,16},{8,24},{17,1},{25,9},{1,17},{9,25},{18,2},{26... | collective-permute-start | bytes 442376 | tf_op jit(solution)/shard_map/ppermute | solution.py:447
  63.1 2.9 %collective-permute-done.11 = bf16[96,768]{1,0:T(8,128)(2,1)S(1)} collective-permute-done((bf16[96,768]{1,0:T(8,128)(2,1)S(1)}, bf16[96,768]{1,0:T(8,128)(2,1)S(1)}, u32[]{:S(2)}, u32[]{:S(2)}) %collective-permute-start.11) | collective-permute-done | bytes 147488 | tf_op jit(solution)/shard_map/ppermute | solution.py:447
  66.1 10.7 %collective-permute-start.13 = (bf16[96,768]{1,0:T(8,128)(2,1)S(1)}, bf16[96,768]{1,0:T(8,128)(2,1)S(1)}, u32[]{:S(2)}, u32[]{:S(2)}) collective-permute-start(bf16[96,768]{1,0:T(8,128)(2,1)S(1)} %pad_maximum_fusion.6), channel_id=1, source_target_pairs={{24,0},{0,8},{8,16},{16,24},{25,1},{1,9},{9,17},{17,25},{26,2},{2,... | collective-permute-start | bytes 442376 | tf_op jit(solution)/shard_map/ppermute | solution.py:447
  77.6 6.4 %collective-permute-done.12 = bf16[96,768]{1,0:T(8,128)(2,1)S(1)} collective-permute-done((bf16[96,768]{1,0:T(8,128)(2,1)S(1)}, bf16[96,768]{1,0:T(8,128)(2,1)S(1)}, u32[]{:S(2)}, u32[]{:S(2)}) %collective-permute-start.12) | collective-permute-done | bytes 147488 | tf_op jit(solution)/shard_map/ppermute | solution.py:447
  84.0 2.2 %collective-permute-start.6 = (bf16[384,512]{1,0:T(8,128)(2,1)S(1)}, bf16[384,512]{1,0:T(8,128)(2,1)}, u32[]{:S(2)}, u32[]{:S(2)}) collective-permute-start(bf16[384,512]{1,0:T(8,128)(2,1)S(1)} %slice.94), channel_id=1, source_target_pairs={{0,4},{1,5},{2,6},{3,7},{4,0},{5,1},{6,2},{7,3},{8,12},{9,13},{10,... | collective-permute-start | bytes 1179656 | tf_op jit(solution)/shard_map/ppermute | solution.py:437
  86.8 1.0 slice.95
  89.1 1.1 pad_maximum_fusion.refs_11_.refs_10_.refs_7_
  90.2 7.5 %collective-permute-done.7.refs_8_ = bf16[384,384]{1,0:T(8,128)(2,1)S(1)} collective-permute-done((bf16[384,384]{1,0:T(8,128)(2,1)S(1)}, bf16[384,384]{1,0:T(8,128)(2,1)S(1)}, u32[]{:S(2)}, u32[]{:S(2)}) %collective-permute-start.7) | collective-permute-done | bytes 294944 | tf_op jit(solution)/shard_map/ppermute | solution.py:437
  98.5 22.8 %group.3 = (bf16[768,512]{1,0:T(8,128)(2,1)}, bf16[768,512]{1,0:T(8,128)(2,1)}, f32[3,3,8,256]{3,2,1,0:T(8,128)}, bf16[768,1536]{1,0:T(8,128)(2,1)}, bf16[768,15...) custom-call(s32[16]{0:T(128)} %fusion.32.refs_0_, s32[1]{0:T(128)S(6)} %mul.113.refs_1_, s32[4]{0:T(128)} %refs_2_.3, ...), custom_call_target="tpu_custom_call" | custom-call | flops 22000001024 | bytes 100000 | tf_op jit(solution)/shard_map/group/pallas_call | solution.py:316
  121.4 1.5 collective-permute-start.17
  122.9 2.0 %collective-permute-start.16 = (bf16[384,384]{1,0:T(8,128)(2,1)S(1)}, bf16[384,384]{1,0:T(8,128)(2,1)S(1)}, u32[]{:S(2)}, u32[]{:S(2)}) collective-permute-start(bf16[384,384]{1,0:T(8,128)(2,1)S(1)} %slice.90), channel_id=1, source_target_pairs={{0,4},{1,5},{2,6},{3,7},{4,0},{5,1},{6,2},{7,3},{8,12},{9,13},{10,... | collective-permute-start | bytes 884744 | tf_op jit(solution)/shard_map/ppermute | solution.py:437
  124.9 0.9 constant_dynamic-update-slice_fusion.1
  125.8 2.3 %collective-permute-done.17.refs_8_.refs_5_ = bf16[384,384]{1,0:T(8,128)(2,1)S(1)} collective-permute-done((bf16[384,384]{1,0:T(8,128)(2,1)S(1)}, bf16[384,384]{1,0:T(8,128)(2,1)S(1)}, u32[]{:S(2)}, u32[]{:S(2)}) %collective-permute-start.17) | collective-permute-done | bytes 294944 | tf_op jit(solution)/shard_map/ppermute | solution.py:437
  128.2 1.5 collective-permute-done.16.refs_7_.refs_4_
  130.4 13.4 %group.4 = (bf16[768,512]{1,0:T(8,128)(2,1)}, f32[3,3,8,256]{3,2,1,0:T(8,128)}) custom-call(s32[16]{0:T(128)} %fusion.32.refs_0_, s32[1]{0:T(128)S(6)} %add.88.refs_1_, s32[4]{0:T(128)} %refs_2_.3, s32[2]{0:T(128)} %pad_add_fusion.1.refs_3_, bf16[384,768]{1,0:T(8,128)(2,1)} %copy-done.2, bf16[384,768]{1,0:T(8,128)(2,1)} %copy-done.6, ...), custom_call_target="tpu_custom_call" | custom-call | flops 11000000512 | bytes 100000 | tf_op jit(solution)/shard_map/group/pallas_call | solution.py:316
  143.8 0.9 constant_dynamic-update-slice_fusion
  145.3 1.4 collective-permute-start.21
  146.8 1.5 collective-permute-start.22
  148.2 10.6 %group.5.rest_2_ = bf16[768,512]{1,0:T(8,128)(2,1)} custom-call(s32[16]{0:T(128)} %fusion.32.refs_0_, bf16[384,768]{1,0:T(8,128)(2,1)} %copy-done.2, bf16[384,768]{1,0:T(8,128)(2,1)} %copy-done.6, bf16[384,768]{1,0:T(8,128)(2,1)} %copy-done.5, bf16[384,384]{1,0:T(8,128)(2,1)} %copy-done.16, bf16[384,384]{1,0:T(8,128)(2,1)} %copy-done.14, ...), custom_call_target="tpu_custom_call" | custom-call | flops 11000000512 | bytes 100000 | tf_op jit(solution)/shard_map/group/pallas_call | solution.py:316
  162.3 10.3 %output.1 = (bf16[768,1536]{1,0:T(8,128)(2,1)}, bf16[4,1536]{1,0:T(4,128)(2,1)}) custom-call(s32[2]{0:T(128)} %pad_add_fusion.core_ref, s32[16]{0:T(128)} %iota_multiply_fusion.offs_ref, bf16[1536,1536]{1,0:T(8,128)(2,1)} %all-gather.2.cloned.1.call-done.rest_0_, bf16[768,512]{1,0:T(8,128)(2,1)} %get-tuple-element.16.rest_1_, ...), custom_call_target="tpu_custom_call" | custom-call | flops 9900000256 | bytes 100000 | tf_op jit(solution)/shard_map/output/pallas_call | solution.py:410
  (97 shorter events, 10.5 us)
Async XLA Ops:
  7.2 154.0 %all-gather.2.cloned.1.call-start = ((), (), s32[]{:S(2)}) async-start(), calls=%async_computation | async-start | bytes 4866048 | tf_op jit(solution)/shard_map/all_gather | solution.py:492
  10.1 6.0 %collective-permute-start = (bf16[48,1664]{1,0:T(8,128)(2,1)S(1)}, bf16[48,1664]{1,0:T(8,128)(2,1)S(1)}, u32[]{:S(2)}, u32[]{:S(2)}) collective-permute-start(bf16[48,1664]{1,0:T(8,128)(2,1)S(1)} %pad_maximum_fusion.4), channel_id=1, source_target_pairs={{0,1},{1,0},{2,3},{3,2},{4,5},{5,4},{6,7},{7,6},{8,9},{9,8},{10,11... | collective-permute-start | bytes 479240 | tf_op jit(solution)/shard_map/ppermute | solution.py:437
  14.2 83.6 %collective-permute-start.10 = (bf16[4,512,384]{2,1,0:T(8,128)(2,1)}, bf16[4,512,384]{2,1,0:T(8,128)(2,1)}, u32[]{:S(2)}, u32[]{:S(2)}) collective-permute-start(bf16[4,512,384]{2,1,0:T(8,128)(2,1)} %slice_select_fusion), channel_id=1, source_target_pairs={{0,1},{1,0},{2,3},{3,2},{4,5},{5,4},{6,7},{7,6},{8,9},{9,8},{10,11... | collective-permute-start | bytes 4718600 | tf_op jit(solution)/shard_map/ppermute | solution.py:437
  14.2 83.7 %collective-permute-start.8 = (bf16[768,1536]{1,0:T(8,128)(2,1)}, bf16[768,1536]{1,0:T(8,128)(2,1)}, u32[]{:S(2)}, u32[]{:S(2)}) collective-permute-start(bf16[768,1536]{1,0:T(8,128)(2,1)} %refs_9_.1), channel_id=1, source_target_pairs={{0,1},{1,0},{2,3},{3,2},{4,5},{5,4},{6,7},{7,6},{8,9},{9,8},{10,11... | collective-permute-start | bytes 7077896 | tf_op jit(solution)/shard_map/ppermute | solution.py:437
  16.1 26.1 %copy-start.17 = (s32[4]{0:T(128)S(1)}, s32[4]{0:T(128)}, u32[]{:S(2)}) copy-start(s32[4]{0:T(128)} %refs_2_.3) | copy-start | bytes 52
  16.2 60.7 %copy-start.8 = (f32[3,16,192]{2,1,0:T(8,128)S(1)}, f32[3,16,192]{2,1,0:T(8,128)}, u32[]{:S(2)}) copy-start(f32[3,16,192]{2,1,0:T(8,128)} %constant.116.clone.1) | copy-start | bytes 110596
  16.2 10.4 %collective-permute-start.1 = (bf16[96,896]{1,0:T(8,128)(2,1)S(1)}, bf16[96,896]{1,0:T(8,128)(2,1)S(1)}, u32[]{:S(2)}, u32[]{:S(2)}) collective-permute-start(bf16[96,896]{1,0:T(8,128)(2,1)S(1)} %fusion.4), channel_id=1, source_target_pairs={{8,0},{16,8},{24,16},{0,24},{9,1},{17,9},{25,17},{1,25},{10,2},{18... | collective-permute-start | bytes 516104 | tf_op jit(solution)/shard_map/ppermute | solution.py:447
  20.8 18.3 %collective-permute-start.2 = (bf16[96,896]{1,0:T(8,128)(2,1)S(1)}, bf16[96,896]{1,0:T(8,128)(2,1)S(1)}, u32[]{:S(2)}, u32[]{:S(2)}) collective-permute-start(bf16[96,896]{1,0:T(8,128)(2,1)S(1)} %fusion.4), channel_id=1, source_target_pairs={{16,0},{24,8},{0,16},{8,24},{17,1},{25,9},{1,17},{9,25},{18,2},{26... | collective-permute-start | bytes 516104 | tf_op jit(solution)/shard_map/ppermute | solution.py:447
  20.8 18.3 %collective-permute-start.3 = (bf16[96,896]{1,0:T(8,128)(2,1)S(1)}, bf16[96,896]{1,0:T(8,128)(2,1)S(1)}, u32[]{:S(2)}, u32[]{:S(2)}) collective-permute-start(bf16[96,896]{1,0:T(8,128)(2,1)S(1)} %fusion.4), channel_id=1, source_target_pairs={{24,0},{0,8},{8,16},{16,24},{25,1},{1,9},{9,17},{17,25},{26,2},{2,... | collective-permute-start | bytes 516104 | tf_op jit(solution)/shard_map/ppermute | solution.py:447
  26.6 71.2 %collective-permute-start.9 = (bf16[4,512,384]{2,1,0:T(8,128)(2,1)}, bf16[4,512,384]{2,1,0:T(8,128)(2,1)}, u32[]{:S(2)}, u32[]{:S(2)}) collective-permute-start(bf16[4,512,384]{2,1,0:T(8,128)(2,1)} %slice_select_fusion.1), channel_id=1, source_target_pairs={{0,1},{1,0},{2,3},{3,2},{4,5},{5,4},{6,7},{7,6},{8,9},{9,8},{10,11... | collective-permute-start | bytes 4718600 | tf_op jit(solution)/shard_map/ppermute | solution.py:437
  39.1 48.7 %copy-start.1 = (bf16[384,896]{1,0:T(8,128)(2,1)}, bf16[384,896]{1,0:T(8,128)(2,1)S(1)}, u32[]{:S(2)}) copy-start(bf16[384,896]{1,0:T(8,128)(2,1)S(1)} %pad_maximum_fusion.1.refs_4_) | copy-start | bytes 2064388
  39.1 21.3 %collective-permute-start.4 = (bf16[384,896]{1,0:T(8,128)(2,1)S(1)}, bf16[384,896]{1,0:T(8,128)(2,1)S(1)}, u32[]{:S(2)}, u32[]{:S(2)}) collective-permute-start(bf16[384,896]{1,0:T(8,128)(2,1)S(1)} %pad_maximum_fusion.1.refs_4_), channel_id=1, source_target_pairs={{0,2},{1,3},{2,0},{3,1},{4,6},{5,7},{6,4},{7,5},{8,10},{9,11},{10,... | collective-permute-start | bytes 2064392 | tf_op jit(solution)/shard_map/ppermute | solution.py:437
  40.7 19.7 %collective-permute-start.5 = (bf16[384,896]{1,0:T(8,128)(2,1)S(1)}, bf16[384,896]{1,0:T(8,128)(2,1)S(1)}, u32[]{:S(2)}, u32[]{:S(2)}) collective-permute-start(bf16[384,896]{1,0:T(8,128)(2,1)S(1)} %pad_maximum_fusion.1.refs_4_), channel_id=1, source_target_pairs={{0,4},{1,5},{2,6},{3,7},{4,0},{5,1},{6,2},{7,3},{8,12},{9,13},{10,... | collective-permute-start | bytes 2064392 | tf_op jit(solution)/shard_map/ppermute | solution.py:437
  42.2 46.2 %copy-start.9 = (bf16[4,1536]{1,0:T(4,128)(2,1)S(1)}, bf16[4,1536]{1,0:T(4,128)(2,1)}, u32[]{:S(2)}) copy-start(bf16[4,1536]{1,0:T(4,128)(2,1)} %param.9) | copy-start | bytes 36868
  60.4 29.8 %copy-start.4 = (bf16[384,896]{1,0:T(8,128)(2,1)}, bf16[384,896]{1,0:T(8,128)(2,1)S(1)}, u32[]{:S(2)}) copy-start(bf16[384,896]{1,0:T(8,128)(2,1)S(1)} %collective-permute-done.4.refs_5_) | copy-start | bytes 2064388
  60.4 5.7 %collective-permute-start.11 = (bf16[96,768]{1,0:T(8,128)(2,1)S(1)}, bf16[96,768]{1,0:T(8,128)(2,1)S(1)}, u32[]{:S(2)}, u32[]{:S(2)}) collective-permute-start(bf16[96,768]{1,0:T(8,128)(2,1)S(1)} %pad_maximum_fusion.6), channel_id=1, source_target_pairs={{8,0},{16,8},{24,16},{0,24},{9,1},{17,9},{25,17},{1,25},{10,2},{18... | collective-permute-start | bytes 442376 | tf_op jit(solution)/shard_map/ppermute | solution.py:447
  60.5 23.6 %collective-permute-start.12 = (bf16[96,768]{1,0:T(8,128)(2,1)S(1)}, bf16[96,768]{1,0:T(8,128)(2,1)S(1)}, u32[]{:S(2)}, u32[]{:S(2)}) collective-permute-start(bf16[96,768]{1,0:T(8,128)(2,1)S(1)} %pad_maximum_fusion.6), channel_id=1, source_target_pairs={{16,0},{24,8},{0,16},{8,24},{17,1},{25,9},{1,17},{9,25},{18,2},{26... | collective-permute-start | bytes 442376 | tf_op jit(solution)/shard_map/ppermute | solution.py:447
  66.1 21.7 %collective-permute-start.13 = (bf16[96,768]{1,0:T(8,128)(2,1)S(1)}, bf16[96,768]{1,0:T(8,128)(2,1)S(1)}, u32[]{:S(2)}, u32[]{:S(2)}) collective-permute-start(bf16[96,768]{1,0:T(8,128)(2,1)S(1)} %pad_maximum_fusion.6), channel_id=1, source_target_pairs={{24,0},{0,8},{8,16},{16,24},{25,1},{1,9},{9,17},{17,25},{26,2},{2,... | collective-permute-start | bytes 442376 | tf_op jit(solution)/shard_map/ppermute | solution.py:447
  84.0 13.7 %collective-permute-start.6 = (bf16[384,512]{1,0:T(8,128)(2,1)S(1)}, bf16[384,512]{1,0:T(8,128)(2,1)}, u32[]{:S(2)}, u32[]{:S(2)}) collective-permute-start(bf16[384,512]{1,0:T(8,128)(2,1)S(1)} %slice.94), channel_id=1, source_target_pairs={{0,4},{1,5},{2,6},{3,7},{4,0},{5,1},{6,2},{7,3},{8,12},{9,13},{10,... | collective-permute-start | bytes 1179656 | tf_op jit(solution)/shard_map/ppermute | solution.py:437
  87.8 9.9 %collective-permute-start.7 = (bf16[384,384]{1,0:T(8,128)(2,1)S(1)}, bf16[384,384]{1,0:T(8,128)(2,1)S(1)}, u32[]{:S(2)}, u32[]{:S(2)}) collective-permute-start(bf16[384,384]{1,0:T(8,128)(2,1)S(1)} %slice.95), channel_id=1, source_target_pairs={{0,2},{1,3},{2,0},{3,1},{4,6},{5,7},{6,4},{7,5},{8,10},{9,11},{10,... | collective-permute-start | bytes 884744 | tf_op jit(solution)/shard_map/ppermute | solution.py:437
  90.2 31.1 %copy-start.2 = (bf16[384,768]{1,0:T(8,128)(2,1)}, bf16[384,768]{1,0:T(8,128)(2,1)S(1)}, u32[]{:S(2)}) copy-start(bf16[384,768]{1,0:T(8,128)(2,1)S(1)} %pad_maximum_fusion.2.refs_4_.refs_1_) | copy-start | bytes 1769476
  97.8 23.6 %collective-permute-start.15 = (bf16[384,768]{1,0:T(8,128)(2,1)S(1)}, bf16[384,768]{1,0:T(8,128)(2,1)S(1)}, u32[]{:S(2)}, u32[]{:S(2)}) collective-permute-start(bf16[384,768]{1,0:T(8,128)(2,1)S(1)} %pad_maximum_fusion.2.refs_4_.refs_1_), channel_id=1, source_target_pairs={{0,4},{1,5},{2,6},{3,7},{4,0},{5,1},{6,2},{7,3},{8,12},{9,13},{10,... | collective-permute-start | bytes 1769480 | tf_op jit(solution)/shard_map/ppermute | solution.py:437
  97.8 25.1 %collective-permute-start.14 = (bf16[384,768]{1,0:T(8,128)(2,1)S(1)}, bf16[384,768]{1,0:T(8,128)(2,1)S(1)}, u32[]{:S(2)}, u32[]{:S(2)}) collective-permute-start(bf16[384,768]{1,0:T(8,128)(2,1)S(1)} %pad_maximum_fusion.2.refs_4_.refs_1_), channel_id=1, source_target_pairs={{0,2},{1,3},{2,0},{3,1},{4,6},{5,7},{6,4},{7,5},{8,10},{9,11},{10,... | collective-permute-start | bytes 1769480 | tf_op jit(solution)/shard_map/ppermute | solution.py:437
  121.3 8.4 %copy-start.5 = (bf16[384,768]{1,0:T(8,128)(2,1)}, bf16[384,768]{1,0:T(8,128)(2,1)S(1)}, u32[]{:S(2)}) copy-start(bf16[384,768]{1,0:T(8,128)(2,1)S(1)} %collective-permute-done.15.refs_6_.refs_3_) | copy-start | bytes 1769476
  121.4 6.8 %collective-permute-start.17 = (bf16[384,384]{1,0:T(8,128)(2,1)S(1)}, bf16[384,384]{1,0:T(8,128)(2,1)S(1)}, u32[]{:S(2)}, u32[]{:S(2)}) collective-permute-start(bf16[384,384]{1,0:T(8,128)(2,1)S(1)} %slice.91), channel_id=1, source_target_pairs={{0,2},{1,3},{2,0},{3,1},{4,6},{5,7},{6,4},{7,5},{8,10},{9,11},{10,... | collective-permute-start | bytes 884744 | tf_op jit(solution)/shard_map/ppermute | solution.py:437
  122.9 6.8 %collective-permute-start.16 = (bf16[384,384]{1,0:T(8,128)(2,1)S(1)}, bf16[384,384]{1,0:T(8,128)(2,1)S(1)}, u32[]{:S(2)}, u32[]{:S(2)}) collective-permute-start(bf16[384,384]{1,0:T(8,128)(2,1)S(1)} %slice.90), channel_id=1, source_target_pairs={{0,4},{1,5},{2,6},{3,7},{4,0},{5,1},{6,2},{7,3},{8,12},{9,13},{10,... | collective-permute-start | bytes 884744 | tf_op jit(solution)/shard_map/ppermute | solution.py:437
  124.9 35.7 %collective-permute-start.18 = (bf16[768,512]{1,0:T(8,128)(2,1)}, bf16[768,512]{1,0:T(8,128)(2,1)S(1)}, u32[]{:S(2)}, u32[]{:S(2)}) collective-permute-start(bf16[768,512]{1,0:T(8,128)(2,1)} %get-tuple-element.19), channel_id=1, source_target_pairs={{0,1},{1,0},{2,3},{3,2},{4,5},{5,4},{6,7},{7,6},{8,9},{9,8},{10,11... | collective-permute-start | bytes 2359304 | tf_op jit(solution)/shard_map/ppermute | solution.py:437
  144.7 14.1 %collective-permute-start.20 = (f32[3,3,8,512]{3,2,1,0:T(8,128)S(1)}, f32[3,3,8,512]{3,2,1,0:T(8,128)S(1)}, u32[]{:S(2)}, u32[]{:S(2)}) collective-permute-start(f32[3,3,8,512]{3,2,1,0:T(8,128)S(1)} %constant_dynamic-update-slice_fusion), channel_id=1, source_target_pairs={{0,2},{1,3},{2,0},{3,1},{4,6},{5,7},{6,4},{7,5},{8,10},{9,11},{10,... | collective-permute-start | bytes 442376 | tf_op jit(solution)/shard_map/ppermute | solution.py:437
  145.3 13.5 %collective-permute-start.21 = (f32[3,3,8,512]{3,2,1,0:T(8,128)S(1)}, f32[3,3,8,512]{3,2,1,0:T(8,128)S(1)}, u32[]{:S(2)}, u32[]{:S(2)}) collective-permute-start(f32[3,3,8,512]{3,2,1,0:T(8,128)S(1)} %constant_dynamic-update-slice_fusion), channel_id=1, source_target_pairs={{0,4},{1,5},{2,6},{3,7},{4,0},{5,1},{6,2},{7,3},{8,12},{9,13},{10,... | collective-permute-start | bytes 442376 | tf_op jit(solution)/shard_map/ppermute | solution.py:437
  146.8 12.1 %collective-permute-start.22 = (f32[3,3,8,512]{3,2,1,0:T(8,128)S(1)}, f32[3,3,8,512]{3,2,1,0:T(8,128)S(1)}, u32[]{:S(2)}, u32[]{:S(2)}) collective-permute-start(f32[3,3,8,512]{3,2,1,0:T(8,128)S(1)} %constant_dynamic-update-slice_fusion), channel_id=1, source_target_pairs={{0,6},{1,7},{2,4},{3,5},{4,2},{5,3},{6,0},{7,1},{8,14},{9,15},{10,... | collective-permute-start | bytes 442376 | tf_op jit(solution)/shard_map/ppermute | solution.py:437
  148.2 12.9 %collective-permute-start.19 = (bf16[768,512]{1,0:T(8,128)(2,1)}, bf16[768,512]{1,0:T(8,128)(2,1)S(1)}, u32[]{:S(2)}, u32[]{:S(2)}) collective-permute-start(bf16[768,512]{1,0:T(8,128)(2,1)} %get-tuple-element.25), channel_id=1, source_target_pairs={{0,1},{1,0},{2,3},{3,2},{4,5},{5,4},{6,7},{7,6},{8,9},{9,8},{10,11... | collective-permute-start | bytes 2359304 | tf_op jit(solution)/shard_map/ppermute | solution.py:437
  158.9 2.2 %collective-permute-start.23 = (f32[4,3,3,8,512]{4,3,2,1,0:T(8,128)S(1)}, f32[4,3,3,8,512]{4,3,2,1,0:T(8,128)S(1)}, u32[]{:S(2)}, u32[]{:S(2)}) collective-permute-start(f32[4,3,3,8,512]{4,3,2,1,0:T(8,128)S(1)} %pad_maximum_fusion.3.rest_5_), channel_id=1, source_target_pairs={{0,1},{1,0},{2,3},{3,2},{4,5},{5,4},{6,7},{7,6},{8,9},{9,8},{10,11... | collective-permute-start | bytes 1769480 | tf_op jit(solution)/shard_map/ppermute | solution.py:437
  (11 other events, 28.0 us)
Sparse Core Ops, SparseCore 0:
  10.9 79.5 all-gather.1

commit v3 on v2

--- a/solution.py
+++ b/solution.py
@@ -217,7 +217,8 @@
         (part_ref,) = take()
     if norm:
         xn_hbm = take(stretches)
-        (dxn_ref,) = take()
+        if with_decode:
+            (dxn_ref,) = take()
     x_refs, u_refs, heads_refs = take(stretches), take(stretches), take(stretches)
     (w_ref,) = take()
     if with_decode:
@@ -238,7 +239,7 @@
     if with_decode:
         window = k_ref.shape[3]
         for n, source in enumerate(caches):
-            lane = pl.multiple_of(lane_ref[0], LANES) if n < 2 else 0 if offset == 0 else LANES
+            lane = pl.multiple_of(lane_ref[0], LANES)
             pltpu.make_async_copy(
                 source.at[:, :, pl.ds(lane, window)], (k_ref, v_ref)[n % 2].at[n // 2], sem.at[4 + n]
             ).start()
@@ -246,7 +247,8 @@
         pltpu.make_async_copy(gain_ref, gain_ref, sem.at[1]).wait()
         pick = (lax.broadcasted_iota(jnp.int32, (8, LANES), 1) == 0).astype(BF16)
         gain = lax.dot_general(pick, gain_ref[...], (((1,), (1,)), ((), ())), preferred_element_type=F32)[0:1]
-        dxn_ref[...] = normalize(dx_ref[...], gain)
+        if with_decode:
+            dxn_ref[...] = normalize(dx_ref[...], gain)
     saves = []
     for n in range(stretches):
         loads[n].wait()
@@ -301,8 +303,10 @@
         out_specs.append(vmem)
     if norm:
         out_shape += [jax.ShapeDtypeStruct((stretch, depth), BF16)] * stretches
-        out_shape.append(jax.ShapeDtypeStruct((extra, depth), BF16))
-        out_specs += [hbm] * stretches + [vmem]
+        out_specs += [hbm] * stretches
+        if decoding:
+            out_shape.append(jax.ShapeDtypeStruct((extra, depth), BF16))
+            out_specs.append(vmem)
     rows_all = [stretch + (extra if n == 0 else 0) for n in range(stretches)]
     scratch = [pltpu.VMEM((count, depth), BF16) for count in rows_all]
     scratch += [pltpu.VMEM((count, width), F32) for count in rows_all]
@@ -445,7 +449,7 @@
     found = [local]
     for shift in range(1, n_dp):
         found.append(lax.ppermute(local, "dp", [((i + shift) % n_dp, i) for i in range(n_dp)]))
-    return jnp.concatenate(found, axis=0)
+    return found
 
 
 def pieces_of(here, beside, above, cut, n_shard):
@@ -492,10 +496,6 @@
     wo_all = lax.all_gather(wo, everyone, axis=0, tiled=True)
     wo_plan = [[(0, 0, 0, H)], [(0, width, 0, H)]]
     wo_offs = jnp.arange(H, dtype=jnp.int32) * LANES
-    sib_x = swap(prefill_x, 1, n_shard)
-    sib_caches = [
-        swap(jnp.where(core == 0, cache[:, :, half:], cache[:, :, :half]), 1, n_shard) for cache in (k_cache, v_cache)
-    ]
     extra = 16
     dx = jnp.pad(decode_x, ((0, extra - requests), (0, 0)))
     decode_positions = jnp.concatenate([cache_len, jnp.zeros((extra - requests,), jnp.int32)])
@@ -509,20 +509,24 @@
         mine = jnp.concatenate([gain_columns, jnp.where(first, low, high)], axis=1)
         theirs = jnp.concatenate([gain_columns, jnp.where(first, high, low)], axis=1)
         theirs = swap(theirs, 1, n_shard)
+        free = theirs
         pair = jnp.concatenate([jnp.where(first, mine, theirs), jnp.where(first, theirs, mine)], axis=0)
         order = jnp.arange(n_shard // 2 * n_dp, dtype=jnp.int32)
         chip = (me_dp + order % n_dp) % n_dp * (n_shard // 2) + (me // 2 ^ (order // n_dp))
         block_rows = 2 * block_rows
         offs = chip * block_rows
-        here = along_dp(pair[:, :head], n_dp)
+        found = along_dp(pair, n_dp)
+        here = jnp.concatenate([block[:, :head] for block in found], axis=0)
         beside, above = swap(here, 2, n_shard), swap(here, 4, n_shard)
-        later_here = along_dp(after(pair[:, head:], beside, above), n_dp)
         pieces = pieces_of(here, beside, above, LANES + half, n_shard)
         plan = lay_out(pieces, {LANES: 0, LANES + half: 1, 0: 2}, n_dp)
         pieces = [piece[0] for piece in pieces]
+        found[0] = after(found[0], beside)
+        later_here = jnp.concatenate([block[:, head:] for block in found], axis=0)
         later_here = after(later_here, *pieces)
         beside, above = swap(later_here, 2, n_shard), swap(later_here, 4, n_shard)
     else:
+        free = norm_gain
         offs = jnp.zeros((1,), jnp.int32)
         every = lax.all_gather(jnp.concatenate([gain_columns, low, high], axis=1), everyone, axis=0, tiled=True)
         block_rows = every.shape[0]
@@ -530,21 +534,24 @@
         pieces = [jnp.concatenate([every[:, :LANES], chosen[:, :width]], axis=1)]
         plan = [[(0, LANES, 0, 1)], [(0, LANES + half, 0, 1)], [(0, 0, 0, 1)]]
 
+    sib_x, sib_k, sib_v = [swap(after(array, free), 1, n_shard) for array in (prefill_x, k_cache, v_cache)]
     lane = core.astype(jnp.int32).reshape(1) * half
     starts = jnp.stack([me * span, (me ^ 1) * span]).astype(jnp.int32)
-    caches = [k_cache, v_cache, *sib_caches]
-    own_o, sib_o, part, xn, sib_xn, dxn = run_group(
-        [prefill_x, sib_x], tables, offs, pieces, block_rows, plan, norm=True,
+    caches = [k_cache, v_cache, sib_k, sib_v]
+    sib_o, part, sib_xn, dxn = run_group(
+        [sib_x], tables, offs, pieces, block_rows, plan, norm=True,
         decoding=(0, lane, cache_len, starts, dx, dtable, caches),
     )
+    later_pieces, later_plan = [], [[(0, 0, 0, 1)], [(0, half, 0, 1)]]
+    if split:
+        later_pieces = pieces_of(later_here, after(beside, sib_o), after(above, sib_o), half, n_shard)
+        later_plan = lay_out(later_pieces, {0: 0, half: 1}, n_dp)
+        later_pieces = [piece[0] for piece in later_pieces]
+    else:
+        later_pieces = [chosen[:, width:]]
+    own_o, xn = run_group([after(prefill_x, sib_o)], tables, offs, pieces, block_rows, plan, norm=True)
     mine, theirs = [own_o], [sib_o]
-    if split:
-        pieces = pieces_of(later_here, after(beside, sib_o), after(above, sib_o), half, n_shard)
-        plan = lay_out(pieces, {0: 0, half: 1}, n_dp)
-        pieces = [piece[0] for piece in pieces]
-    else:
-        pieces = [chosen[:, width:]]
-        plan = [[(0, 0, 0, 1)], [(0, half, 0, 1)]]
+    pieces, plan = [after(later_pieces[0], own_o)] + later_pieces[1:], later_plan
     sib_o, later_part = run_group(
         [sib_xn], tables, offs, pieces, block_rows, plan,
         decoding=(LANES // 2, lane + LANES, cache_len, starts, dxn, dtable, caches),

time: 180 us -> 169 us (0.939)
  starting transfers between devices: 33 us -> 21.5 us
  other arithmetic: 10.9 us -> 6.14 us
  Pallas kernels: 57.1 us -> 61 us
  waiting for transfers between devices: 55.9 us -> 58.8 us
    ppermute x6 -> x3, starting transfers between devices: 18.9 us -> 4.87 us  [along_dp(): lax.ppermute(local, 'dp', [((i + shift) % n_dp, i) for i in range(n_dp)])]
    select_n x3 -> x1, other arithmetic: 4.95 us -> 0.06 us  [per_device(): jnp.where(first, mine, theirs)]
    ppermute x6 -> x3, waiting for transfers between devices: 26.6 us -> 30.8 us  [along_dp(): lax.ppermute(local, 'dp', [((i + shift) % n_dp, i) for i in range(n_dp)])]
    pallas_call x3 -> x4, Pallas kernels: 46.9 us -> 50.8 us  [run_group(): pl.pallas_call(functools.partial(group_kernel, block_rows, plan, norm, of...]
    ppermute x18, starting transfers between devices: 14.1 us -> 16.5 us  [swap(): return lax.ppermute(array, 'shard', [(i, i ^ mask) for i in range(n_shard)])]
  transfers between devices with their start and end apart: 25 -> 22, of which waited for: 9 -> 6; matrix products, arithmetic and copies ran while one was open for 9% -> 6% of each run, Pallas kernels for 26% -> 30%
where the time goes in v3:
time: 169 us
  Pallas kernels  61 us (36%)
  waiting for transfers between devices  58.8 us (35%)
  starting transfers between devices  21.5 us (13%)
  between operations  14.5 us (9%)
  local copies, waits for them, and re-layouts  6.74 us (4%)
  other arithmetic  6.14 us (4%)
    pallas_call x4, Pallas kernels, run_group(): pl.pallas_call(functools.partial(group_kernel, block_rows, plan, norm, of...  50.8 us
    ppermute x3, waiting for transfers between devices, along_dp(): lax.ppermute(local, 'dp', [((i + shift) % n_dp, i) for i in range(n_dp)])  30.8 us
    ppermute x18, waiting for transfers between devices, swap(): return lax.ppermute(array, 'shard', [(i, i ^ mask) for i in range(n_shard)])  27.4 us
    ppermute x18, starting transfers between devices, swap(): return lax.ppermute(array, 'shard', [(i, i ^ mask) for i in range(n_shard)])  16.5 us
    pallas_call x1, Pallas kernels, output(): pl.pallas_call(functools.partial(output_kernel, requests, block_rows, pla...  10.3 us
    ppermute x3, starting transfers between devices, along_dp(): lax.ppermute(local, 'dp', [((i + shift) % n_dp, i) for i in range(n_dp)])  4.87 us
  transfers between devices with their start and end apart: 22, of which 6 were waited for; matrix products, arithmetic and copies ran while one was open for 6% of the time, Pallas kernels for 30%

profile of v3, /device:TPU:0, one launch (start us, length us, event | category | flops | bytes accessed | tf_op | source)
XLA Modules:
  0.0 168.8 jit_solution(3050157624688210547)
XLA Ops:
  7.2 0.7 all-gather.2.cloned.1.call-update
  7.9 1.0 fusion.34
  8.9 0.8 fusion.33
  10.6 1.0 collective-permute-done
  12.7 4.8 %collective-permute-start.1 = (bf16[96,1664]{1,0:T(8,128)(2,1)S(1)}, bf16[96,1664]{1,0:T(8,128)(2,1)S(1)}, u32[]{:S(2)}, u32[]{:S(2)}) collective-permute-start(bf16[96,1664]{1,0:T(8,128)(2,1)S(1)} %pad_maximum_fusion.4), channel_id=1, source_target_pairs={{8,0},{16,8},{24,16},{0,24},{9,1},{17,9},{25,17},{1,25},{10,2},{18... | collective-permute-start | bytes 958472 | tf_op jit(solution)/shard_map/ppermute | solution.py:451
  17.7 8.9 %collective-permute-done.1 = bf16[96,1664]{1,0:T(8,128)(2,1)S(1)} collective-permute-done((bf16[96,1664]{1,0:T(8,128)(2,1)S(1)}, bf16[96,1664]{1,0:T(8,128)(2,1)S(1)}, u32[]{:S(2)}, u32[]{:S(2)}) %collective-permute-start.1) | collective-permute-done | bytes 319520 | tf_op jit(solution)/shard_map/ppermute | solution.py:451
  26.7 21.8 %collective-permute-done.2 = bf16[96,1664]{1,0:T(8,128)(2,1)S(1)} collective-permute-done((bf16[96,1664]{1,0:T(8,128)(2,1)S(1)}, bf16[96,1664]{1,0:T(8,128)(2,1)S(1)}, u32[]{:S(2)}, u32[]{:S(2)}) %collective-permute-start.2) | collective-permute-done | bytes 319520 | tf_op jit(solution)/shard_map/ppermute | solution.py:451
  48.6 1.6 collective-permute-start.4
  50.2 1.5 collective-permute-start.5
  51.9 0.7 fusion.6.refs_12_
  52.7 1.5 fusion.3
  54.2 15.6 %collective-permute-done.4.refs_5_.refs_2_ = bf16[384,896]{1,0:T(8,128)(2,1)S(1)} collective-permute-done((bf16[384,896]{1,0:T(8,128)(2,1)S(1)}, bf16[384,896]{1,0:T(8,128)(2,1)S(1)}, u32[]{:S(2)}, u32[]{:S(2)}) %collective-permute-start.4) | collective-permute-done | bytes 688160 | tf_op jit(solution)/shard_map/ppermute | solution.py:441
  69.8 1.6 collective-permute-start.6
  71.9 1.0 slice.106
  72.9 1.6 collective-permute-start.7
  75.1 0.6 pad.5.refs_11_
  75.7 1.1 pad_maximum_fusion.refs_10_.refs_7_
  76.9 10.3 %collective-permute-done.7.refs_8_.refs_5_ = bf16[384,384]{1,0:T(8,128)(2,1)S(1)} collective-permute-done((bf16[384,384]{1,0:T(8,128)(2,1)S(1)}, bf16[384,384]{1,0:T(8,128)(2,1)S(1)}, u32[]{:S(2)}, u32[]{:S(2)}) %collective-permute-start.7) | collective-permute-done | bytes 294944 | tf_op jit(solution)/shard_map/ppermute | solution.py:441
  87.2 1.9 %collective-permute-start.12 = (bf16[384,768]{1,0:T(8,128)(2,1)S(1)}, bf16[384,768]{1,0:T(8,128)(2,1)S(1)}, u32[]{:S(2)}, u32[]{:S(2)}) collective-permute-start(bf16[384,768]{1,0:T(8,128)(2,1)S(1)} %pad_maximum_fusion.2.refs_4_.refs_1_), channel_id=1, source_target_pairs={{0,4},{1,5},{2,6},{3,7},{4,0},{5,1},{6,2},{7,3},{8,12},{9,13},{10,... | collective-permute-start | bytes 1769480 | tf_op jit(solution)/shard_map/ppermute | solution.py:441
  89.1 0.8 collective-permute-start.11
  89.9 14.8 %group.4 = (bf16[768,512]{1,0:T(8,128)(2,1)}, f32[3,3,8,256]{3,2,1,0:T(8,128)}, bf16[768,1536]{1,0:T(8,128)(2,1)}, bf16[16,1536]{1,0:T(8,128)(2,1)}) custom-call(s32[16]{0:T(128)} %fusion.32.refs_0_, s32[1]{0:T(128)S(6)} %mul.113.refs_1_, s32[4]{0:T(128)} %refs_2_.3, s32[2]{0:T(128)} %pad_add_fusion.1.refs_3_, bf16[384,896]{1,0:T(8,128)(2,1)} %copy-done, ...), custom_call_target="tpu_custom_call" | custom-call | flops 11000000512 | bytes 100000 | tf_op jit(solution)/shard_map/group/pallas_call | solution.py:320
  104.9 1.3 collective-permute-start.14
  106.2 0.7 collective-permute-start.13
  106.9 11.9 %group.5 = (bf16[768,512]{1,0:T(8,128)(2,1)}, bf16[768,1536]{1,0:T(8,128)(2,1)}) custom-call(s32[16]{0:T(128)} %fusion.32.refs_0_, bf16[384,896]{1,0:T(8,128)(2,1)} %copy-done, bf16[384,896]{1,0:T(8,128)(2,1)} %copy-done.3, bf16[384,896]{1,0:T(8,128)(2,1)} %collective-permute-done.5.refs_6_.refs_3_, bf16[384,512]{1,0:T(8,128)(2,1)} %collective-permute-done.6.refs_7_.refs_4_, ...), custom_call_target="tpu_custom_call" | custom-call | flops 11000000512 | bytes 100000 | tf_op jit(solution)/shard_map/group/pallas_call | solution.py:320
  118.9 0.7 copy-done.14
  119.7 13.5 %group.6 = (bf16[768,512]{1,0:T(8,128)(2,1)}, f32[3,3,8,256]{3,2,1,0:T(8,128)}) custom-call(s32[16]{0:T(128)} %fusion.32.refs_0_, s32[1]{0:T(128)S(6)} %add.88.refs_1_, s32[4]{0:T(128)} %refs_2_.3, s32[2]{0:T(128)} %pad_add_fusion.1.refs_3_, bf16[384,768]{1,0:T(8,128)(2,1)} %copy-done.1, bf16[384,768]{1,0:T(8,128)(2,1)} %copy-done.5, ...), custom_call_target="tpu_custom_call" | custom-call | flops 11000000512 | bytes 100000 | tf_op jit(solution)/shard_map/group/pallas_call | solution.py:320
  133.2 0.9 constant_dynamic-update-slice_fusion
  134.1 2.0 %collective-permute-start.17 = (f32[3,3,8,512]{3,2,1,0:T(8,128)S(1)}, f32[3,3,8,512]{3,2,1,0:T(8,128)S(1)}, u32[]{:S(2)}, u32[]{:S(2)}) collective-permute-start(f32[3,3,8,512]{3,2,1,0:T(8,128)S(1)} %constant_dynamic-update-slice_fusion), channel_id=1, source_target_pairs={{0,2},{1,3},{2,0},{3,1},{4,6},{5,7},{6,4},{7,5},{8,10},{9,11},{10,... | collective-permute-start | bytes 442376 | tf_op jit(solution)/shard_map/ppermute | solution.py:441
  136.3 1.3 collective-permute-start.19
  137.6 10.6 %group.7.rest_2_ = bf16[768,512]{1,0:T(8,128)(2,1)} custom-call(s32[16]{0:T(128)} %fusion.32.refs_0_, bf16[384,768]{1,0:T(8,128)(2,1)} %copy-done.1, bf16[384,768]{1,0:T(8,128)(2,1)} %copy-done.5, bf16[384,768]{1,0:T(8,128)(2,1)} %copy-done.4, bf16[384,384]{1,0:T(8,128)(2,1)} %copy-done.15, bf16[384,384]{1,0:T(8,128)(2,1)} %copy-done.14, ...), custom_call_target="tpu_custom_call" | custom-call | flops 11000000512 | bytes 100000 | tf_op jit(solution)/shard_map/group/pallas_call | solution.py:320
  149.4 0.6 pad_add_fusion.core_ref
  151.6 10.3 %output.1 = (bf16[768,1536]{1,0:T(8,128)(2,1)}, bf16[4,1536]{1,0:T(4,128)(2,1)}) custom-call(s32[2]{0:T(128)} %pad_add_fusion.core_ref, s32[16]{0:T(128)} %iota_multiply_fusion.offs_ref, bf16[1536,1536]{1,0:T(8,128)(2,1)} %all-gather.2.cloned.1.call-done.rest_0_, bf16[768,512]{1,0:T(8,128)(2,1)} %get-tuple-element.26.rest_1_, ...), custom_call_target="tpu_custom_call" | custom-call | flops 9900000256 | bytes 100000 | tf_op jit(solution)/shard_map/output/pallas_call | solution.py:414
  (95 shorter events, 6.8 us)
Async XLA Ops:
  7.2 2.9 %copy-start.9 = (bf16[48]{0:T(256)(128)(2,1)S(1)}, bf16[48]{0:T(256)(128)(2,1)}, u32[]{:S(2)}) copy-start(bf16[48]{0:T(256)(128)(2,1)} %param.10) | copy-start | bytes 292
  7.2 143.4 %all-gather.2.cloned.1.call-start = ((), (), s32[]{:S(2)}) async-start(), calls=%async_computation | async-start | bytes 4866048 | tf_op jit(solution)/shard_map/all_gather | solution.py:496
  10.1 1.5 collective-permute-start
  11.7 78.2 %collective-permute-start.10 = (bf16[4,512,768]{2,1,0:T(8,128)(2,1)}, bf16[4,512,768]{2,1,0:T(8,128)(2,1)}, u32[]{:S(2)}, u32[]{:S(2)}) collective-permute-start(bf16[4,512,768]{2,1,0:T(8,128)(2,1)} %refs_14_.3), channel_id=1, source_target_pairs={{0,1},{1,0},{2,3},{3,2},{4,5},{5,4},{6,7},{7,6},{8,9},{9,8},{10,11... | collective-permute-start | bytes 9437192 | tf_op jit(solution)/shard_map/ppermute | solution.py:441
  12.0 77.9 %collective-permute-start.9 = (bf16[4,512,768]{2,1,0:T(8,128)(2,1)}, bf16[4,512,768]{2,1,0:T(8,128)(2,1)}, u32[]{:S(2)}, u32[]{:S(2)}) collective-permute-start(bf16[4,512,768]{2,1,0:T(8,128)(2,1)} %refs_13_.3), channel_id=1, source_target_pairs={{0,1},{1,0},{2,3},{3,2},{4,5},{5,4},{6,7},{7,6},{8,9},{9,8},{10,11... | collective-permute-start | bytes 9437192 | tf_op jit(solution)/shard_map/ppermute | solution.py:441
  12.2 77.7 %collective-permute-start.8 = (bf16[768,1536]{1,0:T(8,128)(2,1)}, bf16[768,1536]{1,0:T(8,128)(2,1)}, u32[]{:S(2)}, u32[]{:S(2)}) collective-permute-start(bf16[768,1536]{1,0:T(8,128)(2,1)} %refs_6_), channel_id=1, source_target_pairs={{0,1},{1,0},{2,3},{3,2},{4,5},{5,4},{6,7},{7,6},{8,9},{9,8},{10,11... | collective-permute-start | bytes 7077896 | tf_op jit(solution)/shard_map/ppermute | solution.py:441
  12.7 13.8 %collective-permute-start.1 = (bf16[96,1664]{1,0:T(8,128)(2,1)S(1)}, bf16[96,1664]{1,0:T(8,128)(2,1)S(1)}, u32[]{:S(2)}, u32[]{:S(2)}) collective-permute-start(bf16[96,1664]{1,0:T(8,128)(2,1)S(1)} %pad_maximum_fusion.4), channel_id=1, source_target_pairs={{8,0},{16,8},{24,16},{0,24},{9,1},{17,9},{25,17},{1,25},{10,2},{18... | collective-permute-start | bytes 958472 | tf_op jit(solution)/shard_map/ppermute | solution.py:451
  17.6 30.9 %collective-permute-start.2 = (bf16[96,1664]{1,0:T(8,128)(2,1)S(1)}, bf16[96,1664]{1,0:T(8,128)(2,1)S(1)}, u32[]{:S(2)}, u32[]{:S(2)}) collective-permute-start(bf16[96,1664]{1,0:T(8,128)(2,1)S(1)} %pad_maximum_fusion.4), channel_id=1, source_target_pairs={{16,0},{24,8},{0,16},{8,24},{17,1},{25,9},{1,17},{9,25},{18,2},{26... | collective-permute-start | bytes 958472 | tf_op jit(solution)/shard_map/ppermute | solution.py:451
  26.6 22.0 %collective-permute-start.3 = (bf16[96,1664]{1,0:T(8,128)(2,1)S(1)}, bf16[96,1664]{1,0:T(8,128)(2,1)S(1)}, u32[]{:S(2)}, u32[]{:S(2)}) collective-permute-start(bf16[96,1664]{1,0:T(8,128)(2,1)S(1)} %pad_maximum_fusion.4), channel_id=1, source_target_pairs={{24,0},{0,8},{8,16},{16,24},{25,1},{1,9},{9,17},{17,25},{26,2},{2,... | collective-permute-start | bytes 958472 | tf_op jit(solution)/shard_map/ppermute | solution.py:451
  26.6 23.6 %copy-start.16 = (s32[4]{0:T(128)S(1)}, s32[4]{0:T(128)}, u32[]{:S(2)}) copy-start(s32[4]{0:T(128)} %refs_2_.3) | copy-start | bytes 52
  26.6 25.3 %copy-start.7 = (f32[3,16,192]{2,1,0:T(8,128)S(1)}, f32[3,16,192]{2,1,0:T(8,128)}, u32[]{:S(2)}) copy-start(f32[3,16,192]{2,1,0:T(8,128)} %constant.116.clone.1) | copy-start | bytes 110596
  48.6 24.3 %copy-start = (bf16[384,896]{1,0:T(8,128)(2,1)}, bf16[384,896]{1,0:T(8,128)(2,1)S(1)}, u32[]{:S(2)}) copy-start(bf16[384,896]{1,0:T(8,128)(2,1)S(1)} %pad_maximum_fusion.1.refs_4_.refs_1_) | copy-start | bytes 2064388
  48.6 21.1 %collective-permute-start.4 = (bf16[384,896]{1,0:T(8,128)(2,1)S(1)}, bf16[384,896]{1,0:T(8,128)(2,1)S(1)}, u32[]{:S(2)}, u32[]{:S(2)}) collective-permute-start(bf16[384,896]{1,0:T(8,128)(2,1)S(1)} %pad_maximum_fusion.1.refs_4_.refs_1_), channel_id=1, source_target_pairs={{0,2},{1,3},{2,0},{3,1},{4,6},{5,7},{6,4},{7,5},{8,10},{9,11},{10,... | collective-permute-start | bytes 2064392 | tf_op jit(solution)/shard_map/ppermute | solution.py:441
  50.2 21.7 %collective-permute-start.5 = (bf16[384,896]{1,0:T(8,128)(2,1)S(1)}, bf16[384,896]{1,0:T(8,128)(2,1)}, u32[]{:S(2)}, u32[]{:S(2)}) collective-permute-start(bf16[384,896]{1,0:T(8,128)(2,1)S(1)} %pad_maximum_fusion.1.refs_4_.refs_1_), channel_id=1, source_target_pairs={{0,4},{1,5},{2,6},{3,7},{4,0},{5,1},{6,2},{7,3},{8,12},{9,13},{10,... | collective-permute-start | bytes 2064392 | tf_op jit(solution)/shard_map/ppermute | solution.py:441
  51.9 23.1 %copy-start.8 = (bf16[4,1536]{1,0:T(4,128)(2,1)S(1)}, bf16[4,1536]{1,0:T(4,128)(2,1)}, u32[]{:S(2)}) copy-start(bf16[4,1536]{1,0:T(4,128)(2,1)} %param.9) | copy-start | bytes 36868
  69.8 17.4 %collective-permute-start.6 = (bf16[384,512]{1,0:T(8,128)(2,1)S(1)}, bf16[384,512]{1,0:T(8,128)(2,1)}, u32[]{:S(2)}, u32[]{:S(2)}) collective-permute-start(bf16[384,512]{1,0:T(8,128)(2,1)S(1)} %slice.105), channel_id=1, source_target_pairs={{0,4},{1,5},{2,6},{3,7},{4,0},{5,1},{6,2},{7,3},{8,12},{9,13},{10,... | collective-permute-start | bytes 1179656 | tf_op jit(solution)/shard_map/ppermute | solution.py:441
  72.9 14.3 %collective-permute-start.7 = (bf16[384,384]{1,0:T(8,128)(2,1)S(1)}, bf16[384,384]{1,0:T(8,128)(2,1)S(1)}, u32[]{:S(2)}, u32[]{:S(2)}) collective-permute-start(bf16[384,384]{1,0:T(8,128)(2,1)S(1)} %slice.106), channel_id=1, source_target_pairs={{0,2},{1,3},{2,0},{3,1},{4,6},{5,7},{6,4},{7,5},{8,10},{9,11},{10,... | collective-permute-start | bytes 884744 | tf_op jit(solution)/shard_map/ppermute | solution.py:441
  76.9 27.8 %copy-start.1 = (bf16[384,768]{1,0:T(8,128)(2,1)}, bf16[384,768]{1,0:T(8,128)(2,1)S(1)}, u32[]{:S(2)}) copy-start(bf16[384,768]{1,0:T(8,128)(2,1)S(1)} %pad_maximum_fusion.2.refs_4_.refs_1_) | copy-start | bytes 1769476
  87.2 2.7 %copy-start.13 = (bf16[384,384]{1,0:T(8,128)(2,1)}, bf16[384,384]{1,0:T(8,128)(2,1)S(1)}, u32[]{:S(2)}) copy-start(bf16[384,384]{1,0:T(8,128)(2,1)S(1)} %collective-permute-done.7.refs_8_.refs_5_) | copy-start | bytes 884740
  87.2 17.6 %collective-permute-start.12 = (bf16[384,768]{1,0:T(8,128)(2,1)S(1)}, bf16[384,768]{1,0:T(8,128)(2,1)S(1)}, u32[]{:S(2)}, u32[]{:S(2)}) collective-permute-start(bf16[384,768]{1,0:T(8,128)(2,1)S(1)} %pad_maximum_fusion.2.refs_4_.refs_1_), channel_id=1, source_target_pairs={{0,4},{1,5},{2,6},{3,7},{4,0},{5,1},{6,2},{7,3},{8,12},{9,13},{10,... | collective-permute-start | bytes 1769480 | tf_op jit(solution)/shard_map/ppermute | solution.py:441
  89.1 17.1 %collective-permute-start.11 = (bf16[384,768]{1,0:T(8,128)(2,1)S(1)}, bf16[384,768]{1,0:T(8,128)(2,1)S(1)}, u32[]{:S(2)}, u32[]{:S(2)}) collective-permute-start(bf16[384,768]{1,0:T(8,128)(2,1)S(1)} %pad_maximum_fusion.2.refs_4_.refs_1_), channel_id=1, source_target_pairs={{0,2},{1,3},{2,0},{3,1},{4,6},{5,7},{6,4},{7,5},{8,10},{9,11},{10,... | collective-permute-start | bytes 1769480 | tf_op jit(solution)/shard_map/ppermute | solution.py:441
  104.7 45.3 %collective-permute-start.15 = (bf16[768,512]{1,0:T(8,128)(2,1)}, bf16[768,512]{1,0:T(8,128)(2,1)S(1)}, u32[]{:S(2)}, u32[]{:S(2)}) collective-permute-start(bf16[768,512]{1,0:T(8,128)(2,1)} %get-tuple-element.24), channel_id=1, source_target_pairs={{0,1},{1,0},{2,3},{3,2},{4,5},{5,4},{6,7},{7,6},{8,9},{9,8},{10,11... | collective-permute-start | bytes 2359304 | tf_op jit(solution)/shard_map/ppermute | solution.py:441
  104.8 14.0 %copy-start.4 = (bf16[384,768]{1,0:T(8,128)(2,1)}, bf16[384,768]{1,0:T(8,128)(2,1)S(1)}, u32[]{:S(2)}) copy-start(bf16[384,768]{1,0:T(8,128)(2,1)S(1)} %collective-permute-done.12.refs_6_.refs_3_) | copy-start | bytes 1769476
  104.9 14.0 %collective-permute-start.14 = (bf16[384,384]{1,0:T(8,128)(2,1)S(1)}, bf16[384,384]{1,0:T(8,128)(2,1)S(1)}, u32[]{:S(2)}, u32[]{:S(2)}) collective-permute-start(bf16[384,384]{1,0:T(8,128)(2,1)S(1)} %slice.99), channel_id=1, source_target_pairs={{0,2},{1,3},{2,0},{3,1},{4,6},{5,7},{6,4},{7,5},{8,10},{9,11},{10,... | collective-permute-start | bytes 884744 | tf_op jit(solution)/shard_map/ppermute | solution.py:441
  106.2 12.6 %copy-start.5 = (bf16[384,768]{1,0:T(8,128)(2,1)}, bf16[384,768]{1,0:T(8,128)(2,1)S(1)}, u32[]{:S(2)}) copy-start(bf16[384,768]{1,0:T(8,128)(2,1)S(1)} %collective-permute-done.11.refs_5_.refs_2_) | copy-start | bytes 1769476
  106.2 12.6 %copy-start.6 = (f32[3,3,8,256]{3,2,1,0:T(8,128)S(1)}, f32[3,3,8,256]{3,2,1,0:T(8,128)}, u32[]{:S(2)}) copy-start(f32[3,3,8,256]{3,2,1,0:T(8,128)} %get-tuple-element.37) | copy-start | bytes 221188
  106.2 12.6 %collective-permute-start.13 = (bf16[384,384]{1,0:T(8,128)(2,1)S(1)}, bf16[384,384]{1,0:T(8,128)(2,1)S(1)}, u32[]{:S(2)}, u32[]{:S(2)}) collective-permute-start(bf16[384,384]{1,0:T(8,128)(2,1)S(1)} %slice.98), channel_id=1, source_target_pairs={{0,4},{1,5},{2,6},{3,7},{4,0},{5,1},{6,2},{7,3},{8,12},{9,13},{10,... | collective-permute-start | bytes 884744 | tf_op jit(solution)/shard_map/ppermute | solution.py:441
  134.1 14.2 %collective-permute-start.17 = (f32[3,3,8,512]{3,2,1,0:T(8,128)S(1)}, f32[3,3,8,512]{3,2,1,0:T(8,128)S(1)}, u32[]{:S(2)}, u32[]{:S(2)}) collective-permute-start(f32[3,3,8,512]{3,2,1,0:T(8,128)S(1)} %constant_dynamic-update-slice_fusion), channel_id=1, source_target_pairs={{0,2},{1,3},{2,0},{3,1},{4,6},{5,7},{6,4},{7,5},{8,10},{9,11},{10,... | collective-permute-start | bytes 442376 | tf_op jit(solution)/shard_map/ppermute | solution.py:441
  136.1 12.2 %collective-permute-start.18 = (f32[3,3,8,512]{3,2,1,0:T(8,128)S(1)}, f32[3,3,8,512]{3,2,1,0:T(8,128)S(1)}, u32[]{:S(2)}, u32[]{:S(2)}) collective-permute-start(f32[3,3,8,512]{3,2,1,0:T(8,128)S(1)} %constant_dynamic-update-slice_fusion), channel_id=1, source_target_pairs={{0,4},{1,5},{2,6},{3,7},{4,0},{5,1},{6,2},{7,3},{8,12},{9,13},{10,... | collective-permute-start | bytes 442376 | tf_op jit(solution)/shard_map/ppermute | solution.py:441
  136.3 12.0 %collective-permute-start.19 = (f32[3,3,8,512]{3,2,1,0:T(8,128)S(1)}, f32[3,3,8,512]{3,2,1,0:T(8,128)S(1)}, u32[]{:S(2)}, u32[]{:S(2)}) collective-permute-start(f32[3,3,8,512]{3,2,1,0:T(8,128)S(1)} %constant_dynamic-update-slice_fusion), channel_id=1, source_target_pairs={{0,6},{1,7},{2,4},{3,5},{4,2},{5,3},{6,0},{7,1},{8,14},{9,15},{10,... | collective-permute-start | bytes 442376 | tf_op jit(solution)/shard_map/ppermute | solution.py:441
  137.6 12.9 %collective-permute-start.16 = (bf16[768,512]{1,0:T(8,128)(2,1)}, bf16[768,512]{1,0:T(8,128)(2,1)S(1)}, u32[]{:S(2)}, u32[]{:S(2)}) collective-permute-start(bf16[768,512]{1,0:T(8,128)(2,1)} %get-tuple-element.35), channel_id=1, source_target_pairs={{0,1},{1,0},{2,3},{3,2},{4,5},{5,4},{6,7},{7,6},{8,9},{9,8},{10,11... | collective-permute-start | bytes 2359304 | tf_op jit(solution)/shard_map/ppermute | solution.py:441
  148.3 2.2 %collective-permute-start.20 = (f32[4,3,3,8,512]{4,3,2,1,0:T(8,128)S(1)}, f32[4,3,3,8,512]{4,3,2,1,0:T(8,128)S(1)}, u32[]{:S(2)}, u32[]{:S(2)}) collective-permute-start(f32[4,3,3,8,512]{4,3,2,1,0:T(8,128)S(1)} %pad_maximum_fusion.3.rest_5_), channel_id=1, source_target_pairs={{0,1},{1,0},{2,3},{3,2},{4,5},{5,4},{6,7},{7,6},{8,9},{9,8},{10,11... | collective-permute-start | bytes 1769480 | tf_op jit(solution)/shard_map/ppermute | solution.py:441
  (7 other events, 8.2 us)
Sparse Core Ops, SparseCore 0:
  10.9 88.1 all-gather.1

commit v4 on v3

--- a/solution.py
+++ b/solution.py
@@ -324,7 +324,7 @@
         out_shape=out_shape,
         scratch_shapes=scratch,
         compiler_params=pltpu.CompilerParams(vmem_limit_bytes=VMEM_BYTES),
-        cost_estimate=cost(10 * stretches),
+        cost_estimate=cost(1),
         name="group",
     )(*operands)
 
@@ -432,7 +432,7 @@
         compiler_params=pltpu.CompilerParams(
             dimension_semantics=("arbitrary",), vmem_limit_bytes=VMEM_BYTES
         ),
-        cost_estimate=cost(9),
+        cost_estimate=cost(1),
         name="output",
     )(core, offs, *wo_pieces, *[piece[0] for piece in attended], parts, other_parts)
 
@@ -443,6 +443,22 @@
 
 def after(array, *others):
     return lax.optimization_barrier((array, *others))[0]
+
+
+def fence_kernel(operand_ref, token_ref):
+    token_ref[...] = jnp.zeros_like(token_ref)
+
+
+def fence(array):
+    token = pl.pallas_call(
+        fence_kernel,
+        in_specs=[pl.BlockSpec(memory_space=pl.ANY)],
+        out_specs=pl.BlockSpec(memory_space=pltpu.VMEM),
+        out_shape=jax.ShapeDtypeStruct((1, 1), BF16),
+        cost_estimate=cost(200),
+        name="fence",
+    )(array)
+    return token.reshape(())
 
 
 def along_dp(local, n_dp):
@@ -493,7 +509,6 @@
     head = LANES + width
     split = n_shard == 8 and block_rows == HALF
 
-    wo_all = lax.all_gather(wo, everyone, axis=0, tiled=True)
     wo_plan = [[(0, 0, 0, H)], [(0, width, 0, H)]]
     wo_offs = jnp.arange(H, dtype=jnp.int32) * LANES
     extra = 16
@@ -509,24 +524,26 @@
         mine = jnp.concatenate([gain_columns, jnp.where(first, low, high)], axis=1)
         theirs = jnp.concatenate([gain_columns, jnp.where(first, high, low)], axis=1)
         theirs = swap(theirs, 1, n_shard)
-        free = theirs
         pair = jnp.concatenate([jnp.where(first, mine, theirs), jnp.where(first, theirs, mine)], axis=0)
         order = jnp.arange(n_shard // 2 * n_dp, dtype=jnp.int32)
         chip = (me_dp + order % n_dp) % n_dp * (n_shard // 2) + (me // 2 ^ (order // n_dp))
         block_rows = 2 * block_rows
         offs = chip * block_rows
-        found = along_dp(pair, n_dp)
-        here = jnp.concatenate([block[:, :head] for block in found], axis=0)
+        sib_x, sib_k, sib_v = [swap(after(array, theirs), 1, n_shard) for array in (prefill_x, k_cache, v_cache)]
+        here = jnp.concatenate(along_dp(pair[:, :head], n_dp), axis=0)
+        here = after(here, sib_x, sib_k, sib_v, tables, dtable, dx)
         beside, above = swap(here, 2, n_shard), swap(here, 4, n_shard)
-        pieces = pieces_of(here, beside, above, LANES + half, n_shard)
+        wo = after(wo, here)
+        later = after(pair[:, head:], here)
+        found = along_dp(later, n_dp)
+        later_here = jnp.concatenate(found, axis=0) + fence(later)
+        pieces = pieces_of(here, after(beside, later_here), after(above, later_here), LANES + half, n_shard)
         plan = lay_out(pieces, {LANES: 0, LANES + half: 1, 0: 2}, n_dp)
         pieces = [piece[0] for piece in pieces]
-        found[0] = after(found[0], beside)
-        later_here = jnp.concatenate([block[:, head:] for block in found], axis=0)
         later_here = after(later_here, *pieces)
         beside, above = swap(later_here, 2, n_shard), swap(later_here, 4, n_shard)
     else:
-        free = norm_gain
+        sib_x, sib_k, sib_v = [swap(array, 1, n_shard) for array in (prefill_x, k_cache, v_cache)]
         offs = jnp.zeros((1,), jnp.int32)
         every = lax.all_gather(jnp.concatenate([gain_columns, low, high], axis=1), everyone, axis=0, tiled=True)
         block_rows = every.shape[0]
@@ -534,7 +551,7 @@
         pieces = [jnp.concatenate([every[:, :LANES], chosen[:, :width]], axis=1)]
         plan = [[(0, LANES, 0, 1)], [(0, LANES + half, 0, 1)], [(0, 0, 0, 1)]]
 
-    sib_x, sib_k, sib_v = [swap(after(array, free), 1, n_shard) for array in (prefill_x, k_cache, v_cache)]
+    wo_all = lax.all_gather(wo, everyone, axis=0, tiled=True)
     lane = core.astype(jnp.int32).reshape(1) * half
     starts = jnp.stack([me * span, (me ^ 1) * span]).astype(jnp.int32)
     caches = [k_cache, v_cache, sib_k, sib_v]

time: 169 us -> 153 us (0.905)
  waiting for transfers between devices: 58.8 us -> 34.7 us
  other arithmetic: 6.14 us -> 9.63 us
  starting transfers between devices: 21.5 us -> 24.6 us
    ppermute x18, waiting for transfers between devices: 27.4 us -> 13.7 us  [swap(): return lax.ppermute(array, 'shard', [(i, i ^ mask) for i in range(n_shard)])]
    ppermute x3 -> x6, waiting for transfers between devices: 30.8 us -> 20.9 us  [along_dp(): lax.ppermute(local, 'dp', [((i + shift) % n_dp, i) for i in range(n_dp)])]
    ppermute x3 -> x6, starting transfers between devices: 4.87 us -> 9.79 us  [along_dp(): lax.ppermute(local, 'dp', [((i + shift) % n_dp, i) for i in range(n_dp)])]
    add x0 -> x1, other arithmetic: none -> 1.77 us  [per_device(): later_here = jnp.concatenate(found, axis=0) + fence(later)]
    ppermute x18, starting transfers between devices: 16.5 us -> 14.8 us  [swap(): return lax.ppermute(array, 'shard', [(i, i ^ mask) for i in range(n_shard)])]
  transfers between devices with their start and end apart: 22 -> 25, of which waited for: 6 -> 10; matrix products, arithmetic and copies ran while one was open for 6% -> 9% of each run, Pallas kernels for 30% -> 34%
where the time goes in v4:
time: 153 us
  Pallas kernels  61.7 us (40%)
  waiting for transfers between devices  34.7 us (23%)
  starting transfers between devices  24.6 us (16%)
  between operations  14.5 us (9%)
  other arithmetic  9.63 us (6%)
  local copies, waits for them, and re-layouts  7.62 us (5%)
    pallas_call x4, Pallas kernels, run_group(): pl.pallas_call(functools.partial(group_kernel, block_rows, plan, norm, of...  50.9 us
    ppermute x6, waiting for transfers between devices, along_dp(): lax.ppermute(local, 'dp', [((i + shift) % n_dp, i) for i in range(n_dp)])  20.9 us
    ppermute x18, starting transfers between devices, swap(): return lax.ppermute(array, 'shard', [(i, i ^ mask) for i in range(n_shard)])  14.8 us
    ppermute x18, waiting for transfers between devices, swap(): return lax.ppermute(array, 'shard', [(i, i ^ mask) for i in range(n_shard)])  13.7 us
    pallas_call x1, Pallas kernels, output(): pl.pallas_call(functools.partial(output_kernel, requests, block_rows, pla...  10.3 us
    ppermute x6, starting transfers between devices, along_dp(): lax.ppermute(local, 'dp', [((i + shift) % n_dp, i) for i in range(n_dp)])  9.79 us
  transfers between devices with their start and end apart: 25, of which 10 were waited for; matrix products, arithmetic and copies ran while one was open for 9% of the time, Pallas kernels for 34%

profile of v4, /device:TPU:0, one launch (start us, length us, event | category | flops | bytes accessed | tf_op | source)
XLA Modules:
  0.0 152.7 jit_solution(17627524973697982896)
XLA Ops:
  7.2 1.0 fusion.34
  10.0 1.0 collective-permute-done
  12.0 1.5 fusion.3
  13.6 4.8 %collective-permute-start.1 = (bf16[96,896]{1,0:T(8,128)(2,1)S(1)}, bf16[96,896]{1,0:T(8,128)(2,1)S(1)}, u32[]{:S(2)}, u32[]{:S(2)}) collective-permute-start(bf16[96,896]{1,0:T(8,128)(2,1)S(1)} %fusion.4), channel_id=1, source_target_pairs={{8,0},{16,8},{24,16},{0,24},{9,1},{17,9},{25,17},{1,25},{10,2},{18... | collective-permute-start | bytes 516104 | tf_op jit(solution)/shard_map/ppermute | solution.py:467
  18.6 1.1 pad_maximum_fusion.refs_10_.refs_7_
  19.7 3.5 %collective-permute-done.1 = bf16[96,896]{1,0:T(8,128)(2,1)S(1)} collective-permute-done((bf16[96,896]{1,0:T(8,128)(2,1)S(1)}, bf16[96,896]{1,0:T(8,128)(2,1)S(1)}, u32[]{:S(2)}, u32[]{:S(2)}) %collective-permute-start.1) | collective-permute-done | bytes 172064 | tf_op jit(solution)/shard_map/ppermute | solution.py:467
  25.2 8.9 %collective-permute-done.2 = bf16[96,896]{1,0:T(8,128)(2,1)S(1)} collective-permute-done((bf16[96,896]{1,0:T(8,128)(2,1)S(1)}, bf16[96,896]{1,0:T(8,128)(2,1)S(1)}, u32[]{:S(2)}, u32[]{:S(2)}) %collective-permute-start.2) | collective-permute-done | bytes 172064 | tf_op jit(solution)/shard_map/ppermute | solution.py:467
  34.2 0.9 pad_maximum_fusion.1.refs_4_.refs_1_
  35.1 1.0 collective-permute-start.10
  36.1 2.8 %collective-permute-start.8 = (bf16[96,768]{1,0:T(8,128)(2,1)}, bf16[96,768]{1,0:T(8,128)(2,1)}, u32[]{:S(2)}, u32[]{:S(2)}) collective-permute-start(bf16[96,768]{1,0:T(8,128)(2,1)} %pad_maximum_fusion.5.operand_ref), channel_id=1, source_target_pairs={{8,0},{16,8},{24,16},{0,24},{9,1},{17,9},{25,17},{1,25},{10,2},{18... | collective-permute-start | bytes 442376 | tf_op jit(solution)/shard_map/ppermute | solution.py:467
  39.0 1.1 collective-permute-start.9
  40.1 1.5 collective-permute-start.11
  41.6 1.5 collective-permute-start.7
  44.0 1.8 %collective-permute-done.8 = bf16[96,768]{1,0:T(8,128)(2,1)} collective-permute-done((bf16[96,768]{1,0:T(8,128)(2,1)}, bf16[96,768]{1,0:T(8,128)(2,1)}, u32[]{:S(2)}, u32[]{:S(2)}) %collective-permute-start.8) | collective-permute-done | bytes 147488 | tf_op jit(solution)/shard_map/ppermute | solution.py:467
  45.8 6.3 %collective-permute-done.9 = bf16[96,768]{1,0:T(8,128)(2,1)} collective-permute-done((bf16[96,768]{1,0:T(8,128)(2,1)}, bf16[96,768]{1,0:T(8,128)(2,1)}, u32[]{:S(2)}, u32[]{:S(2)}) %collective-permute-start.9) | collective-permute-done | bytes 147488 | tf_op jit(solution)/shard_map/ppermute | solution.py:467
  52.1 1.8 %maximum_add_fusion.refs_4_.refs_1_ = bf16[384,768]{1,0:T(8,128)(2,1)S(1)} fusion(bf16[96,768]{1,0:T(8,128)(2,1)} %collective-permute-done.10, bf16[96,768]{1,0:T(8,128)(2,1)} %collective-permute-done.9, bf16[96,768]{1,0:T(8,128)(2,1)} %collective-permute-done.8, bf16[96,768]{1,0:T(8,128)(2,1)} %pad_maximum_fusion.5.operand_ref, bf16[]{:T(256)} %bitcast.2), kind=kLoop, calls=%fused_computation.2 | loop fusion | flops 2949120 | bytes 1179650 | tf_op jit(solution)/shard_map/add | solution.py:539
  53.9 5.3 %collective-permute-done.7.refs_5_.refs_2_ = bf16[384,896]{1,0:T(8,128)(2,1)} collective-permute-done((bf16[384,896]{1,0:T(8,128)(2,1)}, bf16[384,896]{1,0:T(8,128)(2,1)}, u32[]{:S(2)}, u32[]{:S(2)}) %collective-permute-start.7) | collective-permute-done | bytes 688160 | tf_op jit(solution)/shard_map/ppermute | solution.py:441
  59.2 1.0 slice.72
  60.8 1.0 slice.73
  61.8 1.6 %collective-permute-start.13 = (bf16[384,384]{1,0:T(8,128)(2,1)S(1)}, bf16[384,384]{1,0:T(8,128)(2,1)S(1)}, u32[]{:S(2)}, u32[]{:S(2)}) collective-permute-start(bf16[384,384]{1,0:T(8,128)(2,1)S(1)} %slice.73), channel_id=1, source_target_pairs={{0,2},{1,3},{2,0},{3,1},{4,6},{5,7},{6,4},{7,5},{8,10},{9,11},{10,... | collective-permute-start | bytes 884744 | tf_op jit(solution)/shard_map/ppermute | solution.py:441
  63.4 5.8 %collective-permute-done.13.refs_8_.refs_5_ = bf16[384,384]{1,0:T(8,128)(2,1)S(1)} collective-permute-done((bf16[384,384]{1,0:T(8,128)(2,1)S(1)}, bf16[384,384]{1,0:T(8,128)(2,1)S(1)}, u32[]{:S(2)}, u32[]{:S(2)}) %collective-permute-start.13) | collective-permute-done | bytes 294944 | tf_op jit(solution)/shard_map/ppermute | solution.py:441
  70.1 1.0 collective-permute-start.15
  71.1 1.7 %collective-permute-start.14 = (bf16[384,768]{1,0:T(8,128)(2,1)S(1)}, bf16[384,768]{1,0:T(8,128)(2,1)S(1)}, u32[]{:S(2)}, u32[]{:S(2)}) collective-permute-start(bf16[384,768]{1,0:T(8,128)(2,1)S(1)} %maximum_add_fusion.refs_4_.refs_1_), channel_id=1, source_target_pairs={{0,2},{1,3},{2,0},{3,1},{4,6},{5,7},{6,4},{7,5},{8,10},{9,11},{10,... | collective-permute-start | bytes 1769480 | tf_op jit(solution)/shard_map/ppermute | solution.py:441
  74.0 14.7 %group.4 = (bf16[768,512]{1,0:T(8,128)(2,1)}, f32[3,3,8,256]{3,2,1,0:T(8,128)}, bf16[768,1536]{1,0:T(8,128)(2,1)}, bf16[16,1536]{1,0:T(8,128)(2,1)}) custom-call(s32[16]{0:T(128)} %fusion.32.refs_0_, s32[1]{0:T(128)S(6)} %mul.123.refs_1_, s32[4]{0:T(128)} %refs_2_.3, s32[2]{0:T(128)} %pad_add_fusion.1.refs_3_, ...), custom_call_target="tpu_custom_call" | custom-call | flops 1100000000 | bytes 100000 | tf_op jit(solution)/shard_map/group/pallas_call | solution.py:320
  89.2 1.1 collective-permute-start.16
  90.4 12.0 %group.5 = (bf16[768,512]{1,0:T(8,128)(2,1)}, bf16[768,1536]{1,0:T(8,128)(2,1)}) custom-call(s32[16]{0:T(128)} %fusion.32.refs_0_, bf16[384,896]{1,0:T(8,128)(2,1)} %pad_maximum_fusion.1.refs_4_.refs_1_, bf16[384,896]{1,0:T(8,128)(2,1)} %collective-permute-done.7.refs_5_.refs_2_, bf16[384,896]{1,0:T(8,128)(2,1)} %collective-permute-done.11.refs_6_.refs_3_, ...), custom_call_target="tpu_custom_call" | custom-call | flops 1100000000 | bytes 100000 | tf_op jit(solution)/shard_map/group/pallas_call | solution.py:320
  103.2 13.6 %group.6 = (bf16[768,512]{1,0:T(8,128)(2,1)}, f32[3,3,8,256]{3,2,1,0:T(8,128)}) custom-call(s32[16]{0:T(128)} %fusion.32.refs_0_, s32[1]{0:T(128)S(6)} %add.96.refs_1_, s32[4]{0:T(128)} %refs_2_.3, s32[2]{0:T(128)} %pad_add_fusion.1.refs_3_, bf16[384,768]{1,0:T(8,128)(2,1)} %copy-done, bf16[384,768]{1,0:T(8,128)(2,1)} %copy-done.2, ...), custom_call_target="tpu_custom_call" | custom-call | flops 1100000000 | bytes 100000 | tf_op jit(solution)/shard_map/group/pallas_call | solution.py:320
  116.8 0.9 constant_dynamic-update-slice_fusion
  117.7 1.6 %collective-permute-start.20 = (f32[3,3,8,512]{3,2,1,0:T(8,128)S(1)}, f32[3,3,8,512]{3,2,1,0:T(8,128)S(1)}, u32[]{:S(2)}, u32[]{:S(2)}) collective-permute-start(f32[3,3,8,512]{3,2,1,0:T(8,128)S(1)} %constant_dynamic-update-slice_fusion), channel_id=1, source_target_pairs={{0,2},{1,3},{2,0},{3,1},{4,6},{5,7},{6,4},{7,5},{8,10},{9,11},{10,... | collective-permute-start | bytes 442376 | tf_op jit(solution)/shard_map/ppermute | solution.py:441
  119.3 1.0 collective-permute-start.21
  121.7 10.6 %group.7.rest_2_ = bf16[768,512]{1,0:T(8,128)(2,1)} custom-call(s32[16]{0:T(128)} %fusion.32.refs_0_, bf16[384,768]{1,0:T(8,128)(2,1)} %copy-done, bf16[384,768]{1,0:T(8,128)(2,1)} %copy-done.2, bf16[384,768]{1,0:T(8,128)(2,1)} %copy-done.1, bf16[384,384]{1,0:T(8,128)(2,1)} %copy-done.7, bf16[384,384]{1,0:T(8,128)(2,1)} %copy-done.6, ...), custom_call_target="tpu_custom_call" | custom-call | flops 1100000000 | bytes 100000 | tf_op jit(solution)/shard_map/group/pallas_call | solution.py:320
  135.6 10.3 %output.1 = (bf16[768,1536]{1,0:T(8,128)(2,1)}, bf16[4,1536]{1,0:T(4,128)(2,1)}) custom-call(s32[2]{0:T(128)} %pad_add_fusion.core_ref, s32[16]{0:T(128)} %iota_multiply_fusion.offs_ref, bf16[1536,1536]{1,0:T(8,128)(2,1)} %all-gather.2.cloned.1.call-done.rest_0_, bf16[768,512]{1,0:T(8,128)(2,1)} %get-tuple-element.35.rest_1_, ...), custom_call_target="tpu_custom_call" | custom-call | flops 1100000000 | bytes 100000 | tf_op jit(solution)/shard_map/output/pallas_call | solution.py:414
  (95 shorter events, 14.4 us)
Async XLA Ops:
  7.2 127.3 %all-gather.2.cloned.1.call-start = ((), (), s32[]{:S(2)}) async-start(), calls=%async_computation | async-start | bytes 4866048 | tf_op jit(solution)/shard_map/all_gather | solution.py:554
  9.5 1.5 %collective-permute-start = (bf16[48,1664]{1,0:T(8,128)(2,1)S(1)}, bf16[48,1664]{1,0:T(8,128)(2,1)S(1)}, u32[]{:S(2)}, u32[]{:S(2)}) collective-permute-start(bf16[48,1664]{1,0:T(8,128)(2,1)S(1)} %pad_maximum_fusion.3), channel_id=1, source_target_pairs={{0,1},{1,0},{2,3},{3,2},{4,5},{5,4},{6,7},{7,6},{8,9},{9,8},{10,11... | collective-permute-start | bytes 479240 | tf_op jit(solution)/shard_map/ppermute | solution.py:441
  11.0 24.1 %collective-permute-start.5 = (bf16[4,512,768]{2,1,0:T(8,128)(2,1)}, bf16[4,512,768]{2,1,0:T(8,128)(2,1)}, u32[]{:S(2)}, u32[]{:S(2)}) collective-permute-start(bf16[4,512,768]{2,1,0:T(8,128)(2,1)} %refs_13_.3), channel_id=1, source_target_pairs={{0,1},{1,0},{2,3},{3,2},{4,5},{5,4},{6,7},{7,6},{8,9},{9,8},{10,11... | collective-permute-start | bytes 9437192 | tf_op jit(solution)/shard_map/ppermute | solution.py:441
  11.4 23.7 %collective-permute-start.6 = (bf16[4,512,768]{2,1,0:T(8,128)(2,1)}, bf16[4,512,768]{2,1,0:T(8,128)(2,1)}, u32[]{:S(2)}, u32[]{:S(2)}) collective-permute-start(bf16[4,512,768]{2,1,0:T(8,128)(2,1)} %refs_14_.3), channel_id=1, source_target_pairs={{0,1},{1,0},{2,3},{3,2},{4,5},{5,4},{6,7},{7,6},{8,9},{9,8},{10,11... | collective-permute-start | bytes 9437192 | tf_op jit(solution)/shard_map/ppermute | solution.py:441
  11.5 23.6 %collective-permute-start.4 = (bf16[768,1536]{1,0:T(8,128)(2,1)}, bf16[768,1536]{1,0:T(8,128)(2,1)}, u32[]{:S(2)}, u32[]{:S(2)}) collective-permute-start(bf16[768,1536]{1,0:T(8,128)(2,1)} %refs_6_), channel_id=1, source_target_pairs={{0,1},{1,0},{2,3},{3,2},{4,5},{5,4},{6,7},{7,6},{8,9},{9,8},{10,11... | collective-permute-start | bytes 7077896 | tf_op jit(solution)/shard_map/ppermute | solution.py:441
  13.6 9.6 %copy-start.12 = (f32[3,16,192]{2,1,0:T(8,128)S(1)}, f32[3,16,192]{2,1,0:T(8,128)}, u32[]{:S(2)}) copy-start(f32[3,16,192]{2,1,0:T(8,128)} %constant.109.clone.1) | copy-start | bytes 110596
  13.6 10.3 %copy-start.13 = (bf16[4,1536]{1,0:T(4,128)(2,1)S(1)}, bf16[4,1536]{1,0:T(4,128)(2,1)}, u32[]{:S(2)}) copy-start(bf16[4,1536]{1,0:T(4,128)(2,1)} %param.9) | copy-start | bytes 36868
  13.6 9.6 %collective-permute-start.1 = (bf16[96,896]{1,0:T(8,128)(2,1)S(1)}, bf16[96,896]{1,0:T(8,128)(2,1)S(1)}, u32[]{:S(2)}, u32[]{:S(2)}) collective-permute-start(bf16[96,896]{1,0:T(8,128)(2,1)S(1)} %fusion.4), channel_id=1, source_target_pairs={{8,0},{16,8},{24,16},{0,24},{9,1},{17,9},{25,17},{1,25},{10,2},{18... | collective-permute-start | bytes 516104 | tf_op jit(solution)/shard_map/ppermute | solution.py:467
  19.7 14.4 %collective-permute-start.2 = (bf16[96,896]{1,0:T(8,128)(2,1)S(1)}, bf16[96,896]{1,0:T(8,128)(2,1)S(1)}, u32[]{:S(2)}, u32[]{:S(2)}) collective-permute-start(bf16[96,896]{1,0:T(8,128)(2,1)S(1)} %fusion.4), channel_id=1, source_target_pairs={{16,0},{24,8},{0,16},{8,24},{17,1},{25,9},{1,17},{9,25},{18,2},{26... | collective-permute-start | bytes 516104 | tf_op jit(solution)/shard_map/ppermute | solution.py:467
  23.2 11.0 %collective-permute-start.3 = (bf16[96,896]{1,0:T(8,128)(2,1)S(1)}, bf16[96,896]{1,0:T(8,128)(2,1)S(1)}, u32[]{:S(2)}, u32[]{:S(2)}) collective-permute-start(bf16[96,896]{1,0:T(8,128)(2,1)S(1)} %fusion.4), channel_id=1, source_target_pairs={{24,0},{0,8},{8,16},{16,24},{25,1},{1,9},{9,17},{17,25},{26,2},{2,... | collective-permute-start | bytes 516104 | tf_op jit(solution)/shard_map/ppermute | solution.py:467
  35.1 8.9 %collective-permute-start.10 = (bf16[96,768]{1,0:T(8,128)(2,1)}, bf16[96,768]{1,0:T(8,128)(2,1)}, u32[]{:S(2)}, u32[]{:S(2)}) collective-permute-start(bf16[96,768]{1,0:T(8,128)(2,1)} %pad_maximum_fusion.5.operand_ref), channel_id=1, source_target_pairs={{24,0},{0,8},{8,16},{16,24},{25,1},{1,9},{9,17},{17,25},{26,2},{2,... | collective-permute-start | bytes 442376 | tf_op jit(solution)/shard_map/ppermute | solution.py:467
  36.1 9.7 %collective-permute-start.8 = (bf16[96,768]{1,0:T(8,128)(2,1)}, bf16[96,768]{1,0:T(8,128)(2,1)}, u32[]{:S(2)}, u32[]{:S(2)}) collective-permute-start(bf16[96,768]{1,0:T(8,128)(2,1)} %pad_maximum_fusion.5.operand_ref), channel_id=1, source_target_pairs={{8,0},{16,8},{24,16},{0,24},{9,1},{17,9},{25,17},{1,25},{10,2},{18... | collective-permute-start | bytes 442376 | tf_op jit(solution)/shard_map/ppermute | solution.py:467
  39.0 13.2 %collective-permute-start.9 = (bf16[96,768]{1,0:T(8,128)(2,1)}, bf16[96,768]{1,0:T(8,128)(2,1)}, u32[]{:S(2)}, u32[]{:S(2)}) collective-permute-start(bf16[96,768]{1,0:T(8,128)(2,1)} %pad_maximum_fusion.5.operand_ref), channel_id=1, source_target_pairs={{16,0},{24,8},{0,16},{8,24},{17,1},{25,9},{1,17},{9,25},{18,2},{26... | collective-permute-start | bytes 442376 | tf_op jit(solution)/shard_map/ppermute | solution.py:467
  40.1 20.7 %collective-permute-start.11 = (bf16[384,896]{1,0:T(8,128)(2,1)}, bf16[384,896]{1,0:T(8,128)(2,1)}, u32[]{:S(2)}, u32[]{:S(2)}) collective-permute-start(bf16[384,896]{1,0:T(8,128)(2,1)} %pad_maximum_fusion.1.refs_4_.refs_1_), channel_id=1, source_target_pairs={{0,4},{1,5},{2,6},{3,7},{4,0},{5,1},{6,2},{7,3},{8,12},{9,13},{10,... | collective-permute-start | bytes 2064392 | tf_op jit(solution)/shard_map/ppermute | solution.py:441
  41.6 17.6 %collective-permute-start.7 = (bf16[384,896]{1,0:T(8,128)(2,1)}, bf16[384,896]{1,0:T(8,128)(2,1)}, u32[]{:S(2)}, u32[]{:S(2)}) collective-permute-start(bf16[384,896]{1,0:T(8,128)(2,1)} %pad_maximum_fusion.1.refs_4_.refs_1_), channel_id=1, source_target_pairs={{0,2},{1,3},{2,0},{3,1},{4,6},{5,7},{6,4},{7,5},{8,10},{9,11},{10,... | collective-permute-start | bytes 2064392 | tf_op jit(solution)/shard_map/ppermute | solution.py:441
  53.9 34.8 %copy-start = (bf16[384,768]{1,0:T(8,128)(2,1)}, bf16[384,768]{1,0:T(8,128)(2,1)S(1)}, u32[]{:S(2)}) copy-start(bf16[384,768]{1,0:T(8,128)(2,1)S(1)} %maximum_add_fusion.refs_4_.refs_1_) | copy-start | bytes 1769476
  60.2 9.9 %collective-permute-start.12 = (bf16[384,512]{1,0:T(8,128)(2,1)S(1)}, bf16[384,512]{1,0:T(8,128)(2,1)S(1)}, u32[]{:S(2)}, u32[]{:S(2)}) collective-permute-start(bf16[384,512]{1,0:T(8,128)(2,1)S(1)} %slice.72), channel_id=1, source_target_pairs={{0,4},{1,5},{2,6},{3,7},{4,0},{5,1},{6,2},{7,3},{8,12},{9,13},{10,... | collective-permute-start | bytes 1179656 | tf_op jit(solution)/shard_map/ppermute | solution.py:441
  61.8 7.4 %collective-permute-start.13 = (bf16[384,384]{1,0:T(8,128)(2,1)S(1)}, bf16[384,384]{1,0:T(8,128)(2,1)S(1)}, u32[]{:S(2)}, u32[]{:S(2)}) collective-permute-start(bf16[384,384]{1,0:T(8,128)(2,1)S(1)} %slice.73), channel_id=1, source_target_pairs={{0,2},{1,3},{2,0},{3,1},{4,6},{5,7},{6,4},{7,5},{8,10},{9,11},{10,... | collective-permute-start | bytes 884744 | tf_op jit(solution)/shard_map/ppermute | solution.py:441
  70.1 18.6 %collective-permute-start.15 = (bf16[384,768]{1,0:T(8,128)(2,1)S(1)}, bf16[384,768]{1,0:T(8,128)(2,1)S(1)}, u32[]{:S(2)}, u32[]{:S(2)}) collective-permute-start(bf16[384,768]{1,0:T(8,128)(2,1)S(1)} %maximum_add_fusion.refs_4_.refs_1_), channel_id=1, source_target_pairs={{0,4},{1,5},{2,6},{3,7},{4,0},{5,1},{6,2},{7,3},{8,12},{9,13},{10,... | collective-permute-start | bytes 1769480 | tf_op jit(solution)/shard_map/ppermute | solution.py:441
  71.1 18.1 %collective-permute-start.14 = (bf16[384,768]{1,0:T(8,128)(2,1)S(1)}, bf16[384,768]{1,0:T(8,128)(2,1)S(1)}, u32[]{:S(2)}, u32[]{:S(2)}) collective-permute-start(bf16[384,768]{1,0:T(8,128)(2,1)S(1)} %maximum_add_fusion.refs_4_.refs_1_), channel_id=1, source_target_pairs={{0,2},{1,3},{2,0},{3,1},{4,6},{5,7},{6,4},{7,5},{8,10},{9,11},{10,... | collective-permute-start | bytes 1769480 | tf_op jit(solution)/shard_map/ppermute | solution.py:441
  88.8 13.6 %copy-start.1 = (bf16[384,768]{1,0:T(8,128)(2,1)}, bf16[384,768]{1,0:T(8,128)(2,1)S(1)}, u32[]{:S(2)}) copy-start(bf16[384,768]{1,0:T(8,128)(2,1)S(1)} %collective-permute-done.15.refs_6_.refs_3_) | copy-start | bytes 1769476
  88.8 13.6 %collective-permute-start.17 = (bf16[384,384]{1,0:T(8,128)(2,1)S(1)}, bf16[384,384]{1,0:T(8,128)(2,1)S(1)}, u32[]{:S(2)}, u32[]{:S(2)}) collective-permute-start(bf16[384,384]{1,0:T(8,128)(2,1)S(1)} %slice.75), channel_id=1, source_target_pairs={{0,2},{1,3},{2,0},{3,1},{4,6},{5,7},{6,4},{7,5},{8,10},{9,11},{10,... | collective-permute-start | bytes 884744 | tf_op jit(solution)/shard_map/ppermute | solution.py:441
  89.2 13.2 %copy-start.2 = (bf16[384,768]{1,0:T(8,128)(2,1)}, bf16[384,768]{1,0:T(8,128)(2,1)S(1)}, u32[]{:S(2)}) copy-start(bf16[384,768]{1,0:T(8,128)(2,1)S(1)} %collective-permute-done.14.refs_5_.refs_2_) | copy-start | bytes 1769476
  89.2 13.2 %collective-permute-start.16 = (bf16[384,384]{1,0:T(8,128)(2,1)S(1)}, bf16[384,384]{1,0:T(8,128)(2,1)S(1)}, u32[]{:S(2)}, u32[]{:S(2)}) collective-permute-start(bf16[384,384]{1,0:T(8,128)(2,1)S(1)} %slice.74), channel_id=1, source_target_pairs={{0,4},{1,5},{2,6},{3,7},{4,0},{5,1},{6,2},{7,3},{8,12},{9,13},{10,... | collective-permute-start | bytes 884744 | tf_op jit(solution)/shard_map/ppermute | solution.py:441
  90.4 12.0 %copy-start.11 = (f32[3,3,8,256]{3,2,1,0:T(8,128)S(1)}, f32[3,3,8,256]{3,2,1,0:T(8,128)}, u32[]{:S(2)}) copy-start(f32[3,3,8,256]{3,2,1,0:T(8,128)} %get-tuple-element.45) | copy-start | bytes 221188
  103.2 18.0 %copy-start.16 = (bf16[768,512]{1,0:T(8,128)(2,1)S(1)}, bf16[768,512]{1,0:T(8,128)(2,1)}, u32[]{:S(2)}) copy-start(bf16[768,512]{1,0:T(8,128)(2,1)} %get-tuple-element.33) | copy-start | bytes 2359300
  117.7 14.7 %collective-permute-start.20 = (f32[3,3,8,512]{3,2,1,0:T(8,128)S(1)}, f32[3,3,8,512]{3,2,1,0:T(8,128)S(1)}, u32[]{:S(2)}, u32[]{:S(2)}) collective-permute-start(f32[3,3,8,512]{3,2,1,0:T(8,128)S(1)} %constant_dynamic-update-slice_fusion), channel_id=1, source_target_pairs={{0,2},{1,3},{2,0},{3,1},{4,6},{5,7},{6,4},{7,5},{8,10},{9,11},{10,... | collective-permute-start | bytes 442376 | tf_op jit(solution)/shard_map/ppermute | solution.py:441
  119.3 13.0 %collective-permute-start.21 = (f32[3,3,8,512]{3,2,1,0:T(8,128)S(1)}, f32[3,3,8,512]{3,2,1,0:T(8,128)S(1)}, u32[]{:S(2)}, u32[]{:S(2)}) collective-permute-start(f32[3,3,8,512]{3,2,1,0:T(8,128)S(1)} %constant_dynamic-update-slice_fusion), channel_id=1, source_target_pairs={{0,4},{1,5},{2,6},{3,7},{4,0},{5,1},{6,2},{7,3},{8,12},{9,13},{10,... | collective-permute-start | bytes 442376 | tf_op jit(solution)/shard_map/ppermute | solution.py:441
  120.3 12.0 %collective-permute-start.22 = (f32[3,3,8,512]{3,2,1,0:T(8,128)S(1)}, f32[3,3,8,512]{3,2,1,0:T(8,128)S(1)}, u32[]{:S(2)}, u32[]{:S(2)}) collective-permute-start(f32[3,3,8,512]{3,2,1,0:T(8,128)S(1)} %constant_dynamic-update-slice_fusion), channel_id=1, source_target_pairs={{0,6},{1,7},{2,4},{3,5},{4,2},{5,3},{6,0},{7,1},{8,14},{9,15},{10,... | collective-permute-start | bytes 442376 | tf_op jit(solution)/shard_map/ppermute | solution.py:441
  121.2 12.6 %collective-permute-start.18 = (bf16[768,512]{1,0:T(8,128)(2,1)S(1)}, bf16[768,512]{1,0:T(8,128)(2,1)S(1)}, u32[]{:S(2)}, u32[]{:S(2)}) collective-permute-start(bf16[768,512]{1,0:T(8,128)(2,1)S(1)} %copy-done.16), channel_id=1, source_target_pairs={{0,1},{1,0},{2,3},{3,2},{4,5},{5,4},{6,7},{7,6},{8,9},{9,8},{10,11... | collective-permute-start | bytes 2359304 | tf_op jit(solution)/shard_map/ppermute | solution.py:441
  121.2 13.3 %collective-permute-start.19 = (bf16[768,512]{1,0:T(8,128)(2,1)}, bf16[768,512]{1,0:T(8,128)(2,1)S(1)}, u32[]{:S(2)}, u32[]{:S(2)}) collective-permute-start(bf16[768,512]{1,0:T(8,128)(2,1)} %get-tuple-element.43), channel_id=1, source_target_pairs={{0,1},{1,0},{2,3},{3,2},{4,5},{5,4},{6,7},{7,6},{8,9},{9,8},{10,11... | collective-permute-start | bytes 2359304 | tf_op jit(solution)/shard_map/ppermute | solution.py:441
  132.4 2.1 %collective-permute-start.23 = (f32[4,3,3,8,512]{4,3,2,1,0:T(8,128)S(1)}, f32[4,3,3,8,512]{4,3,2,1,0:T(8,128)S(1)}, u32[]{:S(2)}, u32[]{:S(2)}) collective-permute-start(f32[4,3,3,8,512]{4,3,2,1,0:T(8,128)S(1)} %pad_maximum_fusion.2.rest_5_), channel_id=1, source_target_pairs={{0,1},{1,0},{2,3},{3,2},{4,5},{5,4},{6,7},{7,6},{8,9},{9,8},{10,11... | collective-permute-start | bytes 1769480 | tf_op jit(solution)/shard_map/ppermute | solution.py:441
  (10 other events, 22.0 us)
Sparse Core Ops, SparseCore 0:
  43.2 67.0 all-gather.1

commit v5 on v4

--- a/solution.py
+++ b/solution.py
@@ -29,8 +29,8 @@
     return pl.CostEstimate(flops=int(microseconds * 1.1e9), bytes_accessed=100_000, transcendentals=0)
 
 
-def rope_tables(positions, width):
-    lane = jnp.arange(width, dtype=jnp.int32)
+def rope_tables(positions, width, zero):
+    lane = jnp.arange(width, dtype=jnp.int32) + zero
     lane = lane % HD if width % HD == 0 else lane
     frequency = jnp.power(THETA, -(lane % HALF).astype(F32) * (2.0 / HD))
     angles = positions.astype(F32)[:, None] * frequency[None, :]
@@ -76,22 +76,27 @@
 
 
 def fetch_weights(plan, refs, offs_ref, block_rows, w_ref, sem):
-    half = w_ref.shape[1] // len(plan)
-    for t, sources in enumerate(plan):
-        fetch(sources, refs, offs_ref, block_rows, half, lambda rows: w_ref.at[rows, pl.ds(t * half, half)], sem)
-
-
-def multiply(x, w_ref, u_ref, rows):
-    for n in range(w_ref.shape[1] // 256):
+    half = w_ref.shape[1] // 2
+    joined = [
+        source for source in plan[0] if (source[0], source[1] + half, source[2], source[3]) in plan[1]
+    ]
+    fetch(joined, refs, offs_ref, block_rows, 2 * half, lambda rows: w_ref.at[rows, pl.ds(0, 2 * half)], sem)
+    taken = {(ref, first) for ref, _, first, _ in joined}
+    for t in range(2):
+        single = [source for source in plan[t] if (source[0], source[2]) not in taken]
+        fetch(single, refs, offs_ref, block_rows, half, lambda rows: w_ref.at[rows, pl.ds(t * half, half)], sem)
+
+
+def project(x, w_ref, u_ref, table_ref, heads_ref):
+    stretch = table_ref.shape[1]
+    lane = lax.broadcasted_iota(jnp.int32, (stretch, LANES), 1)
+
+    def multiply(n):
         cols = slice(n * 256, (n + 1) * 256)
-        u_ref[:rows, cols] = jnp.dot(x, w_ref[:, cols], preferred_element_type=F32)
-
-
-def store_heads(u_ref, table_ref, heads_ref, first):
-    rows = table_ref.shape[1]
-    lane = lax.broadcasted_iota(jnp.int32, (rows, LANES), 1)
-    for h in range(8):
-        u = head_tile(u_ref, slice(0, rows), h)
+        u_ref[: x.shape[0], cols] = jnp.dot(x, w_ref[:, cols], preferred_element_type=F32)
+
+    def store(h):
+        u = head_tile(u_ref, slice(0, stretch), h)
         if h in (2, 3):
             u = jnp.where(lane < HD, u, 1.0)
         else:
@@ -100,7 +105,15 @@
                 + pltpu.roll(u, HALF, 1) * table_ref[1]
                 + pltpu.roll(u, LANES - HALF, 1) * table_ref[2]
             )
-        heads_ref[h, first : first + rows, :] = u.astype(BF16)
+        heads_ref[h] = u.astype(BF16)
+
+    multiply(0)
+    multiply(1)
+    store(0)
+    store(1)
+    multiply(2)
+    for h in range(2, 8):
+        store(h)
 
 
 def turn_decode(u, dtable_ref):
@@ -117,23 +130,28 @@
         jnp.int32, (block, block), 0
     )
     causal = jnp.concatenate([causal, causal], axis=0)
-    for j in range(2):
-        for i in range(stretch // block):
-            rows = slice(i * block, (i + 1) * block)
-            seen = (i + 1) * block
-            both = heads_ref[4 + 2 * j : 6 + 2 * j, rows, :].reshape(2 * block, LANES)
-            scores = lax.dot_general(
-                both, heads_ref[j, :seen, :], (((1,), (1,)), ((), ())), preferred_element_type=F32
-            )
-            last = jnp.where(causal, scores[:, i * block :], NEGATIVE)
-            scores = last if i == 0 else jnp.concatenate([scores[:, : i * block], last], axis=1)
-            peak = jnp.max(scores, axis=-1, keepdims=True)
-            weights = jnp.exp2((scores - peak) * (SCALE * LOG2E)).astype(BF16)
-            mixed = jnp.dot(weights, heads_ref[2 + j, :seen, :], preferred_element_type=F32)
-            mixed = (mixed / mixed[:, HD : HD + 1]).astype(BF16)
-            for parity in range(2):
-                lanes = slice((2 * j + parity) * LANES, (2 * j + parity + 1) * LANES)
-                o_ref[rows, lanes] = mixed[parity * block : (parity + 1) * block]
+    units = [(j, i) for i in range(stretch // block) for j in range(2)]
+
+    def score(j, i):
+        both = heads_ref[4 + 2 * j : 6 + 2 * j, i * block : (i + 1) * block, :].reshape(2 * block, LANES)
+        return lax.dot_general(
+            both, heads_ref[j, : (i + 1) * block, :], (((1,), (1,)), ((), ())), preferred_element_type=F32
+        )
+
+    following = score(*units[0])
+    for n, (j, i) in enumerate(units):
+        scores = following
+        if n + 1 < len(units):
+            following = score(*units[n + 1])
+        last = jnp.where(causal, scores[:, i * block :], NEGATIVE)
+        scores = last if i == 0 else jnp.concatenate([scores[:, : i * block], last], axis=1)
+        peak = jnp.max(scores, axis=-1, keepdims=True)
+        weights = jnp.exp2((scores - peak) * (SCALE * LOG2E)).astype(BF16)
+        mixed = jnp.dot(weights, heads_ref[2 + j, : (i + 1) * block, :], preferred_element_type=F32)
+        mixed = (mixed / mixed[:, HD : HD + 1]).astype(BF16)
+        for parity in range(2):
+            lanes = slice((2 * j + parity) * LANES, (2 * j + parity + 1) * LANES)
+            o_ref[i * block : (i + 1) * block, lanes] = mixed[parity * block : (parity + 1) * block]
 
 
 def decode(turned, requests, offset, k_ref, v_ref, len_ref, start_ref, part_ref):
@@ -181,7 +199,10 @@
                 lax.dot_general(query, k_ref[b, r], (((1,), (1,)), ((), ())), preferred_element_type=F32)
                 * SCALE
             )
-            live = lax.broadcasted_iota(jnp.int32, scores.shape, 1) + start_ref[b] < len_ref[r]
+            start = start_ref[0]
+            if b == 1:
+                start = start + span - 2 * span * lax.rem(lax.div(start, span), 2)
+            live = lax.broadcasted_iota(jnp.int32, scores.shape, 1) + start < len_ref[r]
             scores = jnp.where(live, scores, NEGATIVE)
             peak = jnp.max(scores, axis=-1, keepdims=True)
             expanded = jnp.where(live, jnp.exp(scores - peak), 0.0)
@@ -211,6 +232,7 @@
     (table_ref,) = take()
     if with_decode:
         dx_ref, dtable_ref = take(2)
+        (earlier_ref,) = take() if offset else (None,)
         caches = take(4)
     o_refs = take(stretches)
     if with_decode:
@@ -258,21 +280,26 @@
                 x_refs[n][rows, :] = normalize(x_refs[n][rows, :], gain)
                 return 0
 
-            lax.fori_loop(0, stretch // 64, body, 0)
+            lax.fori_loop(0, stretch // 64, body, 0, unroll=4)
             saves.append(pltpu.make_async_copy(x_refs[n].at[main], xn_hbm[n], sem.at[8 + n]))
             saves[-1].start()
         if n == 0:
             pltpu.make_async_copy(w_ref, w_ref, sem.at[0]).wait()
             if with_decode:
                 x_refs[0][stretch:, :] = dxn_ref[...] if norm else dx_ref[...]
-        multiply(x_refs[n][...], w_ref, u_refs[n], x_refs[n].shape[0])
-        store_heads(u_refs[n], table_ref, heads_refs[n], 0)
+        project(x_refs[n][...], w_ref, u_refs[n], table_ref, heads_refs[n])
         if n == 0 and with_decode:
             turned = turn_decode(u_refs[0][stretch:, :], dtable_ref)
             for m, source in enumerate(caches):
                 target = (k_ref, v_ref)[m % 2].at[m // 2]
                 pltpu.make_async_copy(target, target, sem.at[4 + m]).wait()
-            decode(turned, k_ref.shape[1], offset, k_ref, v_ref, len_ref, start_ref, part_ref)
+            if offset:
+                part_ref[:, :, :, :window] = earlier_ref[...]
+            own_lanes = pl.ds(window if offset else 0, window)
+            decode(
+                turned, k_ref.shape[1], offset, k_ref, v_ref, len_ref, start_ref,
+                part_ref.at[:, :, :, own_lanes] if offset else part_ref,
+            )
         attend(heads_refs[n], o_refs[n], 256)
     for save in saves:
         save.wait()
@@ -287,7 +314,7 @@
     hbm = pl.BlockSpec(memory_space=pl.ANY)
     operands, in_specs, offset, extra = [offs], [smem], None, 0
     if decoding:
-        offset, lane, cache_len, starts, dx, dtable, caches = decoding
+        offset, lane, cache_len, starts, dx, dtable, earlier, caches = decoding
         requests, span = caches[0].shape[:2]
         extra, window = dx.shape[0], 2 * LANES
         operands += [lane, cache_len, starts]
@@ -297,9 +324,9 @@
     out_shape = [jax.ShapeDtypeStruct((stretch, 4 * LANES), BF16)] * stretches
     out_specs = [vmem] * stretches
     if decoding:
-        operands += [dx, dtable, *caches]
-        in_specs += [vmem] * 2 + [hbm] * 4
-        out_shape.append(jax.ShapeDtypeStruct((3, 3, 2 * requests, window), F32))
+        operands += [dx, dtable, *earlier, *caches]
+        in_specs += [vmem] * (2 + len(earlier)) + [hbm] * 4
+        out_shape.append(jax.ShapeDtypeStruct((3, 3, 2 * requests, window * (1 + len(earlier))), F32))
         out_specs.append(vmem)
     if norm:
         out_shape += [jax.ShapeDtypeStruct((stretch, depth), BF16)] * stretches
@@ -329,7 +356,7 @@
     )(*operands)
 
 
-def output_kernel(requests, block_rows, plan, o_plan, core_ref, offs_ref, *rest):
+def output_kernel(requests, block_rows, plan, o_plan, core_ref, *rest):
     count = 1 + max(source[0] for sources in plan for source in sources)
     wo_refs = rest[:count]
     o_refs, rest = rest[count : count + len(o_plan)], rest[count + len(o_plan) :]
@@ -342,7 +369,8 @@
 
     @pl.when(step == 0)
     def _():
-        me, core = core_ref[0], core_ref[1]
+        me = core_ref[0]
+        core = lax.rem(me, 2)
         o_copies = [
             pltpu.make_async_copy(
                 source,
@@ -356,7 +384,7 @@
         for t, sources in enumerate(plan):
             for ref, column, first, blocks in sources:
                 for b in range(blocks):
-                    to = pl.multiple_of(offs_ref[first + b], 16)
+                    to = (first + b) * LANES
                     pltpu.make_async_copy(
                         wo_refs[ref].at[pl.ds(b * block_rows, block_rows), pl.ds(column, columns)],
                         wo_ref.at[t, pl.ds(to, block_rows)],
@@ -404,7 +432,7 @@
     dec_ref[...] = projected[stretch : stretch + requests].astype(BF16)
 
 
-def output(attended, parts, other_parts, core, offs, wo_pieces, block_rows, plan, requests):
+def output(attended, parts, other_parts, core, wo_pieces, block_rows, plan, requests):
     stretch = attended[0][0].shape[0]
     width = H * HD
     steps, extra = 2, 16
@@ -414,7 +442,7 @@
     return pl.pallas_call(
         functools.partial(output_kernel, requests, block_rows, plan, [piece[1:] for piece in attended]),
         grid=(steps,),
-        in_specs=[smem] * 2 + [hbm] * (len(wo_pieces) + len(attended)) + [vmem] * 2,
+        in_specs=[smem] + [hbm] * (len(wo_pieces) + len(attended)) + [vmem] * 2,
         out_specs=[
             pl.BlockSpec((stretch, width // steps), lambda t: (0, t)),
             pl.BlockSpec((requests, width // steps), lambda t: (0, t)),
@@ -434,7 +462,7 @@
         ),
         cost_estimate=cost(1),
         name="output",
-    )(core, offs, *wo_pieces, *[piece[0] for piece in attended], parts, other_parts)
+    )(core, *wo_pieces, *[piece[0] for piece in attended], parts, other_parts)
 
 
 def swap(array, mask, n_shard):
@@ -510,15 +538,20 @@
     split = n_shard == 8 and block_rows == HALF
 
     wo_plan = [[(0, 0, 0, H)], [(0, width, 0, H)]]
-    wo_offs = jnp.arange(H, dtype=jnp.int32) * LANES
     extra = 16
-    dx = jnp.pad(decode_x, ((0, extra - requests), (0, 0)))
-    decode_positions = jnp.concatenate([cache_len, jnp.zeros((extra - requests,), jnp.int32)])
-    tables = rope_tables(jnp.arange(stretch, dtype=jnp.int32), LANES)
-    turning = rope_tables(decode_positions, half)
     quarter = half // 2
-    plain = jnp.stack([jnp.ones((extra, quarter), F32)] + [jnp.zeros((extra, quarter), F32)] * 2)
-    dtable = jnp.concatenate([turning[:, :, :quarter], plain, turning], axis=2)
+
+    def pad_decode(rows):
+        return jnp.pad(rows, ((0, extra - requests), (0, 0)))
+
+    def make_tables(lengths):
+        decode_positions = jnp.concatenate([lengths, jnp.zeros((extra - requests,), jnp.int32)])
+        zero = jnp.minimum(lengths[0], 0)
+        turning = rope_tables(decode_positions, half, zero)
+        plain = jnp.stack([jnp.ones((extra, quarter), F32)] + [jnp.zeros((extra, quarter), F32)] * 2)
+        dtable = jnp.concatenate([turning[:, :, :quarter], plain, turning], axis=2)
+        return rope_tables(jnp.arange(stretch, dtype=jnp.int32) + zero, LANES, zero), dtable
+
     if split:
         first = core == 0
         mine = jnp.concatenate([gain_columns, jnp.where(first, low, high)], axis=1)
@@ -530,8 +563,12 @@
         block_rows = 2 * block_rows
         offs = chip * block_rows
         sib_x, sib_k, sib_v = [swap(after(array, theirs), 1, n_shard) for array in (prefill_x, k_cache, v_cache)]
-        here = jnp.concatenate(along_dp(pair[:, :head], n_dp), axis=0)
-        here = after(here, sib_x, sib_k, sib_v, tables, dtable, dx)
+        found = along_dp(pair[:, :head], n_dp)
+        dx = pad_decode(after(decode_x, found[1]))
+        tables, dtable = make_tables(after(cache_len, found[1]))
+        found[2:] = [after(block, tables, dtable, dx) for block in found[2:]]
+        here = jnp.concatenate(found, axis=0)
+        here = after(here, sib_x, sib_k, sib_v, offs)
         beside, above = swap(here, 2, n_shard), swap(here, 4, n_shard)
         wo = after(wo, here)
         later = after(pair[:, head:], here)
@@ -544,6 +581,7 @@
         beside, above = swap(later_here, 2, n_shard), swap(later_here, 4, n_shard)
     else:
         sib_x, sib_k, sib_v = [swap(array, 1, n_shard) for array in (prefill_x, k_cache, v_cache)]
+        dx, (tables, dtable) = pad_decode(decode_x), make_tables(cache_len)
         offs = jnp.zeros((1,), jnp.int32)
         every = lax.all_gather(jnp.concatenate([gain_columns, low, high], axis=1), everyone, axis=0, tiled=True)
         block_rows = every.shape[0]
@@ -553,11 +591,11 @@
 
     wo_all = lax.all_gather(wo, everyone, axis=0, tiled=True)
     lane = core.astype(jnp.int32).reshape(1) * half
-    starts = jnp.stack([me * span, (me ^ 1) * span]).astype(jnp.int32)
+    starts = (me * span).astype(jnp.int32).reshape(1)
     caches = [k_cache, v_cache, sib_k, sib_v]
     sib_o, part, sib_xn, dxn = run_group(
         [sib_x], tables, offs, pieces, block_rows, plan, norm=True,
-        decoding=(0, lane, cache_len, starts, dx, dtable, caches),
+        decoding=(0, lane, cache_len, starts, dx, dtable, [], caches),
     )
     later_pieces, later_plan = [], [[(0, 0, 0, 1)], [(0, half, 0, 1)]]
     if split:
@@ -569,20 +607,18 @@
     own_o, xn = run_group([after(prefill_x, sib_o)], tables, offs, pieces, block_rows, plan, norm=True)
     mine, theirs = [own_o], [sib_o]
     pieces, plan = [after(later_pieces[0], own_o)] + later_pieces[1:], later_plan
-    sib_o, later_part = run_group(
+    sib_o, part = run_group(
         [sib_xn], tables, offs, pieces, block_rows, plan,
-        decoding=(LANES // 2, lane + LANES, cache_len, starts, dxn, dtable, caches),
+        decoding=(LANES // 2, lane + LANES, cache_len, starts, dxn, dtable, [part], caches),
     )
     theirs.append(sib_o)
-    part = jnp.concatenate([part, later_part], axis=-1)
     parts = jnp.stack([part] + [swap(part, 2 * chip, n_shard) for chip in range(1, n_shard // 2)])
     mine += run_group([after(xn, sib_o)], tables, offs, pieces, block_rows, plan)
     other_parts = swap(after(parts, mine[1]), 1, n_shard)
     group_lanes = PAD // 4
     attended = [(piece, True, g * group_lanes) for g, piece in enumerate(mine)]
     attended += [(swap(piece, 1, n_shard), False, g * group_lanes) for g, piece in enumerate(theirs)]
-    me_and_core = jnp.stack([me, core]).astype(jnp.int32)
-    return output(attended, parts, other_parts, me_and_core, wo_offs, [wo_all], HD, wo_plan, requests)
+    return output(attended, parts, other_parts, me.astype(jnp.int32).reshape(1), [wo_all], HD, wo_plan, requests)
 
 
 def solution(mesh):

time: 153 us -> 150 us (0.980)
  other arithmetic: 9.63 us -> 7.73 us
    ppermute x6, waiting for transfers between devices: 20.9 us -> 17.5 us  [along_dp(): lax.ppermute(local, 'dp', [((i + shift) % n_dp, i) for i in range(n_dp)])]
    ppermute x18, waiting for transfers between devices: 13.7 us -> 16 us  [swap(): return lax.ppermute(array, 'shard', [(i, i ^ mask) for i in range(n_shard)])]
    unnamed x35 -> x38, local copies, waits for them, and re-layouts: 1.9 us -> 3.24 us
  transfers between devices with their start and end apart: 25 -> 25, of which waited for: 10 -> 11; matrix products, arithmetic and copies ran while one was open for 9% -> 7% of each run, Pallas kernels for 34% -> 34%
where the time goes in v5:
time: 150 us; the launch traced here: 149 us
  Pallas kernels  60.5 us (40%)
  waiting for transfers between devices  33.5 us (22%)
  starting transfers between devices  25 us (17%)
  between operations  14.5 us (10%)
  local copies, waits for them, and re-layouts  8.06 us (5%)
  other arithmetic  7.73 us (5%)
    pallas_call x4, Pallas kernels, run_group(): pl.pallas_call(functools.partial(group_kernel, block_rows, plan, norm, of...  49.7 us
    ppermute x6, waiting for transfers between devices, along_dp(): lax.ppermute(local, 'dp', [((i + shift) % n_dp, i) for i in range(n_dp)])  17.5 us
    ppermute x18, waiting for transfers between devices, swap(): return lax.ppermute(array, 'shard', [(i, i ^ mask) for i in range(n_shard)])  16 us
    ppermute x18, starting transfers between devices, swap(): return lax.ppermute(array, 'shard', [(i, i ^ mask) for i in range(n_shard)])  14.8 us
    pallas_call x1, Pallas kernels, output(): pl.pallas_call(functools.partial(output_kernel, requests, block_rows, pla...  10.2 us
    ppermute x6, starting transfers between devices, along_dp(): lax.ppermute(local, 'dp', [((i + shift) % n_dp, i) for i in range(n_dp)])  10.1 us
    unnamed x38, local copies, waits for them, and re-layouts  3.24 us
  transfers between devices with their start and end apart: 25, of which 11 were waited for; matrix products, arithmetic and copies ran while one was open for 7% of the time, Pallas kernels for 34%

profile of v5, /device:TPU:0, one launch (start us, length us, event | category | flops | bytes accessed | tf_op | source)
XLA Modules:
  0.0 149.2 jit_solution(118642435302075345)
XLA Ops:
  7.2 1.0 fusion.31
  10.0 1.0 collective-permute-done
  12.0 4.8 %collective-permute-start.1 = (bf16[96,896]{1,0:T(8,128)(2,1)S(1)}, bf16[96,896]{1,0:T(8,128)(2,1)S(1)}, u32[]{:S(2)}, u32[]{:S(2)}) collective-permute-start(bf16[96,896]{1,0:T(8,128)(2,1)S(1)} %fusion.4), channel_id=1, source_target_pairs={{8,0},{16,8},{24,16},{0,24},{9,1},{17,9},{25,17},{1,25},{10,2},{18... | collective-permute-start | bytes 516104 | tf_op jit(solution)/shard_map/ppermute | solution.py:495
  18.0 3.6 %collective-permute-done.1 = bf16[96,896]{1,0:T(8,128)(2,1)S(1)} collective-permute-done((bf16[96,896]{1,0:T(8,128)(2,1)S(1)}, bf16[96,896]{1,0:T(8,128)(2,1)S(1)}, u32[]{:S(2)}, u32[]{:S(2)}) %collective-permute-start.1) | collective-permute-done | bytes 172064 | tf_op jit(solution)/shard_map/ppermute | solution.py:495
  21.9 1.5 fusion.3
  24.8 1.1 pad_maximum_fusion.refs_10_.refs_7_
  25.9 6.0 %collective-permute-done.2 = bf16[96,896]{1,0:T(8,128)(2,1)S(1)} collective-permute-done((bf16[96,896]{1,0:T(8,128)(2,1)S(1)}, bf16[96,896]{1,0:T(8,128)(2,1)S(1)}, u32[]{:S(2)}, u32[]{:S(2)}) %collective-permute-start.2) | collective-permute-done | bytes 172064 | tf_op jit(solution)/shard_map/ppermute | solution.py:495
  31.9 0.9 pad_maximum_fusion.1.refs_4_.refs_1_
  32.8 1.4 copy-done.4
  34.2 1.4 collective-permute-start.10
  35.6 2.5 %collective-permute-start.8 = (bf16[96,768]{1,0:T(8,128)(2,1)}, bf16[96,768]{1,0:T(8,128)(2,1)}, u32[]{:S(2)}, u32[]{:S(2)}) collective-permute-start(bf16[96,768]{1,0:T(8,128)(2,1)} %pad_maximum_fusion.5.operand_ref), channel_id=1, source_target_pairs={{8,0},{16,8},{24,16},{0,24},{9,1},{17,9},{25,17},{1,25},{10,2},{18... | collective-permute-start | bytes 442376 | tf_op jit(solution)/shard_map/ppermute | solution.py:495
  38.1 1.5 collective-permute-start.9
  39.6 1.5 %collective-permute-start.11 = (bf16[384,896]{1,0:T(8,128)(2,1)}, bf16[384,896]{1,0:T(8,128)(2,1)}, u32[]{:S(2)}, u32[]{:S(2)}) collective-permute-start(bf16[384,896]{1,0:T(8,128)(2,1)} %pad_maximum_fusion.1.refs_4_.refs_1_), channel_id=1, source_target_pairs={{0,4},{1,5},{2,6},{3,7},{4,0},{5,1},{6,2},{7,3},{8,12},{9,13},{10,... | collective-permute-start | bytes 2064392 | tf_op jit(solution)/shard_map/ppermute | solution.py:469
  41.1 1.5 collective-permute-start.7
  43.2 1.6 %collective-permute-done.8 = bf16[96,768]{1,0:T(8,128)(2,1)} collective-permute-done((bf16[96,768]{1,0:T(8,128)(2,1)}, bf16[96,768]{1,0:T(8,128)(2,1)}, u32[]{:S(2)}, u32[]{:S(2)}) %collective-permute-start.8) | collective-permute-done | bytes 147488 | tf_op jit(solution)/shard_map/ppermute | solution.py:495
  44.8 6.3 %collective-permute-done.9 = bf16[96,768]{1,0:T(8,128)(2,1)} collective-permute-done((bf16[96,768]{1,0:T(8,128)(2,1)}, bf16[96,768]{1,0:T(8,128)(2,1)}, u32[]{:S(2)}, u32[]{:S(2)}) %collective-permute-start.9) | collective-permute-done | bytes 147488 | tf_op jit(solution)/shard_map/ppermute | solution.py:495
  51.1 1.9 %maximum_add_fusion.refs_4_.refs_1_ = bf16[384,768]{1,0:T(8,128)(2,1)S(1)} fusion(bf16[96,768]{1,0:T(8,128)(2,1)} %collective-permute-done.10, bf16[96,768]{1,0:T(8,128)(2,1)} %collective-permute-done.9, bf16[96,768]{1,0:T(8,128)(2,1)} %collective-permute-done.8, bf16[96,768]{1,0:T(8,128)(2,1)} %pad_maximum_fusion.5.operand_ref, bf16[]{:T(256)} %bitcast.2), kind=kLoop, calls=%fused_computation.2 | loop fusion | flops 2949120 | bytes 1179650 | tf_op jit(solution)/shard_map/add | solution.py:576
  52.9 5.5 %collective-permute-done.7.refs_5_.refs_2_ = bf16[384,896]{1,0:T(8,128)(2,1)} collective-permute-done((bf16[384,896]{1,0:T(8,128)(2,1)}, bf16[384,896]{1,0:T(8,128)(2,1)}, u32[]{:S(2)}, u32[]{:S(2)}) %collective-permute-start.7) | collective-permute-done | bytes 688160 | tf_op jit(solution)/shard_map/ppermute | solution.py:469
  58.5 1.0 slice.76
  60.1 1.0 slice.77
  61.1 1.6 %collective-permute-start.13 = (bf16[384,384]{1,0:T(8,128)(2,1)S(1)}, bf16[384,384]{1,0:T(8,128)(2,1)S(1)}, u32[]{:S(2)}, u32[]{:S(2)}) collective-permute-start(bf16[384,384]{1,0:T(8,128)(2,1)S(1)} %slice.77), channel_id=1, source_target_pairs={{0,2},{1,3},{2,0},{3,1},{4,6},{5,7},{6,4},{7,5},{8,10},{9,11},{10,... | collective-permute-start | bytes 884744 | tf_op jit(solution)/shard_map/ppermute | solution.py:469
  62.6 6.3 %collective-permute-done.13.refs_8_.refs_5_ = bf16[384,384]{1,0:T(8,128)(2,1)S(1)} collective-permute-done((bf16[384,384]{1,0:T(8,128)(2,1)S(1)}, bf16[384,384]{1,0:T(8,128)(2,1)S(1)}, u32[]{:S(2)}, u32[]{:S(2)}) %collective-permute-start.13) | collective-permute-done | bytes 294944 | tf_op jit(solution)/shard_map/ppermute | solution.py:469
  70.1 2.5 %collective-permute-start.14 = (bf16[384,768]{1,0:T(8,128)(2,1)S(1)}, bf16[384,768]{1,0:T(8,128)(2,1)S(1)}, u32[]{:S(2)}, u32[]{:S(2)}) collective-permute-start(bf16[384,768]{1,0:T(8,128)(2,1)S(1)} %maximum_add_fusion.refs_4_.refs_1_), channel_id=1, source_target_pairs={{0,2},{1,3},{2,0},{3,1},{4,6},{5,7},{6,4},{7,5},{8,10},{9,11},{10,... | collective-permute-start | bytes 1769480 | tf_op jit(solution)/shard_map/ppermute | solution.py:469
  72.7 14.4 %group.4 = (bf16[768,512]{1,0:T(8,128)(2,1)}, f32[3,3,8,256]{3,2,1,0:T(8,128)}, bf16[768,1536]{1,0:T(8,128)(2,1)}, bf16[16,1536]{1,0:T(8,128)(2,1)}) custom-call(s32[16]{0:T(128)} %fusion.27.refs_0_, s32[1]{0:T(128)} %bitcast.3.refs_1_, s32[4]{0:T(128)} %refs_2_.3, s32[1]{0:T(128)} %bitcast.4.refs_3_, bf16[384,896]{1,0:T(8,128)(2,1)} %pad_maximum_fusion.1.refs_4_.refs_1_, ...), custom_call_target="tpu_custom_call" | custom-call | flops 1100000000 | bytes 100000 | tf_op jit(solution)/shard_map/group/pallas_call | solution.py:347
  87.3 0.9 collective-permute-start.16
  88.3 11.6 %group.5 = (bf16[768,512]{1,0:T(8,128)(2,1)}, bf16[768,1536]{1,0:T(8,128)(2,1)}) custom-call(s32[16]{0:T(128)} %fusion.27.refs_0_, bf16[384,896]{1,0:T(8,128)(2,1)} %pad_maximum_fusion.1.refs_4_.refs_1_, bf16[384,896]{1,0:T(8,128)(2,1)} %collective-permute-done.7.refs_5_.refs_2_, bf16[384,896]{1,0:T(8,128)(2,1)} %collective-permute-done.11.refs_6_.refs_3_, ...), custom_call_target="tpu_custom_call" | custom-call | flops 1100000000 | bytes 100000 | tf_op jit(solution)/shard_map/group/pallas_call | solution.py:347
  101.1 13.3 %group.6 = (bf16[768,512]{1,0:T(8,128)(2,1)}, f32[3,3,8,512]{3,2,1,0:T(8,128)}) custom-call(s32[16]{0:T(128)} %fusion.27.refs_0_, s32[1]{0:T(128)S(6)} %add.140.refs_1_, s32[4]{0:T(128)} %refs_2_.3, s32[1]{0:T(128)} %bitcast.4.refs_3_, bf16[384,768]{1,0:T(8,128)(2,1)} %copy-done.1, bf16[384,768]{1,0:T(8,128)(2,1)} %copy-done.3, bf16[384,768]{1,0:T(8,128)(2,1)} %copy-done.2, ...), custom_call_target="tpu_custom_call" | custom-call | flops 1100000000 | bytes 100000 | tf_op jit(solution)/shard_map/group/pallas_call | solution.py:347
  114.4 1.5 %collective-permute-start.20 = (f32[3,3,8,512]{3,2,1,0:T(8,128)}, f32[3,3,8,512]{3,2,1,0:T(8,128)S(1)}, u32[]{:S(2)}, u32[]{:S(2)}) collective-permute-start(f32[3,3,8,512]{3,2,1,0:T(8,128)} %get-tuple-element.54), channel_id=1, source_target_pairs={{0,2},{1,3},{2,0},{3,1},{4,6},{5,7},{6,4},{7,5},{8,10},{9,11},{10,... | collective-permute-start | bytes 442376 | tf_op jit(solution)/shard_map/ppermute | solution.py:469
  116.0 1.3 collective-permute-start.21
  118.5 10.4 %group.7.rest_2_ = bf16[768,512]{1,0:T(8,128)(2,1)} custom-call(s32[16]{0:T(128)} %fusion.27.refs_0_, bf16[384,768]{1,0:T(8,128)(2,1)} %copy-done.1, bf16[384,768]{1,0:T(8,128)(2,1)} %copy-done.3, bf16[384,768]{1,0:T(8,128)(2,1)} %copy-done.2, bf16[384,384]{1,0:T(8,128)(2,1)} %copy-done.9, bf16[384,384]{1,0:T(8,128)(2,1)} %copy-done.8, ...), custom_call_target="tpu_custom_call" | custom-call | flops 1100000000 | bytes 100000 | tf_op jit(solution)/shard_map/group/pallas_call | solution.py:347
  129.1 2.0 %collective-permute-done.23.rest_6_ = f32[4,3,3,8,512]{4,3,2,1,0:T(8,128)S(1)} collective-permute-done((f32[4,3,3,8,512]{4,3,2,1,0:T(8,128)S(1)}, f32[4,3,3,8,512]{4,3,2,1,0:T(8,128)S(1)}, u32[]{:S(2)}, u32[]{:S(2)}) %collective-permute-start.23) | collective-permute-done | bytes 589856 | tf_op jit(solution)/shard_map/ppermute | solution.py:469
  132.2 10.2 %output.1 = (bf16[768,1536]{1,0:T(8,128)(2,1)}, bf16[4,1536]{1,0:T(4,128)(2,1)}) custom-call(s32[1]{0:T(128)} %bitcast.core_ref, bf16[1536,1536]{1,0:T(8,128)(2,1)} %all-gather.2.cloned.1.call-done.rest_0_, bf16[768,512]{1,0:T(8,128)(2,1)} %get-tuple-element.43.rest_1_, bf16[768,512]{1,0:T(8,128)(2,1)} %group.7.rest_2_, bf16[768,512]{1,0:T(8,128)(2,1)} %copy-done.10, ...), custom_call_target="tpu_custom_call" | custom-call | flops 1100000000 | bytes 100000 | tf_op jit(solution)/shard_map/output/pallas_call | solution.py:442
  (94 shorter events, 11.8 us)
Async XLA Ops:
  7.2 123.9 %all-gather.2.cloned.1.call-start = ((), (), s32[]{:S(2)}) async-start(), calls=%async_computation | async-start | bytes 4866048 | tf_op jit(solution)/shard_map/all_gather | solution.py:592
  9.2 12.3 %copy-start.16 = (s32[4]{0:T(128)S(1)}, s32[4]{0:T(128)}, u32[]{:S(2)}) copy-start(s32[4]{0:T(128)} %refs_2_.3) | copy-start | bytes 52
  9.5 1.5 %collective-permute-start = (bf16[48,1664]{1,0:T(8,128)(2,1)S(1)}, bf16[48,1664]{1,0:T(8,128)(2,1)S(1)}, u32[]{:S(2)}, u32[]{:S(2)}) collective-permute-start(bf16[48,1664]{1,0:T(8,128)(2,1)S(1)} %pad_maximum_fusion.3), channel_id=1, source_target_pairs={{0,1},{1,0},{2,3},{3,2},{4,5},{5,4},{6,7},{7,6},{8,9},{9,8},{10,11... | collective-permute-start | bytes 479240 | tf_op jit(solution)/shard_map/ppermute | solution.py:469
  11.0 21.8 %collective-permute-start.5 = (bf16[4,512,768]{2,1,0:T(8,128)(2,1)}, bf16[4,512,768]{2,1,0:T(8,128)(2,1)S(1)}, u32[]{:S(2)}, u32[]{:S(2)}) collective-permute-start(bf16[4,512,768]{2,1,0:T(8,128)(2,1)} %refs_14_.3), channel_id=1, source_target_pairs={{0,1},{1,0},{2,3},{3,2},{4,5},{5,4},{6,7},{7,6},{8,9},{9,8},{10,11... | collective-permute-start | bytes 9437192 | tf_op jit(solution)/shard_map/ppermute | solution.py:469
  11.4 22.9 %collective-permute-start.6 = (bf16[4,512,768]{2,1,0:T(8,128)(2,1)}, bf16[4,512,768]{2,1,0:T(8,128)(2,1)}, u32[]{:S(2)}, u32[]{:S(2)}) collective-permute-start(bf16[4,512,768]{2,1,0:T(8,128)(2,1)} %refs_15_.1), channel_id=1, source_target_pairs={{0,1},{1,0},{2,3},{3,2},{4,5},{5,4},{6,7},{7,6},{8,9},{9,8},{10,11... | collective-permute-start | bytes 9437192 | tf_op jit(solution)/shard_map/ppermute | solution.py:469
  11.5 21.3 %collective-permute-start.4 = (bf16[768,1536]{1,0:T(8,128)(2,1)}, bf16[768,1536]{1,0:T(8,128)(2,1)S(1)}, u32[]{:S(2)}, u32[]{:S(2)}) collective-permute-start(bf16[768,1536]{1,0:T(8,128)(2,1)} %refs_6_), channel_id=1, source_target_pairs={{0,1},{1,0},{2,3},{3,2},{4,5},{5,4},{6,7},{7,6},{8,9},{9,8},{10,11... | collective-permute-start | bytes 7077896 | tf_op jit(solution)/shard_map/ppermute | solution.py:469
  11.9 11.5 %copy-start.14 = (f32[3,16,192]{2,1,0:T(8,128)S(1)}, f32[3,16,192]{2,1,0:T(8,128)}, u32[]{:S(2)}) copy-start(f32[3,16,192]{2,1,0:T(8,128)} %constant.109.clone.1) | copy-start | bytes 110596
  11.9 12.2 %copy-start.15 = (bf16[4,1536]{1,0:T(4,128)(2,1)S(1)}, bf16[4,1536]{1,0:T(4,128)(2,1)}, u32[]{:S(2)}) copy-start(bf16[4,1536]{1,0:T(4,128)(2,1)} %param.9) | copy-start | bytes 36868
  12.0 9.6 %collective-permute-start.1 = (bf16[96,896]{1,0:T(8,128)(2,1)S(1)}, bf16[96,896]{1,0:T(8,128)(2,1)S(1)}, u32[]{:S(2)}, u32[]{:S(2)}) collective-permute-start(bf16[96,896]{1,0:T(8,128)(2,1)S(1)} %fusion.4), channel_id=1, source_target_pairs={{8,0},{16,8},{24,16},{0,24},{9,1},{17,9},{25,17},{1,25},{10,2},{18... | collective-permute-start | bytes 516104 | tf_op jit(solution)/shard_map/ppermute | solution.py:495
  17.3 14.6 %collective-permute-start.2 = (bf16[96,896]{1,0:T(8,128)(2,1)S(1)}, bf16[96,896]{1,0:T(8,128)(2,1)S(1)}, u32[]{:S(2)}, u32[]{:S(2)}) collective-permute-start(bf16[96,896]{1,0:T(8,128)(2,1)S(1)} %fusion.4), channel_id=1, source_target_pairs={{16,0},{24,8},{0,16},{8,24},{17,1},{25,9},{1,17},{9,25},{18,2},{26... | collective-permute-start | bytes 516104 | tf_op jit(solution)/shard_map/ppermute | solution.py:495
  21.5 10.4 %collective-permute-start.3 = (bf16[96,896]{1,0:T(8,128)(2,1)S(1)}, bf16[96,896]{1,0:T(8,128)(2,1)S(1)}, u32[]{:S(2)}, u32[]{:S(2)}) collective-permute-start(bf16[96,896]{1,0:T(8,128)(2,1)S(1)} %fusion.4), channel_id=1, source_target_pairs={{24,0},{0,8},{8,16},{16,24},{25,1},{1,9},{9,17},{17,25},{26,2},{2,... | collective-permute-start | bytes 516104 | tf_op jit(solution)/shard_map/ppermute | solution.py:495
  34.2 8.9 %collective-permute-start.10 = (bf16[96,768]{1,0:T(8,128)(2,1)}, bf16[96,768]{1,0:T(8,128)(2,1)}, u32[]{:S(2)}, u32[]{:S(2)}) collective-permute-start(bf16[96,768]{1,0:T(8,128)(2,1)} %pad_maximum_fusion.5.operand_ref), channel_id=1, source_target_pairs={{24,0},{0,8},{8,16},{16,24},{25,1},{1,9},{9,17},{17,25},{26,2},{2,... | collective-permute-start | bytes 442376 | tf_op jit(solution)/shard_map/ppermute | solution.py:495
  35.6 9.1 %collective-permute-start.8 = (bf16[96,768]{1,0:T(8,128)(2,1)}, bf16[96,768]{1,0:T(8,128)(2,1)}, u32[]{:S(2)}, u32[]{:S(2)}) collective-permute-start(bf16[96,768]{1,0:T(8,128)(2,1)} %pad_maximum_fusion.5.operand_ref), channel_id=1, source_target_pairs={{8,0},{16,8},{24,16},{0,24},{9,1},{17,9},{25,17},{1,25},{10,2},{18... | collective-permute-start | bytes 442376 | tf_op jit(solution)/shard_map/ppermute | solution.py:495
  38.1 13.0 %collective-permute-start.9 = (bf16[96,768]{1,0:T(8,128)(2,1)}, bf16[96,768]{1,0:T(8,128)(2,1)}, u32[]{:S(2)}, u32[]{:S(2)}) collective-permute-start(bf16[96,768]{1,0:T(8,128)(2,1)} %pad_maximum_fusion.5.operand_ref), channel_id=1, source_target_pairs={{16,0},{24,8},{0,16},{8,24},{17,1},{25,9},{1,17},{9,25},{18,2},{26... | collective-permute-start | bytes 442376 | tf_op jit(solution)/shard_map/ppermute | solution.py:495
  39.6 20.5 %collective-permute-start.11 = (bf16[384,896]{1,0:T(8,128)(2,1)}, bf16[384,896]{1,0:T(8,128)(2,1)}, u32[]{:S(2)}, u32[]{:S(2)}) collective-permute-start(bf16[384,896]{1,0:T(8,128)(2,1)} %pad_maximum_fusion.1.refs_4_.refs_1_), channel_id=1, source_target_pairs={{0,4},{1,5},{2,6},{3,7},{4,0},{5,1},{6,2},{7,3},{8,12},{9,13},{10,... | collective-permute-start | bytes 2064392 | tf_op jit(solution)/shard_map/ppermute | solution.py:469
  41.1 17.4 %collective-permute-start.7 = (bf16[384,896]{1,0:T(8,128)(2,1)}, bf16[384,896]{1,0:T(8,128)(2,1)}, u32[]{:S(2)}, u32[]{:S(2)}) collective-permute-start(bf16[384,896]{1,0:T(8,128)(2,1)} %pad_maximum_fusion.1.refs_4_.refs_1_), channel_id=1, source_target_pairs={{0,2},{1,3},{2,0},{3,1},{4,6},{5,7},{6,4},{7,5},{8,10},{9,11},{10,... | collective-permute-start | bytes 2064392 | tf_op jit(solution)/shard_map/ppermute | solution.py:469
  52.9 34.2 %copy-start.1 = (bf16[384,768]{1,0:T(8,128)(2,1)}, bf16[384,768]{1,0:T(8,128)(2,1)S(1)}, u32[]{:S(2)}) copy-start(bf16[384,768]{1,0:T(8,128)(2,1)S(1)} %maximum_add_fusion.refs_4_.refs_1_) | copy-start | bytes 1769476
  59.5 10.1 %collective-permute-start.12 = (bf16[384,512]{1,0:T(8,128)(2,1)S(1)}, bf16[384,512]{1,0:T(8,128)(2,1)S(1)}, u32[]{:S(2)}, u32[]{:S(2)}) collective-permute-start(bf16[384,512]{1,0:T(8,128)(2,1)S(1)} %slice.76), channel_id=1, source_target_pairs={{0,4},{1,5},{2,6},{3,7},{4,0},{5,1},{6,2},{7,3},{8,12},{9,13},{10,... | collective-permute-start | bytes 1179656 | tf_op jit(solution)/shard_map/ppermute | solution.py:469
  61.1 7.8 %collective-permute-start.13 = (bf16[384,384]{1,0:T(8,128)(2,1)S(1)}, bf16[384,384]{1,0:T(8,128)(2,1)S(1)}, u32[]{:S(2)}, u32[]{:S(2)}) collective-permute-start(bf16[384,384]{1,0:T(8,128)(2,1)S(1)} %slice.77), channel_id=1, source_target_pairs={{0,2},{1,3},{2,0},{3,1},{4,6},{5,7},{6,4},{7,5},{8,10},{9,11},{10,... | collective-permute-start | bytes 884744 | tf_op jit(solution)/shard_map/ppermute | solution.py:469
  69.6 17.6 %collective-permute-start.15 = (bf16[384,768]{1,0:T(8,128)(2,1)S(1)}, bf16[384,768]{1,0:T(8,128)(2,1)S(1)}, u32[]{:S(2)}, u32[]{:S(2)}) collective-permute-start(bf16[384,768]{1,0:T(8,128)(2,1)S(1)} %maximum_add_fusion.refs_4_.refs_1_), channel_id=1, source_target_pairs={{0,4},{1,5},{2,6},{3,7},{4,0},{5,1},{6,2},{7,3},{8,12},{9,13},{10,... | collective-permute-start | bytes 1769480 | tf_op jit(solution)/shard_map/ppermute | solution.py:469
  70.1 17.1 %collective-permute-start.14 = (bf16[384,768]{1,0:T(8,128)(2,1)S(1)}, bf16[384,768]{1,0:T(8,128)(2,1)S(1)}, u32[]{:S(2)}, u32[]{:S(2)}) collective-permute-start(bf16[384,768]{1,0:T(8,128)(2,1)S(1)} %maximum_add_fusion.refs_4_.refs_1_), channel_id=1, source_target_pairs={{0,2},{1,3},{2,0},{3,1},{4,6},{5,7},{6,4},{7,5},{8,10},{9,11},{10,... | collective-permute-start | bytes 1769480 | tf_op jit(solution)/shard_map/ppermute | solution.py:469
  87.1 12.8 %copy-start.2 = (bf16[384,768]{1,0:T(8,128)(2,1)}, bf16[384,768]{1,0:T(8,128)(2,1)S(1)}, u32[]{:S(2)}) copy-start(bf16[384,768]{1,0:T(8,128)(2,1)S(1)} %collective-permute-done.15.refs_6_.refs_3_) | copy-start | bytes 1769476
  87.2 13.0 %collective-permute-start.17 = (bf16[384,384]{1,0:T(8,128)(2,1)S(1)}, bf16[384,384]{1,0:T(8,128)(2,1)S(1)}, u32[]{:S(2)}, u32[]{:S(2)}) collective-permute-start(bf16[384,384]{1,0:T(8,128)(2,1)S(1)} %slice.79), channel_id=1, source_target_pairs={{0,2},{1,3},{2,0},{3,1},{4,6},{5,7},{6,4},{7,5},{8,10},{9,11},{10,... | collective-permute-start | bytes 884744 | tf_op jit(solution)/shard_map/ppermute | solution.py:469
  87.3 12.6 %copy-start.3 = (bf16[384,768]{1,0:T(8,128)(2,1)}, bf16[384,768]{1,0:T(8,128)(2,1)S(1)}, u32[]{:S(2)}) copy-start(bf16[384,768]{1,0:T(8,128)(2,1)S(1)} %collective-permute-done.14.refs_5_.refs_2_) | copy-start | bytes 1769476
  87.3 13.1 %collective-permute-start.16 = (bf16[384,384]{1,0:T(8,128)(2,1)S(1)}, bf16[384,384]{1,0:T(8,128)(2,1)S(1)}, u32[]{:S(2)}, u32[]{:S(2)}) collective-permute-start(bf16[384,384]{1,0:T(8,128)(2,1)S(1)} %slice.78), channel_id=1, source_target_pairs={{0,4},{1,5},{2,6},{3,7},{4,0},{5,1},{6,2},{7,3},{8,12},{9,13},{10,... | collective-permute-start | bytes 884744 | tf_op jit(solution)/shard_map/ppermute | solution.py:469
  101.1 16.9 %copy-start.18 = (bf16[768,512]{1,0:T(8,128)(2,1)S(1)}, bf16[768,512]{1,0:T(8,128)(2,1)}, u32[]{:S(2)}) copy-start(bf16[768,512]{1,0:T(8,128)(2,1)} %get-tuple-element.41) | copy-start | bytes 2359300
  114.4 14.5 %collective-permute-start.20 = (f32[3,3,8,512]{3,2,1,0:T(8,128)}, f32[3,3,8,512]{3,2,1,0:T(8,128)S(1)}, u32[]{:S(2)}, u32[]{:S(2)}) collective-permute-start(f32[3,3,8,512]{3,2,1,0:T(8,128)} %get-tuple-element.54), channel_id=1, source_target_pairs={{0,2},{1,3},{2,0},{3,1},{4,6},{5,7},{6,4},{7,5},{8,10},{9,11},{10,... | collective-permute-start | bytes 442376 | tf_op jit(solution)/shard_map/ppermute | solution.py:469
  116.0 13.0 %collective-permute-start.21 = (f32[3,3,8,512]{3,2,1,0:T(8,128)}, f32[3,3,8,512]{3,2,1,0:T(8,128)S(1)}, u32[]{:S(2)}, u32[]{:S(2)}) collective-permute-start(f32[3,3,8,512]{3,2,1,0:T(8,128)} %get-tuple-element.54), channel_id=1, source_target_pairs={{0,4},{1,5},{2,6},{3,7},{4,0},{5,1},{6,2},{7,3},{8,12},{9,13},{10,... | collective-permute-start | bytes 442376 | tf_op jit(solution)/shard_map/ppermute | solution.py:469
  117.3 11.6 %collective-permute-start.22 = (f32[3,3,8,512]{3,2,1,0:T(8,128)}, f32[3,3,8,512]{3,2,1,0:T(8,128)S(1)}, u32[]{:S(2)}, u32[]{:S(2)}) collective-permute-start(f32[3,3,8,512]{3,2,1,0:T(8,128)} %get-tuple-element.54), channel_id=1, source_target_pairs={{0,6},{1,7},{2,4},{3,5},{4,2},{5,3},{6,0},{7,1},{8,14},{9,15},{10,... | collective-permute-start | bytes 442376 | tf_op jit(solution)/shard_map/ppermute | solution.py:469
  118.0 11.1 %collective-permute-start.18 = (bf16[768,512]{1,0:T(8,128)(2,1)S(1)}, bf16[768,512]{1,0:T(8,128)(2,1)S(1)}, u32[]{:S(2)}, u32[]{:S(2)}) collective-permute-start(bf16[768,512]{1,0:T(8,128)(2,1)S(1)} %copy-done.18), channel_id=1, source_target_pairs={{0,1},{1,0},{2,3},{3,2},{4,5},{5,4},{6,7},{7,6},{8,9},{9,8},{10,11... | collective-permute-start | bytes 2359304 | tf_op jit(solution)/shard_map/ppermute | solution.py:469
  118.0 13.1 %collective-permute-start.19 = (bf16[768,512]{1,0:T(8,128)(2,1)}, bf16[768,512]{1,0:T(8,128)(2,1)S(1)}, u32[]{:S(2)}, u32[]{:S(2)}) collective-permute-start(bf16[768,512]{1,0:T(8,128)(2,1)} %get-tuple-element.52), channel_id=1, source_target_pairs={{0,1},{1,0},{2,3},{3,2},{4,5},{5,4},{6,7},{7,6},{8,9},{9,8},{10,11... | collective-permute-start | bytes 2359304 | tf_op jit(solution)/shard_map/ppermute | solution.py:469
  129.0 2.1 %collective-permute-start.23 = (f32[4,3,3,8,512]{4,3,2,1,0:T(8,128)S(1)}, f32[4,3,3,8,512]{4,3,2,1,0:T(8,128)S(1)}, u32[]{:S(2)}, u32[]{:S(2)}) collective-permute-start(f32[4,3,3,8,512]{4,3,2,1,0:T(8,128)S(1)} %pad_maximum_fusion.2.rest_5_), channel_id=1, source_target_pairs={{0,1},{1,0},{2,3},{3,2},{4,5},{5,4},{6,7},{7,6},{8,9},{9,8},{10,11... | collective-permute-start | bytes 1769480 | tf_op jit(solution)/shard_map/ppermute | solution.py:469
  (12 other events, 37.4 us)
Sparse Core Ops, SparseCore 0:
  42.7 67.5 all-gather.1

commit v6 on v5

--- a/solution.py
+++ b/solution.py
@@ -146,7 +146,7 @@
         last = jnp.where(causal, scores[:, i * block :], NEGATIVE)
         scores = last if i == 0 else jnp.concatenate([scores[:, : i * block], last], axis=1)
         peak = jnp.max(scores, axis=-1, keepdims=True)
-        weights = jnp.exp2((scores - peak) * (SCALE * LOG2E)).astype(BF16)
+        weights = jnp.exp2(scores * (SCALE * LOG2E) - peak * (SCALE * LOG2E)).astype(BF16)
         mixed = jnp.dot(weights, heads_ref[2 + j, : (i + 1) * block, :], preferred_element_type=F32)
         mixed = (mixed / mixed[:, HD : HD + 1]).astype(BF16)
         for parity in range(2):
@@ -568,11 +568,12 @@
         tables, dtable = make_tables(after(cache_len, found[1]))
         found[2:] = [after(block, tables, dtable, dx) for block in found[2:]]
         here = jnp.concatenate(found, axis=0)
-        here = after(here, sib_x, sib_k, sib_v, offs)
+        here = after(here, offs)
         beside, above = swap(here, 2, n_shard), swap(here, 4, n_shard)
         wo = after(wo, here)
-        later = after(pair[:, head:], here)
+        later = after(pair[:, head:], here, sib_x, sib_k, sib_v)
         found = along_dp(later, n_dp)
+        found[1:] = [after(block, beside, above) for block in found[1:]]
         later_here = jnp.concatenate(found, axis=0) + fence(later)
         pieces = pieces_of(here, after(beside, later_here), after(above, later_here), LANES + half, n_shard)
         plan = lay_out(pieces, {LANES: 0, LANES + half: 1, 0: 2}, n_dp)

time: 150 us -> 152 us (1.013)
  waiting for transfers between devices: 33.5 us -> 36.9 us
    ppermute x18, waiting for transfers between devices: 16 us -> 24.9 us  [swap(): return lax.ppermute(array, 'shard', [(i, i ^ mask) for i in range(n_shard)])]
    ppermute x6, waiting for transfers between devices: 17.5 us -> 12 us  [along_dp(): lax.ppermute(local, 'dp', [((i + shift) % n_dp, i) for i in range(n_dp)])]
    unnamed x38 -> x36, local copies, waits for them, and re-layouts: 3.24 us -> 1.92 us
  transfers between devices with their start and end apart: 25 -> 25, of which waited for: 11 -> 8; matrix products, arithmetic and copies ran while one was open for 7% -> 7% of each run, Pallas kernels for 34% -> 34%
where the time goes in v6:
time: 152 us
  Pallas kernels  61.1 us (40%)
  waiting for transfers between devices  36.9 us (24%)
  starting transfers between devices  24.4 us (16%)
  between operations  14.5 us (10%)
  other arithmetic  7.77 us (5%)
  local copies, waits for them, and re-layouts  6.94 us (5%)
    pallas_call x4, Pallas kernels, run_group(): pl.pallas_call(functools.partial(group_kernel, block_rows, plan, norm, of...  50.3 us
    ppermute x18, waiting for transfers between devices, swap(): return lax.ppermute(array, 'shard', [(i, i ^ mask) for i in range(n_shard)])  24.9 us
    ppermute x18, starting transfers between devices, swap(): return lax.ppermute(array, 'shard', [(i, i ^ mask) for i in range(n_shard)])  14.2 us
    ppermute x6, waiting for transfers between devices, along_dp(): lax.ppermute(local, 'dp', [((i + shift) % n_dp, i) for i in range(n_dp)])  12 us
    pallas_call x1, Pallas kernels, output(): pl.pallas_call(functools.partial(output_kernel, requests, block_rows, pla...  10.2 us
    ppermute x6, starting transfers between devices, along_dp(): lax.ppermute(local, 'dp', [((i + shift) % n_dp, i) for i in range(n_dp)])  10.2 us
  transfers between devices with their start and end apart: 25, of which 8 were waited for; matrix products, arithmetic and copies ran while one was open for 7% of the time, Pallas kernels for 34%

profile of v6, /device:TPU:0, one launch (start us, length us, event | category | flops | bytes accessed | tf_op | source)
XLA Modules:
  0.0 151.7 jit_solution(11515779354930200040)
XLA Ops:
  7.2 1.0 fusion.31
  8.2 0.8 fusion.30
  10.0 1.0 collective-permute-done
  12.0 4.8 %collective-permute-start.1 = (bf16[96,896]{1,0:T(8,128)(2,1)S(1)}, bf16[96,896]{1,0:T(8,128)(2,1)S(1)}, u32[]{:S(2)}, u32[]{:S(2)}) collective-permute-start(bf16[96,896]{1,0:T(8,128)(2,1)S(1)} %fusion.4), channel_id=1, source_target_pairs={{8,0},{16,8},{24,16},{0,24},{9,1},{17,9},{25,17},{1,25},{10,2},{18... | collective-permute-start | bytes 516104 | tf_op jit(solution)/shard_map/ppermute | solution.py:495
  18.0 3.6 %collective-permute-done.1 = bf16[96,896]{1,0:T(8,128)(2,1)S(1)} collective-permute-done((bf16[96,896]{1,0:T(8,128)(2,1)S(1)}, bf16[96,896]{1,0:T(8,128)(2,1)S(1)}, u32[]{:S(2)}, u32[]{:S(2)}) %collective-permute-start.1) | collective-permute-done | bytes 172064 | tf_op jit(solution)/shard_map/ppermute | solution.py:495
  21.9 1.5 fusion.3
  24.8 1.1 pad_maximum_fusion.refs_10_.refs_7_
  25.9 6.0 %collective-permute-done.2 = bf16[96,896]{1,0:T(8,128)(2,1)S(1)} collective-permute-done((bf16[96,896]{1,0:T(8,128)(2,1)S(1)}, bf16[96,896]{1,0:T(8,128)(2,1)S(1)}, u32[]{:S(2)}, u32[]{:S(2)}) %collective-permute-start.2) | collective-permute-done | bytes 172064 | tf_op jit(solution)/shard_map/ppermute | solution.py:495
  31.9 0.9 pad_maximum_fusion.1.refs_4_.refs_1_
  32.8 1.5 collective-permute-start.4
  34.3 1.5 %collective-permute-start.9 = (bf16[384,896]{1,0:T(8,128)(2,1)}, bf16[384,896]{1,0:T(8,128)(2,1)}, u32[]{:S(2)}, u32[]{:S(2)}) collective-permute-start(bf16[384,896]{1,0:T(8,128)(2,1)} %pad_maximum_fusion.1.refs_4_.refs_1_), channel_id=1, source_target_pairs={{0,4},{1,5},{2,6},{3,7},{4,0},{5,1},{6,2},{7,3},{8,12},{9,13},{10,... | collective-permute-start | bytes 2064392 | tf_op jit(solution)/shard_map/ppermute | solution.py:469
  35.9 2.6 %collective-permute-start.8 = (bf16[96,768]{1,0:T(8,128)(2,1)}, bf16[96,768]{1,0:T(8,128)(2,1)}, u32[]{:S(2)}, u32[]{:S(2)}) collective-permute-start(bf16[96,768]{1,0:T(8,128)(2,1)} %pad_maximum_fusion.5.operand_ref), channel_id=1, source_target_pairs={{8,0},{16,8},{24,16},{0,24},{9,1},{17,9},{25,17},{1,25},{10,2},{18... | collective-permute-start | bytes 442376 | tf_op jit(solution)/shard_map/ppermute | solution.py:495
  38.5 0.8 collective-permute-start.10
  39.3 1.9 %collective-permute-start.11 = (bf16[96,768]{1,0:T(8,128)(2,1)}, bf16[96,768]{1,0:T(8,128)(2,1)}, u32[]{:S(2)}, u32[]{:S(2)}) collective-permute-start(bf16[96,768]{1,0:T(8,128)(2,1)} %pad_maximum_fusion.5.operand_ref), channel_id=1, source_target_pairs={{24,0},{0,8},{8,16},{16,24},{25,1},{1,9},{9,17},{17,25},{26,2},{2,... | collective-permute-start | bytes 442376 | tf_op jit(solution)/shard_map/ppermute | solution.py:495
  41.8 9.2 %collective-permute-done.4.refs_5_.refs_2_ = bf16[384,896]{1,0:T(8,128)(2,1)} collective-permute-done((bf16[384,896]{1,0:T(8,128)(2,1)}, bf16[384,896]{1,0:T(8,128)(2,1)}, u32[]{:S(2)}, u32[]{:S(2)}) %collective-permute-start.4) | collective-permute-done | bytes 688160 | tf_op jit(solution)/shard_map/ppermute | solution.py:469
  51.0 1.2 collective-permute-done.9.refs_6_.refs_3_
  52.2 2.4 %collective-permute-done.10 = bf16[96,768]{1,0:T(8,128)(2,1)} collective-permute-done((bf16[96,768]{1,0:T(8,128)(2,1)}, bf16[96,768]{1,0:T(8,128)(2,1)}, u32[]{:S(2)}, u32[]{:S(2)}) %collective-permute-start.10) | collective-permute-done | bytes 147488 | tf_op jit(solution)/shard_map/ppermute | solution.py:495
  54.6 1.9 %maximum_add_fusion.refs_4_.refs_1_ = bf16[384,768]{1,0:T(8,128)(2,1)S(1)} fusion(bf16[96,768]{1,0:T(8,128)(2,1)} %collective-permute-done.11, bf16[96,768]{1,0:T(8,128)(2,1)} %collective-permute-done.10, bf16[96,768]{1,0:T(8,128)(2,1)} %collective-permute-done.8, bf16[96,768]{1,0:T(8,128)(2,1)} %pad_maximum_fusion.5.operand_ref, bf16[]{:T(256)} %bitcast.2), kind=kLoop, calls=%fused_computation.2 | loop fusion | flops 2949120 | bytes 1179650 | tf_op jit(solution)/shard_map/add | solution.py:577
  56.5 1.2 slice.76
  58.2 1.0 slice.77
  59.7 11.5 %collective-permute-done.13.refs_8_.refs_5_ = bf16[384,384]{1,0:T(8,128)(2,1)S(1)} collective-permute-done((bf16[384,384]{1,0:T(8,128)(2,1)S(1)}, bf16[384,384]{1,0:T(8,128)(2,1)S(1)}, u32[]{:S(2)}, u32[]{:S(2)}) %collective-permute-start.13) | collective-permute-done | bytes 294944 | tf_op jit(solution)/shard_map/ppermute | solution.py:469
  71.2 2.5 %collective-permute-start.15 = (bf16[384,768]{1,0:T(8,128)(2,1)S(1)}, bf16[384,768]{1,0:T(8,128)(2,1)S(1)}, u32[]{:S(2)}, u32[]{:S(2)}) collective-permute-start(bf16[384,768]{1,0:T(8,128)(2,1)S(1)} %maximum_add_fusion.refs_4_.refs_1_), channel_id=1, source_target_pairs={{0,4},{1,5},{2,6},{3,7},{4,0},{5,1},{6,2},{7,3},{8,12},{9,13},{10,... | collective-permute-start | bytes 1769480 | tf_op jit(solution)/shard_map/ppermute | solution.py:469
  73.8 14.5 %group.4 = (bf16[768,512]{1,0:T(8,128)(2,1)}, f32[3,3,8,256]{3,2,1,0:T(8,128)}, bf16[768,1536]{1,0:T(8,128)(2,1)}, bf16[16,1536]{1,0:T(8,128)(2,1)}) custom-call(s32[16]{0:T(128)} %fusion.27.refs_0_, s32[1]{0:T(128)} %bitcast.3.refs_1_, s32[4]{0:T(128)} %refs_2_.3, s32[1]{0:T(128)} %bitcast.4.refs_3_, bf16[384,896]{1,0:T(8,128)(2,1)} %pad_maximum_fusion.1.refs_4_.refs_1_, ...), custom_call_target="tpu_custom_call" | custom-call | flops 1100000000 | bytes 100000 | tf_op jit(solution)/shard_map/group/pallas_call | solution.py:347
  88.3 2.0 %collective-permute-start.17 = (bf16[384,384]{1,0:T(8,128)(2,1)S(1)}, bf16[384,384]{1,0:T(8,128)(2,1)S(1)}, u32[]{:S(2)}, u32[]{:S(2)}) collective-permute-start(bf16[384,384]{1,0:T(8,128)(2,1)S(1)} %slice.79), channel_id=1, source_target_pairs={{0,2},{1,3},{2,0},{3,1},{4,6},{5,7},{6,4},{7,5},{8,10},{9,11},{10,... | collective-permute-start | bytes 884744 | tf_op jit(solution)/shard_map/ppermute | solution.py:469
  90.6 11.8 %group.5 = (bf16[768,512]{1,0:T(8,128)(2,1)}, bf16[768,1536]{1,0:T(8,128)(2,1)}) custom-call(s32[16]{0:T(128)} %fusion.27.refs_0_, bf16[384,896]{1,0:T(8,128)(2,1)} %pad_maximum_fusion.1.refs_4_.refs_1_, bf16[384,896]{1,0:T(8,128)(2,1)} %collective-permute-done.4.refs_5_.refs_2_, bf16[384,896]{1,0:T(8,128)(2,1)} %collective-permute-done.9.refs_6_.refs_3_, ...), custom_call_target="tpu_custom_call" | custom-call | flops 1100000000 | bytes 100000 | tf_op jit(solution)/shard_map/group/pallas_call | solution.py:347
  103.2 13.6 %group.6 = (bf16[768,512]{1,0:T(8,128)(2,1)}, f32[3,3,8,512]{3,2,1,0:T(8,128)}) custom-call(s32[16]{0:T(128)} %fusion.27.refs_0_, s32[1]{0:T(128)S(6)} %add.140.refs_1_, s32[4]{0:T(128)} %refs_2_.3, s32[1]{0:T(128)} %bitcast.4.refs_3_, bf16[384,768]{1,0:T(8,128)(2,1)} %copy-done.1, bf16[384,768]{1,0:T(8,128)(2,1)} %copy-done.3, bf16[384,768]{1,0:T(8,128)(2,1)} %copy-done.2, ...), custom_call_target="tpu_custom_call" | custom-call | flops 1100000000 | bytes 100000 | tf_op jit(solution)/shard_map/group/pallas_call | solution.py:347
  116.8 0.9 collective-permute-start.20
  117.7 1.2 collective-permute-start.21
  118.9 1.4 collective-permute-start.22
  120.9 10.5 %group.7.rest_2_ = bf16[768,512]{1,0:T(8,128)(2,1)} custom-call(s32[16]{0:T(128)} %fusion.27.refs_0_, bf16[384,768]{1,0:T(8,128)(2,1)} %copy-done.1, bf16[384,768]{1,0:T(8,128)(2,1)} %copy-done.3, bf16[384,768]{1,0:T(8,128)(2,1)} %copy-done.2, bf16[384,384]{1,0:T(8,128)(2,1)} %copy-done.8, bf16[384,384]{1,0:T(8,128)(2,1)} %copy-done.7, ...), custom_call_target="tpu_custom_call" | custom-call | flops 1100000000 | bytes 100000 | tf_op jit(solution)/shard_map/group/pallas_call | solution.py:347
  131.5 2.0 %collective-permute-done.23.rest_6_ = f32[4,3,3,8,512]{4,3,2,1,0:T(8,128)S(1)} collective-permute-done((f32[4,3,3,8,512]{4,3,2,1,0:T(8,128)S(1)}, f32[4,3,3,8,512]{4,3,2,1,0:T(8,128)S(1)}, u32[]{:S(2)}, u32[]{:S(2)}) %collective-permute-start.23) | collective-permute-done | bytes 589856 | tf_op jit(solution)/shard_map/ppermute | solution.py:469
  134.6 10.2 %output.1 = (bf16[768,1536]{1,0:T(8,128)(2,1)}, bf16[4,1536]{1,0:T(4,128)(2,1)}) custom-call(s32[1]{0:T(128)} %bitcast.core_ref, bf16[1536,1536]{1,0:T(8,128)(2,1)} %all-gather.2.cloned.1.call-done.rest_0_, bf16[768,512]{1,0:T(8,128)(2,1)} %get-tuple-element.49.rest_1_, bf16[768,512]{1,0:T(8,128)(2,1)} %group.7.rest_2_, bf16[768,512]{1,0:T(8,128)(2,1)} %copy-done.9, ...), custom_call_target="tpu_custom_call" | custom-call | flops 1100000000 | bytes 100000 | tf_op jit(solution)/shard_map/output/pallas_call | solution.py:442
  (92 shorter events, 9.1 us)
Async XLA Ops:
  7.2 126.4 %all-gather.2.cloned.1.call-start = ((), (), s32[]{:S(2)}) async-start(), calls=%async_computation | async-start | bytes 4866048 | tf_op jit(solution)/shard_map/all_gather | solution.py:593
  9.2 12.3 %copy-start.15 = (s32[4]{0:T(128)S(1)}, s32[4]{0:T(128)}, u32[]{:S(2)}) copy-start(s32[4]{0:T(128)} %refs_2_.3) | copy-start | bytes 52
  9.5 1.5 %collective-permute-start = (bf16[48,1664]{1,0:T(8,128)(2,1)S(1)}, bf16[48,1664]{1,0:T(8,128)(2,1)S(1)}, u32[]{:S(2)}, u32[]{:S(2)}) collective-permute-start(bf16[48,1664]{1,0:T(8,128)(2,1)S(1)} %pad_maximum_fusion.3), channel_id=1, source_target_pairs={{0,1},{1,0},{2,3},{3,2},{4,5},{5,4},{6,7},{7,6},{8,9},{9,8},{10,11... | collective-permute-start | bytes 479240 | tf_op jit(solution)/shard_map/ppermute | solution.py:469
  11.0 24.9 %collective-permute-start.6 = (bf16[4,512,768]{2,1,0:T(8,128)(2,1)}, bf16[4,512,768]{2,1,0:T(8,128)(2,1)S(1)}, u32[]{:S(2)}, u32[]{:S(2)}) collective-permute-start(bf16[4,512,768]{2,1,0:T(8,128)(2,1)} %refs_14_.3), channel_id=1, source_target_pairs={{0,1},{1,0},{2,3},{3,2},{4,5},{5,4},{6,7},{7,6},{8,9},{9,8},{10,11... | collective-permute-start | bytes 9437192 | tf_op jit(solution)/shard_map/ppermute | solution.py:469
  11.4 24.6 %collective-permute-start.7 = (bf16[4,512,768]{2,1,0:T(8,128)(2,1)}, bf16[4,512,768]{2,1,0:T(8,128)(2,1)}, u32[]{:S(2)}, u32[]{:S(2)}) collective-permute-start(bf16[4,512,768]{2,1,0:T(8,128)(2,1)} %refs_15_.1), channel_id=1, source_target_pairs={{0,1},{1,0},{2,3},{3,2},{4,5},{5,4},{6,7},{7,6},{8,9},{9,8},{10,11... | collective-permute-start | bytes 9437192 | tf_op jit(solution)/shard_map/ppermute | solution.py:469
  11.5 24.4 %collective-permute-start.5 = (bf16[768,1536]{1,0:T(8,128)(2,1)}, bf16[768,1536]{1,0:T(8,128)(2,1)}, u32[]{:S(2)}, u32[]{:S(2)}) collective-permute-start(bf16[768,1536]{1,0:T(8,128)(2,1)} %refs_6_), channel_id=1, source_target_pairs={{0,1},{1,0},{2,3},{3,2},{4,5},{5,4},{6,7},{7,6},{8,9},{9,8},{10,11... | collective-permute-start | bytes 7077896 | tf_op jit(solution)/shard_map/ppermute | solution.py:469
  11.9 11.5 %copy-start.13 = (f32[3,16,192]{2,1,0:T(8,128)S(1)}, f32[3,16,192]{2,1,0:T(8,128)}, u32[]{:S(2)}) copy-start(f32[3,16,192]{2,1,0:T(8,128)} %constant.109.clone.1) | copy-start | bytes 110596
  11.9 12.2 %copy-start.14 = (bf16[4,1536]{1,0:T(4,128)(2,1)S(1)}, bf16[4,1536]{1,0:T(4,128)(2,1)}, u32[]{:S(2)}) copy-start(bf16[4,1536]{1,0:T(4,128)(2,1)} %param.9) | copy-start | bytes 36868
  12.0 9.6 %collective-permute-start.1 = (bf16[96,896]{1,0:T(8,128)(2,1)S(1)}, bf16[96,896]{1,0:T(8,128)(2,1)S(1)}, u32[]{:S(2)}, u32[]{:S(2)}) collective-permute-start(bf16[96,896]{1,0:T(8,128)(2,1)S(1)} %fusion.4), channel_id=1, source_target_pairs={{8,0},{16,8},{24,16},{0,24},{9,1},{17,9},{25,17},{1,25},{10,2},{18... | collective-permute-start | bytes 516104 | tf_op jit(solution)/shard_map/ppermute | solution.py:495
  17.3 14.6 %collective-permute-start.2 = (bf16[96,896]{1,0:T(8,128)(2,1)S(1)}, bf16[96,896]{1,0:T(8,128)(2,1)S(1)}, u32[]{:S(2)}, u32[]{:S(2)}) collective-permute-start(bf16[96,896]{1,0:T(8,128)(2,1)S(1)} %fusion.4), channel_id=1, source_target_pairs={{16,0},{24,8},{0,16},{8,24},{17,1},{25,9},{1,17},{9,25},{18,2},{26... | collective-permute-start | bytes 516104 | tf_op jit(solution)/shard_map/ppermute | solution.py:495
  21.5 10.4 %collective-permute-start.3 = (bf16[96,896]{1,0:T(8,128)(2,1)S(1)}, bf16[96,896]{1,0:T(8,128)(2,1)S(1)}, u32[]{:S(2)}, u32[]{:S(2)}) collective-permute-start(bf16[96,896]{1,0:T(8,128)(2,1)S(1)} %fusion.4), channel_id=1, source_target_pairs={{24,0},{0,8},{8,16},{16,24},{25,1},{1,9},{9,17},{17,25},{26,2},{2,... | collective-permute-start | bytes 516104 | tf_op jit(solution)/shard_map/ppermute | solution.py:495
  32.8 18.2 %collective-permute-start.4 = (bf16[384,896]{1,0:T(8,128)(2,1)}, bf16[384,896]{1,0:T(8,128)(2,1)}, u32[]{:S(2)}, u32[]{:S(2)}) collective-permute-start(bf16[384,896]{1,0:T(8,128)(2,1)} %pad_maximum_fusion.1.refs_4_.refs_1_), channel_id=1, source_target_pairs={{0,2},{1,3},{2,0},{3,1},{4,6},{5,7},{6,4},{7,5},{8,10},{9,11},{10,... | collective-permute-start | bytes 2064392 | tf_op jit(solution)/shard_map/ppermute | solution.py:469
  34.3 17.9 %collective-permute-start.9 = (bf16[384,896]{1,0:T(8,128)(2,1)}, bf16[384,896]{1,0:T(8,128)(2,1)}, u32[]{:S(2)}, u32[]{:S(2)}) collective-permute-start(bf16[384,896]{1,0:T(8,128)(2,1)} %pad_maximum_fusion.1.refs_4_.refs_1_), channel_id=1, source_target_pairs={{0,4},{1,5},{2,6},{3,7},{4,0},{5,1},{6,2},{7,3},{8,12},{9,13},{10,... | collective-permute-start | bytes 2064392 | tf_op jit(solution)/shard_map/ppermute | solution.py:469
  35.9 16.3 %collective-permute-start.8 = (bf16[96,768]{1,0:T(8,128)(2,1)}, bf16[96,768]{1,0:T(8,128)(2,1)}, u32[]{:S(2)}, u32[]{:S(2)}) collective-permute-start(bf16[96,768]{1,0:T(8,128)(2,1)} %pad_maximum_fusion.5.operand_ref), channel_id=1, source_target_pairs={{8,0},{16,8},{24,16},{0,24},{9,1},{17,9},{25,17},{1,25},{10,2},{18... | collective-permute-start | bytes 442376 | tf_op jit(solution)/shard_map/ppermute | solution.py:495
  38.5 16.1 %collective-permute-start.10 = (bf16[96,768]{1,0:T(8,128)(2,1)}, bf16[96,768]{1,0:T(8,128)(2,1)}, u32[]{:S(2)}, u32[]{:S(2)}) collective-permute-start(bf16[96,768]{1,0:T(8,128)(2,1)} %pad_maximum_fusion.5.operand_ref), channel_id=1, source_target_pairs={{16,0},{24,8},{0,16},{8,24},{17,1},{25,9},{1,17},{9,25},{18,2},{26... | collective-permute-start | bytes 442376 | tf_op jit(solution)/shard_map/ppermute | solution.py:495
  39.3 15.3 %collective-permute-start.11 = (bf16[96,768]{1,0:T(8,128)(2,1)}, bf16[96,768]{1,0:T(8,128)(2,1)}, u32[]{:S(2)}, u32[]{:S(2)}) collective-permute-start(bf16[96,768]{1,0:T(8,128)(2,1)} %pad_maximum_fusion.5.operand_ref), channel_id=1, source_target_pairs={{24,0},{0,8},{8,16},{16,24},{25,1},{1,9},{9,17},{17,25},{26,2},{2,... | collective-permute-start | bytes 442376 | tf_op jit(solution)/shard_map/ppermute | solution.py:495
  56.5 31.8 %copy-start.1 = (bf16[384,768]{1,0:T(8,128)(2,1)}, bf16[384,768]{1,0:T(8,128)(2,1)S(1)}, u32[]{:S(2)}) copy-start(bf16[384,768]{1,0:T(8,128)(2,1)S(1)} %maximum_add_fusion.refs_4_.refs_1_) | copy-start | bytes 1769476
  57.7 13.5 %collective-permute-start.12 = (bf16[384,512]{1,0:T(8,128)(2,1)S(1)}, bf16[384,512]{1,0:T(8,128)(2,1)S(1)}, u32[]{:S(2)}, u32[]{:S(2)}) collective-permute-start(bf16[384,512]{1,0:T(8,128)(2,1)S(1)} %slice.76), channel_id=1, source_target_pairs={{0,4},{1,5},{2,6},{3,7},{4,0},{5,1},{6,2},{7,3},{8,12},{9,13},{10,... | collective-permute-start | bytes 1179656 | tf_op jit(solution)/shard_map/ppermute | solution.py:469
  59.2 12.0 %collective-permute-start.13 = (bf16[384,384]{1,0:T(8,128)(2,1)S(1)}, bf16[384,384]{1,0:T(8,128)(2,1)S(1)}, u32[]{:S(2)}, u32[]{:S(2)}) collective-permute-start(bf16[384,384]{1,0:T(8,128)(2,1)S(1)} %slice.77), channel_id=1, source_target_pairs={{0,2},{1,3},{2,0},{3,1},{4,6},{5,7},{6,4},{7,5},{8,10},{9,11},{10,... | collective-permute-start | bytes 884744 | tf_op jit(solution)/shard_map/ppermute | solution.py:469
  71.2 17.1 %collective-permute-start.15 = (bf16[384,768]{1,0:T(8,128)(2,1)S(1)}, bf16[384,768]{1,0:T(8,128)(2,1)S(1)}, u32[]{:S(2)}, u32[]{:S(2)}) collective-permute-start(bf16[384,768]{1,0:T(8,128)(2,1)S(1)} %maximum_add_fusion.refs_4_.refs_1_), channel_id=1, source_target_pairs={{0,4},{1,5},{2,6},{3,7},{4,0},{5,1},{6,2},{7,3},{8,12},{9,13},{10,... | collective-permute-start | bytes 1769480 | tf_op jit(solution)/shard_map/ppermute | solution.py:469
  73.7 16.7 %collective-permute-start.14 = (bf16[384,768]{1,0:T(8,128)(2,1)S(1)}, bf16[384,768]{1,0:T(8,128)(2,1)S(1)}, u32[]{:S(2)}, u32[]{:S(2)}) collective-permute-start(bf16[384,768]{1,0:T(8,128)(2,1)S(1)} %maximum_add_fusion.refs_4_.refs_1_), channel_id=1, source_target_pairs={{0,2},{1,3},{2,0},{3,1},{4,6},{5,7},{6,4},{7,5},{8,10},{9,11},{10,... | collective-permute-start | bytes 1769480 | tf_op jit(solution)/shard_map/ppermute | solution.py:469
  88.3 14.0 %copy-start.2 = (bf16[384,768]{1,0:T(8,128)(2,1)}, bf16[384,768]{1,0:T(8,128)(2,1)S(1)}, u32[]{:S(2)}) copy-start(bf16[384,768]{1,0:T(8,128)(2,1)S(1)} %collective-permute-done.15.refs_6_.refs_3_) | copy-start | bytes 1769476
  88.3 14.0 %collective-permute-start.17 = (bf16[384,384]{1,0:T(8,128)(2,1)S(1)}, bf16[384,384]{1,0:T(8,128)(2,1)S(1)}, u32[]{:S(2)}, u32[]{:S(2)}) collective-permute-start(bf16[384,384]{1,0:T(8,128)(2,1)S(1)} %slice.79), channel_id=1, source_target_pairs={{0,2},{1,3},{2,0},{3,1},{4,6},{5,7},{6,4},{7,5},{8,10},{9,11},{10,... | collective-permute-start | bytes 884744 | tf_op jit(solution)/shard_map/ppermute | solution.py:469
  90.4 12.0 %copy-start.3 = (bf16[384,768]{1,0:T(8,128)(2,1)}, bf16[384,768]{1,0:T(8,128)(2,1)S(1)}, u32[]{:S(2)}) copy-start(bf16[384,768]{1,0:T(8,128)(2,1)S(1)} %collective-permute-done.14.refs_5_.refs_2_) | copy-start | bytes 1769476
  90.4 12.0 %collective-permute-start.16 = (bf16[384,384]{1,0:T(8,128)(2,1)S(1)}, bf16[384,384]{1,0:T(8,128)(2,1)S(1)}, u32[]{:S(2)}, u32[]{:S(2)}) collective-permute-start(bf16[384,384]{1,0:T(8,128)(2,1)S(1)} %slice.78), channel_id=1, source_target_pairs={{0,4},{1,5},{2,6},{3,7},{4,0},{5,1},{6,2},{7,3},{8,12},{9,13},{10,... | collective-permute-start | bytes 884744 | tf_op jit(solution)/shard_map/ppermute | solution.py:469
  103.2 17.1 %copy-start.17 = (bf16[768,512]{1,0:T(8,128)(2,1)S(1)}, bf16[768,512]{1,0:T(8,128)(2,1)}, u32[]{:S(2)}) copy-start(bf16[768,512]{1,0:T(8,128)(2,1)} %get-tuple-element.47) | copy-start | bytes 2359300
  116.8 14.6 %collective-permute-start.20 = (f32[3,3,8,512]{3,2,1,0:T(8,128)}, f32[3,3,8,512]{3,2,1,0:T(8,128)S(1)}, u32[]{:S(2)}, u32[]{:S(2)}) collective-permute-start(f32[3,3,8,512]{3,2,1,0:T(8,128)} %get-tuple-element.60), channel_id=1, source_target_pairs={{0,2},{1,3},{2,0},{3,1},{4,6},{5,7},{6,4},{7,5},{8,10},{9,11},{10,... | collective-permute-start | bytes 442376 | tf_op jit(solution)/shard_map/ppermute | solution.py:469
  117.7 13.7 %collective-permute-start.21 = (f32[3,3,8,512]{3,2,1,0:T(8,128)}, f32[3,3,8,512]{3,2,1,0:T(8,128)S(1)}, u32[]{:S(2)}, u32[]{:S(2)}) collective-permute-start(f32[3,3,8,512]{3,2,1,0:T(8,128)} %get-tuple-element.60), channel_id=1, source_target_pairs={{0,4},{1,5},{2,6},{3,7},{4,0},{5,1},{6,2},{7,3},{8,12},{9,13},{10,... | collective-permute-start | bytes 442376 | tf_op jit(solution)/shard_map/ppermute | solution.py:469
  118.9 12.4 %collective-permute-start.22 = (f32[3,3,8,512]{3,2,1,0:T(8,128)}, f32[3,3,8,512]{3,2,1,0:T(8,128)S(1)}, u32[]{:S(2)}, u32[]{:S(2)}) collective-permute-start(f32[3,3,8,512]{3,2,1,0:T(8,128)} %get-tuple-element.60), channel_id=1, source_target_pairs={{0,6},{1,7},{2,4},{3,5},{4,2},{5,3},{6,0},{7,1},{8,14},{9,15},{10,... | collective-permute-start | bytes 442376 | tf_op jit(solution)/shard_map/ppermute | solution.py:469
  120.3 11.2 %collective-permute-start.18 = (bf16[768,512]{1,0:T(8,128)(2,1)S(1)}, bf16[768,512]{1,0:T(8,128)(2,1)S(1)}, u32[]{:S(2)}, u32[]{:S(2)}) collective-permute-start(bf16[768,512]{1,0:T(8,128)(2,1)S(1)} %copy-done.17), channel_id=1, source_target_pairs={{0,1},{1,0},{2,3},{3,2},{4,5},{5,4},{6,7},{7,6},{8,9},{9,8},{10,11... | collective-permute-start | bytes 2359304 | tf_op jit(solution)/shard_map/ppermute | solution.py:469
  120.3 13.2 %collective-permute-start.19 = (bf16[768,512]{1,0:T(8,128)(2,1)}, bf16[768,512]{1,0:T(8,128)(2,1)S(1)}, u32[]{:S(2)}, u32[]{:S(2)}) collective-permute-start(bf16[768,512]{1,0:T(8,128)(2,1)} %get-tuple-element.58), channel_id=1, source_target_pairs={{0,1},{1,0},{2,3},{3,2},{4,5},{5,4},{6,7},{7,6},{8,9},{9,8},{10,11... | collective-permute-start | bytes 2359304 | tf_op jit(solution)/shard_map/ppermute | solution.py:469
  131.4 2.1 %collective-permute-start.23 = (f32[4,3,3,8,512]{4,3,2,1,0:T(8,128)S(1)}, f32[4,3,3,8,512]{4,3,2,1,0:T(8,128)S(1)}, u32[]{:S(2)}, u32[]{:S(2)}) collective-permute-start(f32[4,3,3,8,512]{4,3,2,1,0:T(8,128)S(1)} %pad_maximum_fusion.2.rest_5_), channel_id=1, source_target_pairs={{0,1},{1,0},{2,3},{3,2},{4,5},{5,4},{6,7},{7,6},{8,9},{9,8},{10,11... | collective-permute-start | bytes 1769480 | tf_op jit(solution)/shard_map/ppermute | solution.py:469
  (11 other events, 31.3 us)
Sparse Core Ops, SparseCore 0:
  36.0 71.1 all-gather.1
